TPU v7x, 32 devices: a whole 2x2x4 slice. The times are simulated.
32 devices in a mesh: seq: 8 (over z, y), head: 4 (over x, core).
Axes of the slice: x: 2, y: 2, z: 4, core: 2. Of those that a mesh axis runs over, the one named last changes fastest.
Arguments:
- hidden_in: float32 [2048, 1536], P(('seq', 'head')), may hold values from -6 to 6
- norm1_gain: float32 [1536], replicated, may hold values from 0.5 to 1.5
- w_zx: bfloat16 [1536, 2, 3072], P(None, None, 'head'), may hold values from -0.15625 to 0.15625
- w_bc: bfloat16 [1536, 256], replicated, may hold values from -0.15625 to 0.15625
- w_dt: bfloat16 [1536, 48], P(None, 'head'), may hold values from -0.045898438 to 0.045898438
- conv_x: float32 [4, 3072], P(None, 'head'), may hold values from -0.5 to 0.5
- conv_bc: float32 [4, 256], replicated, may hold values from -0.5 to 0.5
- dt_bias: float32 [48], P('head'), may hold values from -4.6 to -2.3
- a_log: float32 [48], P('head'), may hold values from -11 to 0
- d_skip: float32 [48], P('head'), may hold values from 0.5 to 1.5
- gate_gain: float32 [3072], P('head'), may hold values from 0.5 to 1.5
- w_out: bfloat16 [3072, 1536], P('head'), may hold values from -0.109375 to 0.109375
- norm2_gain: float32 [1536], replicated, may hold values from 0.5 to 1.5
- router: bfloat16 [1536, 16], replicated, may hold values from -0.076660156 to 0.076660156
- expert_up: bfloat16 [32, 1536, 2, 256], P(('seq', 'head')), may hold values from -0.15625 to 0.15625
- expert_down: bfloat16 [32, 256, 1536], P(('seq', 'head')), may hold values from -0.25 to 0.25
- shared_up: bfloat16 [1536, 2, 1024], replicated, may hold values from -0.15625 to 0.15625
- shared_down: bfloat16 [1024, 1536], replicated, may hold values from -0.1875 to 0.1875
- out_grad: float32 [2048, 1536], P(('seq', 'head')), may hold values from -6 to 6
- seq_lengths: int32 [4], replicated, may hold values from 16 to 1888, as said below
- routes: int32 [2048, 6], P(('seq', 'head')), may hold values from 0 to 15, all different within a row; in each aligned block of 64 rows (0 to 63, 64 to 127, ...) at most 48 rows name the same one
Outputs:
- output: float32 [2048, 1536], P(('seq', 'head'))
- grad_in: float32 [2048, 1536], P(('seq', 'head'))
- grad_norm1: float32 [1536], replicated
- grad_zx: float32 [1536, 2, 3072], P('seq', None, 'head')
- grad_bc: float32 [1536, 256], P(('seq', 'head'))
- grad_dt: float32 [1536, 48], P('seq', 'head')
- grad_conv_x: float32 [4, 3072], replicated
- grad_conv_bc: float32 [4, 256], replicated
- grad_dt_bias: float32 [48], replicated
- grad_a_log: float32 [48], replicated
- grad_d_skip: float32 [48], replicated
- grad_gate_gain: float32 [3072], replicated
- grad_w_out: float32 [3072, 1536], P('head', 'seq')
- grad_norm2: float32 [1536], replicated
- grad_router: float32 [1536, 16], P(('seq', 'head'))
- grad_expert_up: float32 [32, 1536, 2, 256], P(('seq', 'head'))
- grad_expert_down: float32 [32, 256, 1536], P(('seq', 'head'))
- grad_shared_up: float32 [1536, 2, 1024], P(('seq', 'head'))
- grad_shared_down: float32 [1024, 1536], P(None, ('seq', 'head'))
Inputs may be any that keep to these rules, and one draw needn't show every extreme that they name: `seq_lengths`: the lengths sum to 2048; the longest is 1888 and the other three together 5 * 32. `routes`: within the rows of one device no expert is named more than 48 times; a row names 6 different experts.
All inputs are finite; a program needn't handle non-finite values.
Results may differ from a plain program's by a relative error of at most 0.015.
Values may be sent and summed in bfloat16 or wider, within the bound.
A program may use at most 192 MiB of HBM per device.

v0:
```python
import jax
import jax.numpy as jnp
from jax import lax
from jax.sharding import PartitionSpec as P

BLOCK = 256


highest = lax.Precision.HIGHEST
epsilon = 1e-05


def entering(value, axis, join, neutral, backward):
    count, mine = (lax.axis_size(axis), lax.axis_index(axis))
    pieces = jax.tree.map(lambda part: lax.all_gather(part, axis), value)
    if backward:
        pieces = jax.tree.map(lambda part: part[::-1], pieces)
        mine = count - 1 - mine
    so_far = jax.tree.map(
        lambda part, zero: jnp.full_like(part, 0) + jnp.asarray(zero, part.dtype), value, neutral
    )

    def lap(position, so_far):
        longer = join(so_far, jax.tree.map(lambda part: part[position], pieces))
        return jax.tree.map(lambda new, old: jnp.where(position < mine, new, old), longer, so_far)

    return lax.fori_loop(0, count - 1, lap, so_far)


def shifted(value, axis, steps):
    count = lax.axis_size(axis)
    initial, last = (max(0, -steps), min(count, count - steps))
    return lax.ppermute(value, axis, [(source, source + steps) for source in range(initial, last)])


def rms_scale(values, gain_vec):
    return (
        values * lax.rsqrt(jnp.mean(values * values, axis=-1, keepdims=True) + epsilon) * gain_vec
    )


def rms_back(values, gain_vec, grad_out):
    inverse = lax.rsqrt(jnp.mean(values * values, axis=-1, keepdims=True) + epsilon)
    weighted = grad_out * gain_vec
    inner_mean = jnp.mean(weighted * values, axis=-1, keepdims=True)
    return inverse * weighted - values * inverse**3 * inner_mean


def gain_grad(values, grad_out):
    inverse = lax.rsqrt(jnp.mean(values * values, axis=-1, keepdims=True) + epsilon)
    return jnp.sum(grad_out * values * inverse, axis=0)


def silu_back(values, grad_out):
    sigmoid_vals = jax.nn.sigmoid(values)
    return grad_out * sigmoid_vals * (1.0 + values * (1.0 - sigmoid_vals))


def segment_of(positions, seq_lengths):
    seq_ends = jnp.cumsum(seq_lengths)
    located = jnp.sum((positions[:, None] >= seq_ends[None, :]).astype(jnp.int32), axis=1)
    return jnp.where(positions < 0, -1, located)


def start_flags(positions, seq_lengths):
    begins = jnp.cumsum(seq_lengths) - seq_lengths
    return jnp.sum((positions[:, None] == begins[None, :]).astype(jnp.float32), axis=1)


def causal_conv(extended, weights, segment_ext):
    length = extended.shape[0] - 3
    current = segment_ext[3:]
    summed = weights[3] * extended[3:]
    for offset in (1, 2, 3):
        joined = (segment_ext[3 - offset : 3 - offset + length] == current).astype(jnp.float32)
        summed = (
            summed
            + weights[3 - offset] * extended[3 - offset : 3 - offset + length] * joined[:, None]
        )
    return summed


def block_step(carry_state, block_in):
    x_vals, b_vals, c_vals, log_rates, dt_vals, starts = block_in
    logdec = jnp.cumsum(log_rates, axis=0)
    run_ids = jnp.cumsum(starts)
    order_ids = jnp.arange(x_vals.shape[0])
    linked = ((run_ids[:, None] == run_ids[None, :]) & (order_ids[:, None] >= order_ids[None, :]))[
        :, :, None
    ]
    log_gap = jnp.where(linked, logdec[:, None, :] - logdec[None, :, :], 0.0)
    decays = jnp.where(linked, jnp.exp(log_gap), 0.0)
    scores = jnp.dot(c_vals, b_vals.T, precision=highest)
    inner_out = jnp.einsum(
        "tsh,shp->thp", decays * scores[:, :, None], dt_vals[:, :, None] * x_vals, precision=highest
    )
    unreset = (run_ids == 0.0).astype(jnp.float32)
    carried = (unreset[:, None] * jnp.exp(logdec))[:, :, None] * jnp.einsum(
        "tn,hpn->thp", c_vals, carry_state, precision=highest
    )
    log_last = logdec[-1]
    tail_weight = (
        jnp.exp(log_last[None, :] - logdec) * (run_ids == run_ids[-1]).astype(jnp.float32)[:, None]
    )
    fresh_state = jnp.einsum(
        "sh,shp,sn->hpn", tail_weight * dt_vals, x_vals, b_vals, precision=highest
    )
    keep_gain = jnp.exp(log_last) * (run_ids[-1] == 0.0).astype(jnp.float32)
    return (keep_gain[:, None, None] * carry_state + fresh_state, inner_out + carried)


def link_states(earlier, later):
    return (earlier[0] * later[0], later[0][:, None, None] * earlier[1] + later[1])


def chain_pass(summary, backward):
    identity_pair = (jnp.ones_like(summary[0]), jnp.zeros_like(summary[1]))
    return entering(summary, "seq", link_states, identity_pair, backward)


def move_rim(rim_rows, direction):
    return shifted(rim_rows, "seq", direction)


def head_total(partial_sum):
    return lax.psum(partial_sum, "head")


def route_rows(slot_rows):
    return lax.all_to_all(slot_rows, ("seq", "head"), split_axis=0, concat_axis=0, tiled=True)


def local(
    hidden_in,
    norm1_gain,
    w_zx,
    w_bc,
    w_dt,
    conv_x,
    conv_bc,
    dt_bias,
    a_log,
    d_skip,
    gate_gain,
    w_out,
    norm2_gain,
    router,
    expert_up,
    expert_down,
    shared_up,
    shared_down,
    out_grad,
    seq_lengths,
    routes,
):
    head_count = lax.axis_size("head")
    seq_index = lax.axis_index("seq")
    head_index = lax.axis_index("head")
    row_count = hidden_in.shape[0]
    model_width = hidden_in.shape[1]
    tok_local = row_count * head_count
    local_heads = dt_bias.shape[0]
    inner_local = conv_x.shape[1]
    head_size = inner_local // local_heads
    state_size = w_bc.shape[1] // 2
    inner_width = inner_local * head_count
    expert_count = lax.axis_size("seq") * head_count // 2
    top_count = routes.shape[1]
    capacity = 12 * row_count // expert_count
    half_width = expert_down.shape[1]
    shared_width = shared_down.shape[0]
    block_count = tok_local // BLOCK
    first_pos = seq_index * tok_local
    positions = first_pos + jnp.arange(tok_local, dtype=jnp.int32)
    starts = start_flags(positions, seq_lengths)
    segment_ext = segment_of(
        first_pos - 3 + jnp.arange(tok_local + 3, dtype=jnp.int32), seq_lengths
    )
    reads_in = (jnp.cumsum(starts) == 0.0).astype(jnp.float32)
    normed_rows = rms_scale(hidden_in, norm1_gain).astype(jnp.bfloat16)
    normed_one = lax.all_gather(normed_rows, "head", axis=0, tiled=True)
    zx_flat = w_zx.reshape(model_width, 2 * inner_local)
    zx_vals = jnp.dot(normed_one, zx_flat, preferred_element_type=jnp.float32)
    bc_vals = jnp.dot(normed_one, w_bc, preferred_element_type=jnp.float32)
    dt_raw = jnp.dot(normed_one, w_dt, preferred_element_type=jnp.float32)
    z_vals = zx_vals[:, :inner_local]
    pre_conv = jnp.concatenate([zx_vals[:, inner_local:], bc_vals], axis=1)
    rim_in = move_rim(pre_conv[-3:], 1)
    extended = jnp.concatenate([rim_in, pre_conv], axis=0)
    conv_w = jnp.concatenate([conv_x, conv_bc], axis=1)

    def front(extended, conv_w, dt_raw, dt_bias, a_log):
        activated = jax.nn.silu(causal_conv(extended, conv_w, segment_ext))
        x_heads = activated[:, :inner_local].reshape(tok_local, local_heads, head_size)
        b_vals = activated[:, inner_local : inner_local + state_size]
        c_vals = activated[:, inner_local + state_size :]
        dt_vals = jax.nn.softplus(dt_raw + dt_bias)
        log_rates = -dt_vals * jnp.exp(a_log)
        blocks = (
            x_heads.reshape(block_count, BLOCK, local_heads, head_size),
            b_vals.reshape(block_count, BLOCK, state_size),
            c_vals.reshape(block_count, BLOCK, state_size),
            log_rates.reshape(block_count, BLOCK, local_heads),
            dt_vals.reshape(block_count, BLOCK, local_heads),
            starts.reshape(block_count, BLOCK),
        )
        initial = jnp.zeros((local_heads, head_size, state_size), jnp.float32)
        state_out, mixed_out = lax.scan(block_step, initial, blocks)
        keep_dev = jnp.exp(jnp.sum(log_rates, axis=0)) * (jnp.sum(starts) == 0.0).astype(
            jnp.float32
        )
        return (
            x_heads,
            b_vals,
            c_vals,
            log_rates,
            dt_vals,
            mixed_out.reshape(tok_local, local_heads, head_size),
            keep_dev,
            state_out,
        )

    def finish(x_heads, c_vals, log_rates, mixed_loc, d_skip, z_vals, state_in):
        logdec = jnp.cumsum(log_rates, axis=0)
        carried = (reads_in[:, None] * jnp.exp(logdec))[:, :, None] * jnp.einsum(
            "tn,hpn->thp", c_vals, state_in, precision=highest
        )
        ssd_out = mixed_loc + carried + d_skip[None, :, None] * x_heads
        return ssd_out.reshape(tok_local, inner_local) * jax.nn.silu(z_vals)

    front_out, front_back = jax.vjp(front, extended, conv_w, dt_raw, dt_bias, a_log)
    x_heads, b_vals, c_vals, log_rates, dt_vals, mixed_loc, keep_dev, state_dev = front_out
    chained = chain_pass((keep_dev, state_dev), False)
    state_in = chained[1]
    gated_vals, finish_back = jax.vjp(
        finish, x_heads, c_vals, log_rates, mixed_loc, d_skip, z_vals, state_in
    )
    square_sum = head_total(jnp.sum(gated_vals * gated_vals, axis=1))
    inverse_gate = lax.rsqrt(square_sum / inner_width + epsilon)[:, None]
    normed_gate = (gated_vals * inverse_gate * gate_gain).astype(jnp.bfloat16)
    mixer_rows = lax.psum_scatter(
        jnp.dot(normed_gate, w_out, preferred_element_type=jnp.float32),
        "head",
        scatter_dimension=0,
        tiled=True,
    )
    residual = hidden_in + mixer_rows
    normed_two = rms_scale(residual, norm2_gain).astype(jnp.bfloat16)
    logits = jnp.dot(normed_two, router, preferred_element_type=jnp.float32)
    choose = (
        routes[:, :, None] == jnp.arange(expert_count, dtype=jnp.int32)[None, None, :]
    ).astype(jnp.float32)
    chosen = jnp.einsum("rke,re->rk", choose, logits, precision=highest)
    gate_probs = jax.nn.softmax(chosen, axis=-1)
    flat_routes = routes.reshape(-1)
    onehot = (flat_routes[:, None] == jnp.arange(expert_count, dtype=jnp.int32)[None, :]).astype(
        jnp.int32
    )
    slot_pos = jnp.sum(jnp.cumsum(onehot, axis=0) * onehot, axis=1) - 1

    def both_halves(slot_rows):
        return jnp.broadcast_to(
            slot_rows[:, None], (expert_count, 2) + slot_rows.shape[1:]
        ).reshape((2 * expert_count,) + slot_rows.shape[1:])

    rows_out = jnp.repeat(normed_two, top_count, axis=0)
    send_one = (
        jnp.zeros((expert_count, capacity, model_width), jnp.bfloat16)
        .at[flat_routes, slot_pos]
        .set(rows_out)
    )
    received = route_rows(both_halves(send_one))
    recv_flat = received.reshape(-1, model_width)
    up_local = expert_up[0].reshape(model_width, 2 * half_width)
    down_local = expert_down[0]
    middle = jnp.dot(recv_flat, up_local, preferred_element_type=jnp.float32)
    expert_gate = middle[:, :half_width]
    expert_lin = middle[:, half_width:]
    acting = (jax.nn.silu(expert_gate) * expert_lin).astype(jnp.bfloat16)
    expert_out = (
        jnp.dot(acting, down_local, preferred_element_type=jnp.float32)
        .astype(jnp.bfloat16)
        .reshape(received.shape)
    )
    returned = route_rows(expert_out)
    merged = jnp.sum(
        returned.reshape(expert_count, 2, capacity, model_width).astype(jnp.float32), axis=1
    )
    picked = merged[flat_routes, slot_pos].reshape(row_count, top_count, model_width)
    routed = jnp.einsum("rk,rkd->rd", gate_probs, picked, precision=highest)
    shared_mid = jnp.dot(
        normed_two,
        shared_up.reshape(model_width, 2 * shared_width),
        preferred_element_type=jnp.float32,
    )
    shared_gate = shared_mid[:, :shared_width]
    shared_lin = shared_mid[:, shared_width:]
    shared_act = (jax.nn.silu(shared_gate) * shared_lin).astype(jnp.bfloat16)
    shared_out = jnp.dot(shared_act, shared_down, preferred_element_type=jnp.float32)
    output = residual + routed + shared_out
    grad_out_low = out_grad.astype(jnp.bfloat16)
    grad_shared_act = jnp.dot(grad_out_low, shared_down.T, preferred_element_type=jnp.float32)
    grad_shared_down = jnp.dot(shared_act.T, grad_out_low, preferred_element_type=jnp.float32)
    grad_shared_mid = jnp.concatenate(
        [
            silu_back(shared_gate, grad_shared_act * shared_lin),
            grad_shared_act * jax.nn.silu(shared_gate),
        ],
        axis=1,
    ).astype(jnp.bfloat16)
    grad_two = jnp.dot(
        grad_shared_mid,
        shared_up.reshape(model_width, 2 * shared_width).T,
        preferred_element_type=jnp.float32,
    )
    grad_shared_up = jnp.dot(
        normed_two.T, grad_shared_mid, preferred_element_type=jnp.float32
    ).reshape(shared_up.shape)
    grad_probs = jnp.einsum("rd,rkd->rk", out_grad, picked, precision=highest)
    grad_chosen = gate_probs * (
        grad_probs - jnp.sum(gate_probs * grad_probs, axis=1, keepdims=True)
    )
    grad_logits = jnp.einsum("rk,rke->re", grad_chosen, choose, precision=highest).astype(
        jnp.bfloat16
    )
    grad_two = grad_two + jnp.dot(grad_logits, router.T, preferred_element_type=jnp.float32)
    grad_router = jnp.dot(normed_two.T, grad_logits, preferred_element_type=jnp.float32)
    grad_picked = (
        (gate_probs[:, :, None] * out_grad[:, None, :])
        .astype(jnp.bfloat16)
        .reshape(-1, model_width)
    )
    grad_send = (
        jnp.zeros((expert_count, capacity, model_width), jnp.bfloat16)
        .at[flat_routes, slot_pos]
        .set(grad_picked)
    )
    grad_received = route_rows(both_halves(grad_send)).reshape(-1, model_width)
    grad_acting = jnp.dot(grad_received, down_local.T, preferred_element_type=jnp.float32)
    grad_down = jnp.dot(acting.T, grad_received, preferred_element_type=jnp.float32)
    grad_middle = jnp.concatenate(
        [silu_back(expert_gate, grad_acting * expert_lin), grad_acting * jax.nn.silu(expert_gate)],
        axis=1,
    ).astype(jnp.bfloat16)
    grad_up = jnp.dot(recv_flat.T, grad_middle, preferred_element_type=jnp.float32)
    grad_inputs = (
        jnp.dot(grad_middle, up_local.T, preferred_element_type=jnp.float32)
        .astype(jnp.bfloat16)
        .reshape(received.shape)
    )
    grad_returned = route_rows(grad_inputs)
    grad_merged = jnp.sum(
        grad_returned.reshape(expert_count, 2, capacity, model_width).astype(jnp.float32), axis=1
    )
    grad_two = grad_two + jnp.sum(
        grad_merged[flat_routes, slot_pos].reshape(row_count, top_count, model_width), axis=1
    )
    grad_res = out_grad + rms_back(residual, norm2_gain, grad_two)
    grad_norm2 = gain_grad(residual, grad_two)
    grad_mix_low = grad_res.astype(jnp.bfloat16)
    piece_rows = lax.all_gather(grad_mix_low, "head", axis=0, tiled=True)
    part_gate = jnp.dot(piece_rows, w_out.T, preferred_element_type=jnp.float32)
    grad_w_out = jnp.dot(normed_gate.T, piece_rows, preferred_element_type=jnp.float32)
    weighted_grad = part_gate * gate_gain
    cross_sum = head_total(jnp.sum(weighted_grad * gated_vals, axis=1))[:, None]
    grad_gated = (
        inverse_gate * weighted_grad - gated_vals * inverse_gate**3 * cross_sum / inner_width
    )
    grad_gate_gain = jnp.sum(part_gate * gated_vals * inverse_gate, axis=0)
    grad_x_heads, grad_c_vals, grad_rates, grad_mixed, grad_d_skip, grad_z_vals, grad_state_in = (
        finish_back(grad_gated)
    )
    passed = chain_pass((keep_dev, grad_state_in), True)
    grad_state_out = passed[1]
    grad_keep = jnp.sum(grad_state_out * state_in, axis=(1, 2))
    front_grads = front_back(
        (
            grad_x_heads,
            jnp.zeros_like(b_vals),
            grad_c_vals,
            grad_rates,
            jnp.zeros_like(dt_vals),
            grad_mixed,
            grad_keep,
            grad_state_out,
        )
    )
    grad_extended, grad_conv, grad_dt_raw, grad_dt_bias, grad_a_log = front_grads
    rim_back = move_rim(grad_extended[:3], -1)
    grad_pre = grad_extended[3:].at[-3:].add(rim_back)
    grad_zx_low = jnp.concatenate([grad_z_vals, grad_pre[:, :inner_local]], axis=1).astype(
        jnp.bfloat16
    )
    grad_bc_rows = grad_pre[:, inner_local:]
    w_bc_wide = w_bc.astype(jnp.float32)
    w_dt_wide = w_dt.astype(jnp.float32)
    part_zx = jnp.dot(grad_zx_low, zx_flat.T, preferred_element_type=jnp.float32)
    part_bc = jnp.dot(grad_bc_rows, w_bc_wide.T, precision=highest)
    part_dt = jnp.dot(grad_dt_raw, w_dt_wide.T, precision=highest)
    grad_one = lax.psum_scatter(
        (part_zx + part_bc + part_dt).astype(jnp.bfloat16), "head", scatter_dimension=0, tiled=True
    ).astype(jnp.float32)
    grad_in = grad_res + rms_back(hidden_in, norm1_gain, grad_one)
    grad_norm1 = gain_grad(hidden_in, grad_one)
    normed_wide = normed_one.astype(jnp.float32)
    grad_zx = jnp.dot(normed_one.T, grad_zx_low, preferred_element_type=jnp.float32).reshape(
        w_zx.shape
    )
    grad_bc = jnp.dot(normed_wide.T, grad_bc_rows, precision=highest)
    grad_dt = jnp.dot(normed_wide.T, grad_dt_raw, precision=highest)

    def widen(local_vals, axis_pos):
        full_shape = list(local_vals.shape)
        full_shape[axis_pos] = full_shape[axis_pos] * head_count
        return lax.dynamic_update_slice_in_dim(
            jnp.zeros(full_shape, jnp.float32),
            local_vals,
            head_index * local_vals.shape[axis_pos],
            axis_pos,
        )

    split_sums = (
        lax.psum_scatter(
            grad_zx.astype(jnp.bfloat16), "seq", scatter_dimension=0, tiled=True
        ).astype(jnp.float32),
        lax.psum_scatter(
            grad_dt.astype(jnp.bfloat16), "seq", scatter_dimension=0, tiled=True
        ).astype(jnp.float32),
        lax.psum_scatter(
            grad_w_out.astype(jnp.bfloat16), "seq", scatter_dimension=1, tiled=True
        ).astype(jnp.float32),
    )
    shared_sums = (
        lax.psum_scatter(grad_bc, ("seq", "head"), scatter_dimension=0, tiled=True),
        lax.psum_scatter(grad_router, ("seq", "head"), scatter_dimension=0, tiled=True),
        lax.psum_scatter(grad_shared_up, ("seq", "head"), scatter_dimension=0, tiled=True),
        lax.psum_scatter(grad_shared_down, ("seq", "head"), scatter_dimension=1, tiled=True),
    )
    small_sums = lax.psum(
        (
            grad_norm1,
            grad_norm2,
            widen(grad_conv[:, :inner_local], 1),
            grad_conv[:, inner_local:],
            widen(grad_dt_bias, 0),
            widen(grad_a_log, 0),
            widen(grad_d_skip, 0),
            widen(grad_gate_gain, 0),
        ),
        ("seq", "head"),
    )
    return (
        output,
        grad_in,
        small_sums[0],
        split_sums[0],
        shared_sums[0],
        split_sums[1],
        small_sums[2],
        small_sums[3],
        small_sums[4],
        small_sums[5],
        small_sums[6],
        small_sums[7],
        split_sums[2],
        small_sums[1],
        shared_sums[1],
        grad_up.reshape(expert_up.shape),
        grad_down.reshape(expert_down.shape),
        shared_sums[2],
        shared_sums[3],
    )


def solution(mesh):
    return jax.shard_map(
        local,
        mesh=mesh,
        in_specs=(
            P(("seq", "head"), None),
            P(),
            P(None, None, "head"),
            P(),
            P(None, "head"),
            P(None, "head"),
            P(),
            P("head"),
            P("head"),
            P("head"),
            P("head"),
            P("head", None),
            P(),
            P(),
            P(("seq", "head"), None, None, None),
            P(("seq", "head"), None, None),
            P(),
            P(),
            P(("seq", "head"), None),
            P(),
            P(("seq", "head"), None),
        ),
        out_specs=(
            P(("seq", "head"), None),
            P(("seq", "head"), None),
            P(),
            P("seq", None, "head"),
            P(("seq", "head"), None),
            P("seq", "head"),
            P(),
            P(),
            P(),
            P(),
            P(),
            P(),
            P("head", "seq"),
            P(),
            P(("seq", "head"), None),
            P(("seq", "head"), None, None, None),
            P(("seq", "head"), None, None),
            P(("seq", "head"), None, None),
            P(None, ("seq", "head")),
        ),
        check_vma=False,
    )
```

profile of v0, /device:TPU:0, one launch (start us, length us, event | category | flops | bytes accessed | tf_op | source)
XLA Modules:
  0.0 2103.0 jit_solution(53950871996058415)
XLA Ops:
  10.2 10.0 all_gather.24
  20.2 3.6 copy.222
  27.6 4.0 collective-permute-start
  60.6 19.7 all-reduce.12
  88.9 27.4 %all-gather.6.cloned.1.call-done = f32[96,64,128]{2,1,0:T(8,128)} async-done(((f32[12,64,128]{2,1,0:T(8,128)}), f32[96,64,128]{2,1,0:T(8,128)}) %all-gather.6.cloned.1.call-update) | async-done | bytes 3145744 | tf_op jit(solution)/shard_map/all_gather | solution.py:15
  116.2 8.0 while.21
  126.0 6.6 fusion.39
  137.5 5.7 psum.70
  143.7 3.9 fusion.146
  157.9 16.9 reduce-scatter.12.cloned.1.call-done
  184.7 61.9 %scatter_fusion = bf16[16,48,1536]{2,1,0:T(8,128)(2,1)} fusion(bf16[16,48,1536]{2,1,0:T(8,128)(2,1)} %broadcast.520.clone, s32[384]{0:T(512)S(1)} %get-tuple-element.693, bf16[384,1536]{1,0:T(8,128)(2,1)} %reshape.765), kind=kCustom, calls=%fused_computation.2 | custom fusion | bytes 3542016 | tf_op jit(solution)/shard_map/scatter | solution.py:270
  246.5 4.4 broadcast_in_dim.248
  250.9 4.9 all-to-all-start
  258.7 102.4 %all-to-all-done = bf16[32,48,1536]{2,1,0:T(8,128)(2,1)} async-done(((bf16[32,48,1536]{2,1,0:T(8,128)(2,1)}), bf16[32,48,1536]{2,1,0:T(8,128)(2,1)}, u32[]{:S(2)}, u32[]{:S(2)}) %all-to-all-start) | async-done | bytes 4718624 | tf_op jit(solution)/shard_map/all_to_all | solution.py:130
  361.1 5.0 fusion.161
  367.8 3.6 convolution_convert_fusion.2
  371.4 4.3 all-to-all-start.1
  378.9 3.6 mul.952
  388.2 92.9 %all-to-all-done.1 = bf16[32,48,1536]{2,1,0:T(8,128)(2,1)} async-done(((bf16[32,48,1536]{2,1,0:T(8,128)(2,1)}), bf16[32,48,1536]{2,1,0:T(8,128)(2,1)}, u32[]{:S(2)}, u32[]{:S(2)}) %all-to-all-start.1) | async-done | bytes 4718624 | tf_op jit(solution)/shard_map/all_to_all | solution.py:130
  481.1 5.9 convert_reduce_fusion.1
  486.9 12.6 gather_fusion
  499.6 3.4 reshape.730
  503.0 8.1 fusion.69
  519.0 62.2 %scatter_fusion.1 = bf16[16,48,1536]{2,1,0:T(8,128)(2,1)} fusion(bf16[16,48,1536]{2,1,0:T(8,128)(2,1)} %broadcast.520, s32[384]{0:T(512)S(1)} %get-tuple-element.693, bf16[384,1536]{1,0:T(8,128)(2,1)} %multiply_convert_fusion), kind=kCustom, calls=%fused_computation.3 | custom fusion | bytes 3542016 | tf_op jit(solution)/shard_map/scatter | solution.py:336
  583.5 109.1 %all_to_all.20 = bf16[32,48,1536]{2,1,0:T(8,128)(2,1)S(1)} all-to-all(bf16[32,48,1536]{2,1,0:T(8,128)(2,1)S(1)} %bitcast.301), channel_id=1, replica_groups=mesh['seq'=8,'head'=4] {'seq','head'}, dimensions={0} | all-to-all | bytes 9437184 | tf_op jit(solution)/shard_map/all_to_all | solution.py:130
  695.2 4.4 convolution_convert_fusion.1
  699.7 3.6 all-to-all-start.3
  703.3 5.4 copy.224
  715.6 93.0 %all-to-all-done.3 = bf16[32,48,1536]{2,1,0:T(8,128)(2,1)} async-done(((bf16[32,48,1536]{2,1,0:T(8,128)(2,1)}), bf16[32,48,1536]{2,1,0:T(8,128)(2,1)}, u32[]{:S(2)}, u32[]{:S(2)}) %all-to-all-start.3) | async-done | bytes 4718624 | tf_op jit(solution)/shard_map/all_to_all | solution.py:130
  808.6 5.9 convert_reduce_fusion
  814.4 12.7 gather_fusion.1
  827.1 3.4 reshape.735
  830.5 3.6 reduce_sum.378
  838.4 8.7 all_gather.28
  849.5 6.6 psum.71
  856.1 4.3 multiply_reduce_fusion.6
  865.4 7.4 fusion.88
  872.8 16.9 reshape.748
  901.8 5.0 fusion.30
  906.9 5.6 fusion.15
  918.1 3.8 reduce-window.83
  930.0 4.0 rev.7
  934.0 18.6 while.22
  952.6 3.3 convolution_bitcast_fusion.2
  957.6 3.9 multiply_reduce_fusion.4
  987.7 4.0 reduce-window.85
  1009.1 3.9 fusion.61
  1016.6 3.7 convolution_convert_fusion.3
  1024.4 4.8 convolution_convert_fusion
  1029.2 12.5 copy.197
  1042.8 4.6 fusion.121
  1048.2 112.7 %all-reduce.22.cloned.1.call-done = f32[1536,2,1024]{2,1,0:T(2,128)} async-done(((f32[1536,2,1024]{2,1,0:T(2,128)}), f32[1536,2,1024]{2,1,0:T(2,128)}) %all-reduce.22.cloned.1.call-update) | async-done | bytes 12582928
  1162.7 4.6 fusion.162
  1168.8 93.0 %reduce-scatter.24.cloned.1.call-done = f32[48,16]{1,0:T(8,128)} async-done(((f32[1536,16]{1,0:T(8,128)}), f32[48,16]{1,0:T(8,128)}) %reduce-scatter.24.cloned.1.call-update) | async-done | bytes 3088
  1269.1 18.2 reduce-scatter.14.cloned.1.call-done
  1294.0 4.6 convolution_bitcast_fusion
  1298.6 9.4 copy.199
  1308.0 5.0 convolution_bitcast_fusion.1
  1312.9 46.9 %reduce-scatter.18.cloned.1.call-done = bf16[768,192]{0,1:T(8,128)(2,1)} async-done(((bf16[768,1536]{0,1:T(8,128)(2,1)}), bf16[768,192]{0,1:T(8,128)(2,1)}) %reduce-scatter.18.cloned.1.call-update) | async-done | bytes 294928 | tf_op jit(solution)/shard_map/reduce_scatter | solution.py:429
  1361.6 61.9 %reduce-scatter.22.cloned.1.call-done = bf16[192,12]{1,0:T(8,128)(2,1)} async-done(((bf16[1536,12]{1,0:T(8,128)(2,1)}), bf16[192,12]{1,0:T(8,128)(2,1)}) %reduce-scatter.22.cloned.1.call-update) | async-done | bytes 4624
  1427.7 168.2 %all-reduce.20.cloned.1.call-done = bf16[1536,2,768]{2,1,0:T(2,128)(2,1)} async-done(((bf16[1536,2,768]{2,1,0:T(2,128)(2,1)}), bf16[1536,2,768]{2,1,0:T(2,128)(2,1)}) %all-reduce.20.cloned.1.call-update) | async-done | bytes 4718608
  1598.3 116.9 %reduce-scatter.20.cloned.1.call-done = f32[1024,48]{0,1:T(8,128)} async-done(((f32[1024,1536]{0,1:T(8,128)}), f32[1024,48]{0,1:T(8,128)}) %reduce-scatter.20.cloned.1.call-update) | async-done | bytes 196624 | tf_op jit(solution)/shard_map/reduce_scatter | solution.py:437
  1715.2 265.0 %all-reduce.24.cloned.1.call-done = (f32[1536]{0:T(1024)}, f32[4,3072]{1,0:T(4,128)}, f32[4,256]{1,0:T(4,128)}, f32[48]{0:T(128)}, f32[48]{0:T(128)}, /*index=5*/f32[48]{0:T(128)}, f32[3072]{0:T(1024)}, f32[1536]{0:T(1024)}) async-done(((f32[1536]{0:T(1024)}, f32[4,3072]{1,0:T(4,128)}, f32[4,256]{1,0:T(4,128)}, f32[48]{0:T(128)}, f32[48]{0:T(128)}, /*index=5*/f32[48]{0:T(128)}, f32[3072]{0:T(1024)}, ...) | async-done | bytes 78416 | tf_op jit(solution)/shard_map/psum | solution.py:439
  1980.2 105.5 %reduce-scatter.16.cloned.1.call-done = f32[48,256]{1,0:T(8,128)} async-done(((f32[1536,256]{1,0:T(8,128)}), f32[48,256]{1,0:T(8,128)}) %reduce-scatter.16.cloned.1.call-update) | async-done | bytes 49168 | tf_op jit(solution)/shard_map/reduce_scatter | solution.py:434
  (456 shorter events, 255.4 us)
Async XLA Ops:
  7.2 702.8 %copy-start = (bf16[1024,1536]{1,0:T(8,128)(2,1)S(1)}, bf16[1024,1536]{1,0:T(8,128)(2,1)}, u32[]{:S(2)}) copy-start(bf16[1024,1536]{1,0:T(8,128)(2,1)} %param.44) | copy-start | bytes 9437188
  7.2 109.0 %all-gather.6.cloned.1.call-start = ((), (), s32[]{:S(2)}) async-start(), calls=%async_computation.16 | async-start | bytes 3538944 | tf_op jit(solution)/shard_map/all_gather | solution.py:15
  9.1 11.2 copy-start.88
  20.2 5.8 copy-start.3
  25.9 5.7 copy-start.105
  25.9 6.6 copy-start.83
  25.9 6.6 copy-start.93
  25.9 10.9 copy-start.104
  26.0 10.9 copy-start.106
  26.9 22.2 %copy-start.24 = (f32[256,256]{1,0:T(8,128)}, f32[256,256]{1,0:T(8,128)S(1)}, u32[]{:S(2)}) copy-start(f32[256,256]{1,0:T(8,128)S(1)} %fusion.159) | copy-start | bytes 786436
  27.6 17.0 collective-permute-start
  40.0 9.2 copy-start.26
  44.6 8.9 copy-start.58
  50.2 10.3 copy-start.90
  50.2 33.3 %copy-start.77 = (f32[256]{0:T(256)S(1)}, f32[256]{0:T(256)}, u32[]{:S(2)}) copy-start(f32[256]{0:T(256)} %copy-done.76) | copy-start | bytes 3076
  56.1 118.7 %reduce-scatter.12.cloned.1.call-start = ((), (), s32[]{:S(2)}) async-start(), calls=%async_computation.11 | async-start | bytes 1966080 | tf_op jit(solution)/shard_map/reduce_scatter | solution.py:241
  116.2 9.8 copy-start.103
  124.3 8.4 copy-start.78
  126.0 6.7 copy-start.36
  132.6 11.1 copy-start.60
  250.9 110.2 %all-to-all-start = ((bf16[32,48,1536]{2,1,0:T(8,128)(2,1)}), bf16[32,48,1536]{2,1,0:T(8,128)(2,1)}, u32[]{:S(2)}, u32[]{:S(2)}) async-start(bf16[32,48,1536]{2,1,0:T(8,128)(2,1)} %bitcast.300), calls=%async_computation.1 | async-start | bytes 9437184 | tf_op jit(solution)/shard_map/all_to_all | solution.py:130
  366.1 5.3 copy-start.38
  371.4 109.6 %all-to-all-start.1 = ((bf16[32,48,1536]{2,1,0:T(8,128)(2,1)}), bf16[32,48,1536]{2,1,0:T(8,128)(2,1)}, u32[]{:S(2)}, u32[]{:S(2)}) async-start(bf16[32,48,1536]{2,1,0:T(8,128)(2,1)} %bitcast.298), calls=%async_computation.2 | async-start | bytes 9437184 | tf_op jit(solution)/shard_map/all_to_all | solution.py:130
  503.0 8.7 copy-start.57
  503.0 8.7 copy-start.87
  503.0 8.7 copy-start.96
  583.5 109.1 %copy-start.39 = (f32[1536,512]{0,1:T(8,128)S(1)}, f32[1536,512]{0,1:T(8,128)}, u32[]{:S(2)}) copy-start(f32[1536,512]{0,1:T(8,128)} %copy-done.38) | copy-start | bytes 9437188
  583.5 109.1 %copy-start.49 = (bf16[1,256,1536]{2,1,0:T(8,128)(2,1)S(1)}, bf16[1,256,1536]{2,1,0:T(8,128)(2,1)}, u32[]{:S(2)}) copy-start(bf16[1,256,1536]{2,1,0:T(8,128)(2,1)} %param.42) | copy-start | bytes 2359300
  699.7 108.9 %all-to-all-start.3 = ((bf16[32,48,1536]{2,1,0:T(8,128)(2,1)}), bf16[32,48,1536]{2,1,0:T(8,128)(2,1)}, u32[]{:S(2)}, u32[]{:S(2)}) async-start(bf16[32,48,1536]{2,1,0:T(8,128)(2,1)} %bitcast.323), calls=%async_computation.4 | async-start | bytes 9437184 | tf_op jit(solution)/shard_map/all_to_all | solution.py:130
  703.2 226.8 %all-gather.8.cloned.1.call-start = ((), (), s32[]{:S(2)}) async-start(), calls=%async_computation.17 | async-start | bytes 3538944 | tf_op jit(solution)/shard_map/all_gather | solution.py:15
  703.3 5.5 copy-start.23
  834.1 13.1 copy-start.5
  834.1 13.1 copy-start.41
  838.4 17.7 copy-start.94
  865.4 295.5 %all-reduce.22.cloned.1.call-start = ((), (), s32[]{:S(2)}) async-start(), calls=%async_computation.21 | async-start | bytes 25165824
  889.8 372.0 %reduce-scatter.24.cloned.1.call-start = ((), (), s32[]{:S(2)}) async-start(), calls=%async_computation.19 | async-start | bytes 811008
  898.5 388.7 %reduce-scatter.14.cloned.1.call-start = ((), (), s32[]{:S(2)}) async-start(), calls=%async_computation.12 | async-start | bytes 983040 | tf_op jit(solution)/shard_map/reduce_scatter | solution.py:400
  906.9 5.6 copy-start.35
  906.9 5.6 copy-start.37
  906.9 5.8 copy-start.84
  963.9 8.1 copy-start.54
  963.9 11.2 copy-start.25
  963.9 11.2 copy-start.80
  963.9 11.2 copy-start.81
  969.3 5.8 copy-start.2
  980.9 24.8 %collective-permute-start.1 = (f32[3,1024]{1,0:T(4,128)}, f32[3,1024]{1,0:T(4,128)}, u32[]{:S(2)}, u32[]{:S(2)}) collective-permute-start(f32[3,1024]{1,0:T(4,128)} %pad_add_fusion.1), channel_id=1, source_target_pairs={{4,0},{8,4},{12,8},{16,12},{20,16},{24,20},{28,24},{5,1},{9,5},{13... | collective-permute-start | bytes 36872 | tf_op jit(solution)/shard_map/ppermute | solution.py:33
  1016.6 343.3 %reduce-scatter.18.cloned.1.call-start = ((), (), s32[]{:S(2)}) async-start(), calls=%async_computation.14 | async-start | bytes 2654208 | tf_op jit(solution)/shard_map/reduce_scatter | solution.py:429
  1020.3 403.2 %reduce-scatter.22.cloned.1.call-start = ((), (), s32[]{:S(2)}) async-start(), calls=%async_computation.18 | async-start | bytes 442368
  1024.4 571.5 %all-reduce.20.cloned.1.call-start = ((), (), s32[]{:S(2)}) async-start(), calls=%async_computation.20 | async-start | bytes 9437184
  1041.8 673.4 %reduce-scatter.20.cloned.1.call-start = ((), (), s32[]{:S(2)}) async-start(), calls=%async_computation.15 | async-start | bytes 6488064 | tf_op jit(solution)/shard_map/reduce_scatter | solution.py:437
  1047.4 119.9 %copy-start.20 = (f32[64,1536]{1,0:T(8,128)S(1)}, f32[64,1536]{1,0:T(8,128)}, u32[]{:S(2)}) copy-start(f32[64,1536]{1,0:T(8,128)} %copy-done.19) | copy-start | bytes 1179652
  1047.5 932.7 %all-reduce.24.cloned.1.call-start = ((), (), s32[]{:S(2)}) async-start(), calls=%async_computation.22 | async-start | bytes 166912 | tf_op jit(solution)/shard_map/psum | solution.py:439
  1160.9 6.4 copy-start.43
  1167.3 98.9 %copy-start.68 = (f32[1024]{0:T(1024)S(1)}, f32[1024]{0:T(1024)}, u32[]{:S(2)}) copy-start(f32[1024]{0:T(1024)} %get-tuple-element.676) | copy-start | bytes 12292
  1167.3 98.9 %copy-start.69 = (f32[1024]{0:T(1024)S(1)}, f32[1024]{0:T(1024)}, u32[]{:S(2)}) copy-start(f32[1024]{0:T(1024)} %get-tuple-element.677) | copy-start | bytes 12292
  1167.3 119.9 %copy-start.63 = (f32[1536]{0:T(1024)S(1)}, f32[1536]{0:T(1024)}, u32[]{:S(2)}) copy-start(f32[1536]{0:T(1024)} %param.28) | copy-start | bytes 18436
  1264.5 24.6 %copy-start.101 = (f32[48]{0:T(128)}, f32[48]{0:T(128)S(1)}, u32[]{:S(2)}) copy-start(f32[48]{0:T(128)S(1)} %dynamic_update_slice.87) | copy-start | bytes 580
  1265.4 23.7 %copy-start.66 = (f32[3072]{0:T(1024)}, f32[3072]{0:T(1024)S(1)}, u32[]{:S(2)}) copy-start(f32[3072]{0:T(1024)S(1)} %dynamic_update_slice.88) | copy-start | bytes 36868
  1266.2 22.9 %copy-start.102 = (f32[48]{0:T(128)}, f32[48]{0:T(128)S(1)}, u32[]{:S(2)}) copy-start(f32[48]{0:T(128)S(1)} %dynamic_update_slice.85) | copy-start | bytes 580
  1269.0 20.1 copy-start.100
  1269.0 20.1 copy-start.61
  1289.2 796.5 %reduce-scatter.16.cloned.1.call-start = ((), (), s32[]{:S(2)}) async-start(), calls=%async_computation.13 | async-start | bytes 1622016 | tf_op jit(solution)/shard_map/reduce_scatter | solution.py:434
  1298.6 9.4 copy-start.29
  1308.0 117.7 %copy-start.21 = (f32[64,1536]{1,0:T(8,128)S(1)}, f32[64,1536]{1,0:T(8,128)}, u32[]{:S(2)}) copy-start(f32[64,1536]{1,0:T(8,128)} %param.27) | copy-start | bytes 1179652
  (60 other events, 181.0 us)
Sparse Core Ops, SparseCore 0:
  56.3 59.8 all-gather.5
  147.8 26.9 reduce-scatter.11
  865.5 59.6 all-gather.7
  932.1 228.7 all-reduce.21
  1166.6 95.0 reduce-scatter.23
  1264.9 22.3 reduce-scatter.13
  1290.8 69.0 reduce-scatter.17
  1363.1 60.4 reduce-scatter.21
  1427.1 168.6 all-reduce.19
  1601.9 113.2 reduce-scatter.19
  1723.9 256.1 all-reduce.23
  1987.3 98.2 reduce-scatter.15
where the time goes:
time: 2120 us; the launch traced here: 2100 us
  waiting for transfers between devices  1320 us (62%)
  local copies, waits for them, and re-layouts  319 us (15%)
  blocking collectives  160 us (8%)
  matrix products  141 us (7%)
  other arithmetic  125 us (6%)
    unnamed x16, waiting for transfers between devices  436 us
    all_to_all x3, waiting for transfers between devices, route_rows(): lax.all_to_all(slot_rows, ('seq', 'head'), split_axis=0, concat_axis=0, t...  288 us
    psum x1, waiting for transfers between devices, local(): lax.psum((grad_norm1, grad_norm2, widen(grad_conv[:, :inner_local], 1), g...  265 us
    reduce_scatter x1, waiting for transfers between devices, local(): lax.psum_scatter(grad_shared_down, ('seq', 'head'), scatter_dimension=1,...  117 us
    all_to_all x1, blocking collectives, route_rows(): lax.all_to_all(slot_rows, ('seq', 'head'), split_axis=0, concat_axis=0, t...  109 us
    reduce_scatter x1, waiting for transfers between devices, local(): lax.psum_scatter(grad_bc, ('seq', 'head'), scatter_dimension=0, tiled=True)  106 us
    scatter x1, local copies, waits for them, and re-layouts, local(): grad_send = jnp.zeros((expert_count, capacity, model_width), jnp.bfloat16...  62.2 us
    scatter x1, local copies, waits for them, and re-layouts, local(): send_one = jnp.zeros((expert_count, capacity, model_width), jnp.bfloat16)...  61.9 us
  transfers between devices with their start and end apart: 17, of which 14 were waited for; matrix products, arithmetic and copies ran while one was open for 14% of the time, Pallas kernels for 0%

commit v1 on v0

v1 whole, which is shorter than its diff:
```python
import functools
import jax
import jax.numpy as jnp
from jax import lax
from jax.experimental import pallas as pl
from jax.experimental.pallas import tpu as pltpu
from jax.sharding import PartitionSpec as P

MESH = pl.DeviceIdType.MESH
BLOCK = 256
EPS = 1e-05
LANES = 128
B16 = jnp.bfloat16
F32 = jnp.float32


def mm(left, right, dims=(((1,), (0,)), ((), ()))):
    return lax.dot_general(left, right, dims, preferred_element_type=F32)


NT = (((1,), (1,)), ((), ()))
TN = (((0,), (0,)), ((), ()))


def inverse_rms(values):
    return lax.rsqrt(jnp.mean(values * values, axis=-1, keepdims=True) + EPS)


def rms_back(values, inverse, gain, grad):
    weighted = grad * gain
    inner = jnp.mean(weighted * values, axis=-1, keepdims=True)
    return inverse * weighted - values * inverse**3 * inner


def silu_grad(values):
    sig = jax.nn.sigmoid(values)
    return sig * (1.0 + values * (1.0 - sig))


def pad_lanes(values, width):
    return jnp.pad(values, [(0, 0)] * (values.ndim - 1) + [(0, width - values.shape[-1])])


def hi_lo(values):
    high = values.astype(B16)
    return high, (values - high.astype(F32)).astype(B16)


def sizes(seq_size, head_size):
    return head_size // 2, head_size // 2, seq_size // (head_size // 2)


class Place:
    def __init__(self, seq_size, head_size):
        self.H = head_size
        self.X, self.Y, self.Z = sizes(seq_size, head_size)
        seq, head = lax.axis_index("seq"), lax.axis_index("head")
        self.z, self.y = seq // self.Y, seq % self.Y
        self.x, self.c = head // 2, head % 2

    def dev(self, dz=0, dy=0, dx=0, dc=0):
        z, y, x, c = self.at(dz, dy, dx, dc)
        return (z * self.Y + y, x * 2 + c)

    def at(self, dz=0, dy=0, dx=0, dc=0):
        return (
            (self.z + dz) % self.Z if dz else self.z,
            (self.y + dy) % self.Y if dy else self.y,
            (self.x + dx) % self.X if dx else self.x,
            (self.c + dc) % 2 if dc else self.c,
        )

    def slot(self, dz=0, dy=0, dx=0, dc=0):
        z, y, x, c = self.at(dz, dy, dx, dc)
        return (z * self.Y + y) * self.H + x * 2 + c

    def peers(self):
        out = [self.dev(dz=k) for k in range(1, self.Z)]
        out += [self.dev(dy=k) for k in range(1, self.Y)]
        out += [self.dev(dx=k) for k in range(1, self.X)]
        return out + [self.dev(dc=1)]


    def order(self):
        return list(range(1, self.Z)) + [0]


def greet(peers):
    barrier = pltpu.get_barrier_semaphore()
    for peer in peers:
        pl.semaphore_signal(barrier, inc=1, device_id=peer, device_id_type=MESH)
    pl.semaphore_wait(barrier, len(peers))


class Mail:
    def __init__(self, send, recv):
        self.send, self.recv, self.sent = send, recv, []

    def start(self, src, dst, dev):
        i = len(self.sent)
        copy = pltpu.make_async_remote_copy(
            src_ref=src, dst_ref=dst, send_sem=self.send.at[i], recv_sem=self.recv.at[i],
            device_id=dev, device_id_type=MESH,
        )
        copy.start()
        self.sent.append(copy)
        return copy

    def finish(self, count):
        assert len(self.sent) == count
        for copy in self.sent:
            copy.wait_send()


def gather_count(S, H):
    X, Y, Z = sizes(S, H)
    return (Z - 1) + 2 * Z * (X + Y - 2) + 2 * Z * (X - 1) * (Y - 1) + X * Y * Z


def gather(pc, mail, x_ref, out_ref, own_sem):
    X, Y, Z = pc.X, pc.Y, pc.Z
    R = x_ref.shape[0]
    half = R // 2

    def rows(part, **where):
        base = pl.multiple_of(pc.slot(**where) * R, R)
        if part is None:
            return out_ref.at[pl.ds(base, R)]
        return out_ref.at[pl.ds(pl.multiple_of(base + part * half, half), half)]

    own = pltpu.make_async_copy(x_ref, rows(None), own_sem)
    own.start()
    z_in, x_in, y_in, dga, dgb, sib = {}, {}, {}, {}, {}, []
    for dz in range(1, Z):
        z_in[dz] = mail.start(x_ref, rows(None), pc.dev(dz=dz))

    def column(dz):
        for part in (0, 1):
            src = x_ref.at[pl.ds(part * half, half)] if dz == 0 else rows(part, dz=-dz)
            for k in range(1, X):
                x_in[dz, k, part] = mail.start(src, rows(part, dz=-dz), pc.dev(dx=k))
            other = 1 - part
            src = x_ref.at[pl.ds(other * half, half)] if dz == 0 else rows(other, dz=-dz)
            for k in range(1, Y):
                y_in[dz, k, other] = mail.start(src, rows(other, dz=-dz), pc.dev(dy=k))
        src = x_ref if dz == 0 else rows(None, dz=-dz)
        sib.append(mail.start(src, rows(None, dz=-dz), pc.dev(dc=1)))

    column(0)
    for dz in range(Z):
        if dz + 1 < Z:
            z_in[dz + 1].wait_recv()
            column(dz + 1)
        for k in range(1, X):
            x_in[dz, k, 0].wait_recv()
            block = rows(0, dz=-dz, dx=-k)
            for m in range(1, Y):
                dga[dz, k, m] = mail.start(block, block, pc.dev(dy=m))
        for k in range(1, Y):
            y_in[dz, k, 1].wait_recv()
            block = rows(1, dz=-dz, dy=-k)
            for m in range(1, X):
                dgb[dz, k, m] = mail.start(block, block, pc.dev(dx=m))
        for k in range(1, X):
            x_in[dz, k, 1].wait_recv()
            block = rows(None, dz=-dz, dx=-k)
            sib.append(mail.start(block, block, pc.dev(dc=1)))
        for k in range(1, Y):
            y_in[dz, k, 0].wait_recv()
            block = rows(None, dz=-dz, dy=-k)
            sib.append(mail.start(block, block, pc.dev(dc=1)))
    for dz in range(Z):
        for k in range(1, X):
            for m in range(1, Y):
                dga[dz, k, m].wait_recv()
                dgb[dz, m, k].wait_recv()
                block = rows(None, dz=-dz, dx=-k, dy=-m)
                sib.append(mail.start(block, block, pc.dev(dc=1)))
    for copy in sib:
        copy.wait_recv()
    own.wait()


def scatter_parts(split):
    return (("y", 0), ("x", 1)) if split else (("x", None),)


def scatter_count(S, H, splits=(True,)):
    X, Y, Z = sizes(S, H)
    pieces = sum(len(scatter_parts(split)) for split in splits)
    return len(splits) * (Z + Z - 1) + pieces * Z * (X + Y - 2)


def scatter_scratch(S, H, R, W, split=True):
    X, Y, Z = sizes(S, H)
    out = [pltpu.VMEM((Z, Y, X, R, W), B16), pltpu.VMEM((Z, Y, X, R, W), B16), pltpu.VMEM((Z - 1, R, W), B16)]
    for axis, part in scatter_parts(split):
        rows = R if part is None else R // 2
        first, second = (Y, X) if axis == "y" else (X, Y)
        out += [pltpu.VMEM((Z, first - 1, second, rows, W), B16), pltpu.VMEM((Z, second - 1, rows, W), B16)]
    return out + [pltpu.SemaphoreType.DMA((Z,))]


def accumulate(dst, srcs, rows):
    def body(i, carry):
        at = pl.ds(pl.multiple_of(i * 16, 16), 16)
        total = dst.at[at][...].astype(F32)
        for src in srcs:
            total = total + src.at[at][...].astype(F32)
        dst.at[at][...] = total.astype(dst.dtype)
        return carry

    lax.fori_loop(0, rows // 16, body, 0)


def scatter_local(pc, jobs):
    X, Y, Z = pc.X, pc.Y, pc.Z
    own = {}
    for o, (p_ref, total, scratch, split) in enumerate(jobs):
        for dz in pc.order():
            own[o, dz] = pltpu.make_async_copy(
                p_ref.at[pc.at(dz=dz)[0], :, :, pc.c], scratch[0].at[dz], scratch[-1].at[dz]
            )
            own[o, dz].start()
    return own


def scatter(pc, mail, jobs, own, between=None):
    X, Y, Z = pc.X, pc.Y, pc.Z
    sib, one, two, zs = {}, {}, {}, {}

    def pieces(o):
        p_ref, total, scratch, split = jobs[o]
        R = p_ref.shape[4]
        for j, (axis, part) in enumerate(scatter_parts(split)):
            rows, size = (pl.ds(0, R), R) if part is None else (pl.ds(part * (R // 2), R // 2), R // 2)
            yield j, axis, rows, size, scratch[3 + 2 * j], scratch[4 + 2 * j]

    for dz in pc.order():
        for o, (p_ref, total, scratch, split) in enumerate(jobs):
            sib[o, dz] = mail.start(p_ref.at[pc.at(dz=dz)[0], :, :, 1 - pc.c], scratch[1].at[dz], pc.dev(dc=1))
    for dz in pc.order():
        for o, (p_ref, total, scratch, split) in enumerate(jobs):
            t0, r0 = scratch[0], scratch[1]
            own[o, dz].wait()
            sib[o, dz].wait_recv()
            for yy in range(Y):
                for xx in range(X):
                    accumulate(t0.at[dz, yy, xx], [r0.at[dz, yy, xx]], p_ref.shape[4])
            for j, axis, rows, size, r1, r2 in pieces(o):
                for k in range(1, Y if axis == "y" else X):
                    if axis == "y":
                        src, dev = t0.at[dz, pc.at(dy=k)[1], :, rows], pc.dev(dy=k)
                    else:
                        src, dev = t0.at[dz, :, pc.at(dx=k)[2], rows], pc.dev(dx=k)
                    one[o, dz, j, k] = mail.start(src, r1.at[dz, k - 1], dev)
    if between is not None:
        between()
    for dz in pc.order():
        for o, (p_ref, total, scratch, split) in enumerate(jobs):
            t0 = scratch[0]
            for j, axis, rows, size, r1, r2 in pieces(o):
                firsts = range(1, Y if axis == "y" else X)
                for k in firsts:
                    one[o, dz, j, k].wait_recv()
                for m in range(X if axis == "y" else Y):
                    dst = t0.at[dz, pc.y, m, rows] if axis == "y" else t0.at[dz, m, pc.x, rows]
                    accumulate(dst, [r1.at[dz, k - 1, m] for k in firsts], size)
                for k in range(1, X if axis == "y" else Y):
                    if axis == "y":
                        src, dev = t0.at[dz, pc.y, pc.at(dx=k)[2], rows], pc.dev(dx=k)
                    else:
                        src, dev = t0.at[dz, pc.at(dy=k)[1], pc.x, rows], pc.dev(dy=k)
                    two[o, dz, j, k] = mail.start(src, r2.at[dz, k - 1], dev)
    for dz in pc.order():
        for o, (p_ref, total, scratch, split) in enumerate(jobs):
            mine = scratch[0].at[dz, pc.y, pc.x]
            for j, axis, rows, size, r1, r2 in pieces(o):
                seconds = range(1, X if axis == "y" else Y)
                for k in seconds:
                    two[o, dz, j, k].wait_recv()
                accumulate(mine.at[rows], [r2.at[dz, k - 1] for k in seconds], size)
            if dz:
                zs[o, dz] = mail.start(mine, scratch[2].at[dz - 1], pc.dev(dz=dz))
    for o, (p_ref, total, scratch, split) in enumerate(jobs):
        for dz in range(1, Z):
            zs[o, dz].wait_recv()

        def last(i, carry, total=total, scratch=scratch):
            at = pl.ds(pl.multiple_of(i * 16, 16), 16)
            value = scratch[0].at[0, pc.y, pc.x, at][...].astype(F32)
            for k in range(Z - 1):
                value = value + scratch[2].at[k, at][...].astype(F32)
            total.at[at][...] = value
            return carry

        lax.fori_loop(0, p_ref.shape[4] // 16, last, 0)


ANY = pl.BlockSpec(memory_space=pl.ANY)
VMEM = pl.BlockSpec(memory_space=pltpu.VMEM)


def sems(count):
    return [pltpu.SemaphoreType.DMA((count,)), pltpu.SemaphoreType.DMA((count,))]


def talking(cid):
    return pltpu.CompilerParams(collective_id=cid, has_side_effects=True, vmem_limit_bytes=56 * 1024 * 1024)


def first_kernel(S, H, in_ref, gain_ref, named_ref, out_ref, rows, send, recv, own_sem):
    pc = Place(S, H)
    D = in_ref.shape[1]
    values = in_ref[...]
    rows[:, :D] = (values * inverse_rms(values) * gain_ref[...]).astype(B16)
    rows[:, D:] = named_ref[...]
    greet(pc.peers())
    mail = Mail(send, recv)
    gather(pc, mail, rows, out_ref, own_sem)
    mail.finish(gather_count(S, H))


def first_rows(hidden_in, gain, named, S, H):
    R, D = hidden_in.shape
    W = D + LANES
    return pl.pallas_call(
        functools.partial(first_kernel, S, H),
        out_shape=jax.ShapeDtypeStruct((S * H * R, W), B16),
        in_specs=[VMEM] * 3,
        out_specs=ANY,
        scratch_shapes=[pltpu.VMEM((R, W), B16), *sems(gather_count(S, H)), pltpu.SemaphoreType.DMA],
        compiler_params=talking(1),
    )(hidden_in, gain, named)


def blocks(part, S, H):
    X, Y, Z = sizes(S, H)
    return part.reshape(Z, Y, X, 2, part.shape[0] // (S * H), part.shape[1])


def second_kernel(S, H, width, p_ref, in_ref, gain_ref, out_ref, res_ref, mixed_ref, inv_ref, total, rows, *rest):
    scratch, (send, recv, own_sem) = rest[:-3], rest[-3:]
    pc = Place(S, H)
    D = in_ref.shape[1]
    jobs = [(p_ref, total, scratch, True)]
    own = scatter_local(pc, jobs)
    greet(pc.peers())
    mail = Mail(send, recv)
    scatter(pc, mail, jobs, own)
    mixed = total[:, :D]
    square = jnp.sum(total[:, D:], axis=1, keepdims=True)
    inv = lax.rsqrt(square / width + EPS)
    residual = in_ref[...] + inv * mixed
    mixed_ref[...] = mixed
    res_ref[...] = residual
    inv_ref[...] = jnp.broadcast_to(inv, inv_ref.shape)
    rows[...] = (residual * inverse_rms(residual) * gain_ref[...]).astype(B16)
    gather(pc, mail, rows, out_ref, own_sem)
    mail.finish(scatter_count(S, H) + gather_count(S, H))


def second_rows(part, hidden_in, gain, width, S, H):
    R, D = hidden_in.shape
    count = scatter_count(S, H) + gather_count(S, H)
    return pl.pallas_call(
        functools.partial(second_kernel, S, H, width),
        out_shape=[
            jax.ShapeDtypeStruct((S * H * R, D), B16),
            jax.ShapeDtypeStruct((R, D), F32),
            jax.ShapeDtypeStruct((R, D), F32),
            jax.ShapeDtypeStruct((R, LANES), F32),
        ],
        in_specs=[ANY, VMEM, VMEM],
        out_specs=[ANY, VMEM, VMEM, VMEM],
        scratch_shapes=[
            pltpu.VMEM((R, D + LANES), F32), pltpu.VMEM((R, D), B16), *scatter_scratch(S, H, R, D + LANES),
            *sems(count), pltpu.SemaphoreType.DMA,
        ],
        compiler_params=talking(2),
    )(blocks(part, S, H), hidden_in, gain)


def third_kernel(
    S, H, width, p_ref, probs_ref, res_ref, mixed_ref, inv_ref, grad_ref, gain_ref, router_ref,
    out_ref, gres_ref, gnorm_ref, grouter_ref, total, rows, probs, *rest,
):
    scratch, (send, recv, own_sem, probs_sem) = rest[:-4], rest[-4:]
    pc = Place(S, H)
    R, D = res_ref.shape
    jobs = [(p_ref, total, scratch, True)]
    own = scatter_local(pc, jobs)
    fetch = pltpu.make_async_copy(probs_ref.at[pl.ds(pl.multiple_of(pc.slot() * R, R), R)], probs, probs_sem)
    fetch.start()
    greet(pc.peers())
    mail = Mail(send, recv)
    scatter(pc, mail, jobs, own)
    fetch.wait()
    p = probs[...]
    gp = total[:, D:]
    glogits = (p * (gp - jnp.sum(p * gp, axis=1, keepdims=True))).astype(B16)
    gtwo = total[:, :D] + mm(glogits, router_ref[...], NT)
    residual = res_ref[...]
    inv_two = inverse_rms(residual)
    gain = gain_ref[...]
    gres = grad_ref[...] + rms_back(residual, inv_two, gain, gtwo)
    gres_ref[...] = gres
    inv = inv_ref[:, 0:1]
    cross = jnp.sum(gres * mixed_ref[...], axis=1, keepdims=True) * (inv * inv * inv) / width
    high, low = hi_lo(cross)
    lane = lax.broadcasted_iota(jnp.int32, (R, LANES), 1)
    rows[:, :D] = (inv * gres).astype(B16)
    rows[:, D:] = jnp.where(lane == 0, high.astype(F32), jnp.where(lane == 1, low.astype(F32), 0.0)).astype(B16)
    gnorm_ref[...] = jnp.sum(gtwo * residual * inv_two, axis=0, keepdims=True)
    grouter_ref[...] = mm((residual * inv_two * gain).astype(B16), glogits, TN).astype(B16)
    gather(pc, mail, rows, out_ref, own_sem)
    mail.finish(scatter_count(S, H) + gather_count(S, H))


def third_rows(part, probs, residual, mixed, inv_gate, out_grad, gain, router, width, S, H):
    R, D = residual.shape
    count = scatter_count(S, H) + gather_count(S, H)
    return pl.pallas_call(
        functools.partial(third_kernel, S, H, width),
        out_shape=[
            jax.ShapeDtypeStruct((S * H * R, D + LANES), B16),
            jax.ShapeDtypeStruct((R, D), F32),
            jax.ShapeDtypeStruct((1, D), F32),
            jax.ShapeDtypeStruct((D, LANES), B16),
        ],
        in_specs=[ANY, ANY] + [VMEM] * 6,
        out_specs=[ANY, VMEM, VMEM, VMEM],
        scratch_shapes=[
            pltpu.VMEM((R, D + LANES), F32), pltpu.VMEM((R, D + LANES), B16), pltpu.VMEM((R, LANES), F32),
            *scatter_scratch(S, H, R, D + LANES), *sems(count), pltpu.SemaphoreType.DMA, pltpu.SemaphoreType.DMA,
        ],
        compiler_params=talking(3),
    )(blocks(part, S, H), probs, residual, mixed, inv_gate, out_grad, gain, router)


def last_kernel(
    S, H, p_ref, e_ref, zx_ref, wo_ref, su_ref, sd_ref, small_ref, in_ref, gres_ref, gain_ref,
    gin_ref, extra_ref, norm_ref, zx_out, wo_out, su_out, sd_out, small_out,
    total, norm_in, *rest,
):
    half = len(rest) - 7
    main, extra = rest[: half - 6], rest[half - 6 : half]
    send, recv, all_send, all_recv, local_sem, norm_send, norm_recv = rest[half:]
    pc = Place(S, H)
    N = S * H
    me = pc.slot()
    seq, head = lax.axis_index("seq"), lax.axis_index("head")
    jobs = [(p_ref, total, main, True), (e_ref, extra_ref, extra, False)]
    own = scatter_local(pc, jobs)
    barrier = pltpu.get_barrier_semaphore()

    def other(m):
        to = (me + m) % N
        return to, (to // H, to % H)

    def hello(m, carry):
        pl.semaphore_signal(barrier, inc=1, device_id=other(m)[1], device_id_type=MESH)
        return carry

    lax.fori_loop(1, N, hello, 0)
    pl.semaphore_wait(barrier, N - 1)
    mail = Mail(send, recv)

    def to_group(m):
        to = (seq + m) % S
        return [
            pltpu.make_async_remote_copy(
                src_ref=src.at[to], dst_ref=dst.at[seq], send_sem=all_send.at[j, m], recv_sem=all_recv.at[j, m],
                device_id=(to, head), device_id_type=MESH,
            )
            for j, (src, dst) in enumerate(((zx_ref, zx_out), (wo_ref, wo_out)))
        ]

    def to_all(m):
        to, dev = other(m)
        return [
            pltpu.make_async_remote_copy(
                src_ref=src, dst_ref=dst.at[me], send_sem=all_send.at[2 + j, m], recv_sem=all_recv.at[2 + j, m],
                device_id=dev, device_id_type=MESH,
            )
            for j, (src, dst) in enumerate(((su_ref.at[to], su_out), (sd_ref.at[to], sd_out), (small_ref, small_out)))
        ]

    def each(function, make, count):
        def body(m, carry):
            for copy in make(m):
                function(copy)
            return carry

        lax.fori_loop(1, count, body, 0)

    stay = [
        pltpu.make_async_copy(src, dst, local_sem.at[j])
        for j, (src, dst) in enumerate(
            (
                (zx_ref.at[seq], zx_out.at[seq]), (wo_ref.at[seq], wo_out.at[seq]), (su_ref.at[me], su_out.at[me]),
                (sd_ref.at[me], sd_out.at[me]), (small_ref, small_out.at[me]),
            )
        )
    ]
    for copy in stay:
        copy.start()

    def exchange():
        each(lambda c: c.start(), to_group, S)
        each(lambda c: c.start(), to_all, N)

    scatter(pc, mail, jobs, own, exchange)
    values, gone = in_ref[...], total[...]
    inv = inverse_rms(values)
    gin_ref[...] = gres_ref[...] + rms_back(values, inv, gain_ref[...], gone)
    gnorm = jnp.sum(gone * values * inv, axis=0, keepdims=True)
    D = values.shape[1]
    norm_in[me] = jnp.zeros(norm_in.shape[1:], F32)
    for j in range(D // LANES):
        norm_in[me, j : j + 1, :] = gnorm[:, j * LANES : (j + 1) * LANES]

    def norm_to(m):
        return [
            pltpu.make_async_remote_copy(
                src_ref=norm_in.at[me], dst_ref=norm_in.at[me], send_sem=norm_send.at[m], recv_sem=norm_recv.at[m],
                device_id=other(m)[1], device_id_type=MESH,
            )
        ]

    each(lambda c: c.start(), norm_to, N)
    each(lambda c: c.wait_recv(), to_group, S)
    each(lambda c: c.wait_recv(), to_all, N)
    each(lambda c: c.wait_recv(), norm_to, N)

    def add(k, value):
        return value + norm_in[k]

    norm_ref[...] = lax.fori_loop(0, N, add, jnp.zeros(norm_ref.shape, F32))
    each(lambda c: c.wait_send(), to_group, S)
    each(lambda c: c.wait_send(), to_all, N)
    each(lambda c: c.wait_send(), norm_to, N)
    mail.finish(scatter_count(S, H, (True, False)))
    for copy in stay:
        copy.wait()


def last_rows(part, extra, zx, wo, su, sd, small, hidden_in, grad_res, gain, S, H):
    R, D = hidden_in.shape
    N = S * H
    rows = -(-(D // LANES) // 8) * 8
    count = scatter_count(S, H, (True, False))
    like = [jax.ShapeDtypeStruct(v.shape, v.dtype) for v in (zx, wo, su, sd)]
    return pl.pallas_call(
        functools.partial(last_kernel, S, H),
        out_shape=[
            jax.ShapeDtypeStruct((R, D), F32),
            jax.ShapeDtypeStruct((extra.shape[0] // N, extra.shape[1]), F32),
            jax.ShapeDtypeStruct((rows, LANES), F32),
            *like,
            jax.ShapeDtypeStruct((N,) + small.shape, F32),
        ],
        in_specs=[ANY] * 7 + [VMEM] * 3,
        out_specs=[VMEM] * 3 + [ANY] * 5,
        scratch_shapes=[
            pltpu.VMEM((R, D), F32), pltpu.VMEM((N, rows, LANES), F32), *scatter_scratch(S, H, R, D),
            *scatter_scratch(S, H, extra.shape[0] // N, extra.shape[1], False), *sems(count),
            pltpu.SemaphoreType.DMA((5, N)), pltpu.SemaphoreType.DMA((5, N)), pltpu.SemaphoreType.DMA((5,)),
            *sems(N),
        ],
        compiler_params=talking(4),
    )(blocks(part, S, H), blocks(extra, S, H), zx, wo, su, sd, small, hidden_in, grad_res, gain)


def seg_of(pos, ends_ref, count):
    found = jnp.zeros(pos.shape, jnp.int32)
    for k in range(count):
        found = found + (pos >= ends_ref[k]).astype(jnp.int32)
    return jnp.where(pos < 0, -1, found)


def exact(left, right):
    return jnp.dot(left, right, precision=lax.Precision.HIGHEST, preferred_element_type=F32)


def silu(values):
    return values / (1.0 + jnp.exp(-values))


def softplus(values):
    return jnp.maximum(values, 0.0) + jnp.log1p(jnp.exp(-jnp.abs(values)))


class Block:
    def __init__(self, i, pre, ext, z, taps_ref, rows_ref, ends_ref, count, state, C):
        n = BLOCK
        pos = i * n + lax.broadcasted_iota(jnp.int32, (n, 1), 0)
        pos_row = i * n + lax.broadcasted_iota(jnp.int32, (1, n), 1)
        seg, seg_row = seg_of(pos, ends_ref, count), seg_of(pos_row, ends_ref, count)
        self.joined = {k: ((pos >= k) & (seg_of(pos - k, ends_ref, count) == seg)).astype(F32) for k in (1, 2, 3)}
        self.later = {k: (seg_of(pos + k, ends_ref, count) == seg).astype(F32) for k in (1, 2, 3)}
        conv = taps_ref[3:4, :] * pre
        for k in (1, 2, 3):
            conv = conv + taps_ref[3 - k : 4 - k, :] * ext[8 - k : 8 - k + n, :] * self.joined[k]
        act = silu(conv)
        cp = act.shape[1] - 2 * state
        self.conv = conv
        self.x, self.b, self.c = act[:, :cp], act[:, cp : cp + state].astype(B16), act[:, cp + state :].astype(B16)
        self.m = [rows_ref[j : j + 1, :] for j in range(2)]
        self.skip, self.gain = rows_ref[2:3, :], rows_ref[3:4, :]
        self.C = C
        self.dtr = z + rows_ref[4:5, :]
        self.dt = softplus(self.dtr)
        self.decay = rows_ref[5:6, :]
        self.rate = -self.dt * self.decay
        row, col = lax.broadcasted_iota(jnp.int32, (n, n), 0), lax.broadcasted_iota(jnp.int32, (n, n), 1)
        lower = row >= col
        self.row, self.col = row, col
        logdec = exact(lower.astype(F32), self.rate)
        log_row = logdec.T
        linked = lower & (seg == seg_row)
        self.decays = [
            jnp.exp(jnp.where(linked, logdec[:, C + j : C + j + 1] - log_row[C + j : C + j + 1, :], -1e30)) for j in range(2)
        ]
        scores = mm(self.c, self.b, NT)
        self.mats = [(scores * d).astype(B16) for d in self.decays]
        before = jnp.where(i == 0, -1, seg_of(jnp.full((1, 1), i * n - 1, jnp.int32), ends_ref, count))
        final = seg_of(jnp.full((1, 1), i * n + n - 1, jnp.int32), ends_ref, count)
        last = logdec[n - 1 : n, :]
        self.carry = self.spread(jnp.where(seg == before, jnp.exp(logdec), 0.0))
        self.tail = self.spread(jnp.where(seg == final, jnp.exp(last - logdec), 0.0))
        self.keep = self.spread(jnp.where(final == before, jnp.exp(last), 0.0))
        self.dtc = self.spread(self.dt)
        self.xt = (self.dtc * self.x).astype(B16)
        self.low = [m.astype(B16) for m in self.m]
        self.xts = [self.xt * low for low in self.low]
        self.tail_xt = (self.tail * self.xt.astype(F32)).astype(B16)

    def spread(self, values):
        return values[:, self.C : self.C + 1] * self.m[0] + values[:, self.C + 1 : self.C + 2] * self.m[1]

    def inner(self):
        return mm(self.mats[0], self.xts[0]) + mm(self.mats[1], self.xts[1])


def mixer_forward_kernel(
    count, state, C, ends_ref, in_ref, w_ref, taps_ref, rows_ref, out_w_ref,
    pre_ref, z_ref, y_ref, st_ref, part_ref, held, ext,
):
    i = pl.program_id(0)
    depth = w_ref.shape[0]
    n, cp = BLOCK, z_ref.shape[1]

    @pl.when(i == 0)
    def _():
        held[...] = jnp.zeros_like(held)
        ext[0:8, :] = jnp.zeros((8, ext.shape[1]), F32)

    made = mm(in_ref[:, :depth], w_ref[...])
    z = made[:, :cp]
    pre = made[:, cp:]
    z_ref[...], pre_ref[...] = z, pre
    ext[8 : 8 + n, :] = pre
    blk = Block(i, pre, ext, z, taps_ref, rows_ref, ends_ref, count, state, C)
    ext[0:8, :] = pre[n - 8 :, :]
    st = held[...]
    st_ref[0] = st
    y = blk.inner() + blk.carry * mm(blk.c, st.astype(B16))
    held[...] = blk.keep * st + mm(blk.b, blk.tail_xt, TN)
    y = y + blk.skip * blk.x
    y_ref[...] = y
    gated = y * silu(z)
    part_ref[:, :depth] = mm((gated * blk.gain).astype(B16), out_w_ref[...]).astype(B16)
    high, rest = hi_lo(jnp.sum(gated * gated, axis=1, keepdims=True))
    lane = lax.broadcasted_iota(jnp.int32, (n, LANES), 1)
    part_ref[:, depth:] = jnp.where(lane == 0, high.astype(F32), jnp.where(lane == 1, rest.astype(F32), 0.0)).astype(B16)


def whole(shape):
    return pl.BlockSpec(shape, lambda i: (0,) * len(shape))


def params():
    return pltpu.CompilerParams(dimension_semantics=("arbitrary",), vmem_limit_bytes=60 * 1024 * 1024)


def mixer_forward(ends, gathered, in_w, taps, rows, out_w, state, C):
    T, depth = gathered.shape[0], in_w.shape[0]
    cp, nb = out_w.shape[0], gathered.shape[0] // BLOCK
    conv_width = cp + 2 * state

    def block(width):
        return pl.BlockSpec((BLOCK, width), lambda i: (i, 0))

    return pl.pallas_call(
        functools.partial(mixer_forward_kernel, ends.shape[0], state, C),
        grid=(nb,),
        in_specs=[
            pl.BlockSpec(memory_space=pltpu.SMEM), block(gathered.shape[1]), whole(in_w.shape), whole(taps.shape),
            whole(rows.shape), whole(out_w.shape),
        ],
        out_specs=[
            block(conv_width), block(cp), block(cp),
            pl.BlockSpec((1, state, cp), lambda i: (i, 0, 0)), block(depth + LANES),
        ],
        out_shape=[
            jax.ShapeDtypeStruct((T, conv_width), F32),
            jax.ShapeDtypeStruct((T, cp), F32),
            jax.ShapeDtypeStruct((T, cp), F32),
            jax.ShapeDtypeStruct((nb, state, cp), F32),
            jax.ShapeDtypeStruct((T, depth + LANES), B16),
        ],
        scratch_shapes=[pltpu.VMEM((state, cp), F32), pltpu.VMEM((BLOCK + 8, conv_width), F32)],
        compiler_params=params(),
    )(ends, gathered, in_w, taps, rows, out_w)


def mixer_backward_kernel(
    count, state, C, ends_ref, three_ref, one_ref, pre_ref, halo_ref, z_ref, y_ref, st_ref,
    w_ref, taps_ref, rows_ref, cols_ref, out_w_ref,
    part_ref, gzx_ref, gbc_ref, gout_ref, gtaps_ref, gvec_ref, held, ext, gext, gw_ref,
):
    step = pl.program_id(0)
    i = pl.num_programs(0) - 1 - step
    depth = w_ref.shape[0]
    n, cp = BLOCK, z_ref.shape[1]

    @pl.when(step == 0)
    def _():
        held[...] = jnp.zeros_like(held)
        gext[n : n + 8, :] = jnp.zeros((8, gext.shape[1]), F32)
        gw_ref[...] = jnp.zeros_like(gw_ref)
        gout_ref[...] = jnp.zeros_like(gout_ref)
        gtaps_ref[...] = jnp.zeros_like(gtaps_ref)
        gvec_ref[...] = jnp.zeros_like(gvec_ref)

    pre, z, y = pre_ref[...], z_ref[...], y_ref[...]
    ext[0:8, :] = jnp.where(i == 0, 0.0, halo_ref[...])
    ext[8 : 8 + n, :] = pre
    blk = Block(i, pre, ext, z, taps_ref, rows_ref, ends_ref, count, state, C)
    three = three_ref[:, :depth]
    pg = mm(three, out_w_ref[...], NT)
    cross = jnp.sum(three_ref[:, depth:].astype(F32), axis=1, keepdims=True)
    act_z = silu(z)
    gated = y * act_z
    gout_ref[...] += mm((gated * blk.gain).astype(B16), three, TN)
    grad_gated = pg * blk.gain - gated * cross
    gy = grad_gated * act_z
    gz = grad_gated * y * silu_grad(z)
    st = st_ref[0]
    st_low, grad = st.astype(B16), held[...]
    grad_low = grad.astype(B16)
    gy_low = gy.astype(B16)
    y_all = blk.inner() + blk.carry * mm(blk.c, st_low)
    back = sum(mm(blk.mats[j], gy_low * blk.low[j], TN) for j in range(2))
    gate = (blk.carry * gy_low.astype(F32)).astype(B16)
    tail_back = blk.tail * mm(blk.b, grad_low)
    pull = sum(mm(gy_low, blk.xts[j], NT) * blk.decays[j] for j in range(2)).astype(B16)
    g_c = mm(pull, blk.b) + mm(gate, st_low, NT)
    g_b = mm(pull, blk.c, TN) + mm(blk.tail_xt, grad_low, NT)
    held[...] = blk.keep * grad + mm(blk.c, gate, TN)
    g_xt = back + tail_back
    xt = blk.xt.astype(F32)
    cols = cols_ref[...]
    after = exact(gy_low.astype(F32) * y_all - xt * back, cols)
    used = exact(xt * tail_back, cols)
    through = exact(jnp.broadcast_to(blk.keep * jnp.sum(grad * st, axis=0, keepdims=True), (8, cp)), cols)[0:1, :]
    g_rate = (
        exact((blk.row <= blk.col).astype(F32), after) + exact((blk.row > blk.col).astype(F32), used) + through
    )
    g_dt = exact(g_xt * blk.x, cols) - g_rate * blk.decay
    g_dtr = g_dt / (1.0 + jnp.exp(-blk.dtr))
    g_x = g_xt * blk.dtc + blk.skip * gy
    for r, v in enumerate((pg * gated, g_dtr, g_rate * blk.rate, gy * blk.x)):
        gvec_ref[r : r + 1, :] += jnp.sum(v, axis=0, keepdims=True)
    gconv = jnp.concatenate([g_x, g_b, g_c], axis=1) * silu_grad(blk.conv)
    gext[0:n, :] = gconv
    gpre = taps_ref[3:4, :] * gconv
    gtaps_ref[3:4, :] += jnp.sum(gconv * pre, axis=0, keepdims=True)
    for k in (1, 2, 3):
        gpre = gpre + taps_ref[3 - k : 4 - k, :] * gext[k : n + k, :] * blk.later[k]
        gtaps_ref[3 - k : 4 - k, :] += jnp.sum(gconv * ext[8 - k : 8 - k + n, :] * blk.joined[k], axis=0, keepdims=True)
    gext[n : n + 8, :] = gconv[0:8, :]
    made = jnp.concatenate([gz + g_dtr, gpre], axis=1).astype(B16)
    part_ref[...] = mm(made, w_ref[...], NT).astype(B16)
    gw_ref[...] += mm(one_ref[:, :depth], made, TN)

    @pl.when(i == 0)
    def _():
        gzx_ref[...] = gw_ref[:, : 2 * cp].astype(B16)
        gbc_ref[...] = gw_ref[:, 2 * cp :].astype(B16)


def mixer_backward(ends, three, one, pre, z, y, states, in_w, taps, rows, cols, out_w, state, C):
    T, depth = three.shape[0], in_w.shape[0]
    cp, nb = out_w.shape[0], T // BLOCK
    conv_width = cp + 2 * state

    def block(width):
        return pl.BlockSpec((BLOCK, width), lambda k: (nb - 1 - k, 0))

    def halo(k):
        return (jnp.maximum((nb - 1 - k) * (BLOCK // 8) - 1, 0), 0)

    return pl.pallas_call(
        functools.partial(mixer_backward_kernel, ends.shape[0], state, C),
        grid=(nb,),
        in_specs=[
            pl.BlockSpec(memory_space=pltpu.SMEM), block(three.shape[1]), block(one.shape[1]), block(conv_width),
            pl.BlockSpec((8, conv_width), halo), block(cp), block(cp),
            pl.BlockSpec((1, state, cp), lambda k: (nb - 1 - k, 0, 0)),
            whole(in_w.shape), whole(taps.shape), whole(rows.shape), whole(cols.shape), whole(out_w.shape),
        ],
        out_specs=[
            block(depth), whole((depth, 2 * cp)), whole((depth, 2 * state)), whole(out_w.shape), whole((8, conv_width)),
            whole((8, cp)),
        ],
        out_shape=[
            jax.ShapeDtypeStruct((T, depth), B16),
            jax.ShapeDtypeStruct((depth, 2 * cp), B16),
            jax.ShapeDtypeStruct((depth, 2 * state), B16),
            jax.ShapeDtypeStruct(out_w.shape, F32),
            jax.ShapeDtypeStruct((8, conv_width), F32),
            jax.ShapeDtypeStruct((8, cp), F32),
        ],
        scratch_shapes=[
            pltpu.VMEM((state, cp), F32),
            pltpu.VMEM((BLOCK + 8, conv_width), F32),
            pltpu.VMEM((BLOCK + 8, conv_width), F32),
            pltpu.VMEM(in_w.shape, F32),
        ],
        compiler_params=params(),
    )(ends, three, one, pre, pre, z, y, states, in_w, taps, rows, cols, out_w)


def expert_kernel(
    F, two_ref, grad_ref, named_ref, up_ref, down_ref, mine_ref,
    out_ref, part_ref, probs_ref, gup_ref, gdown_ref,
):
    depth = two_ref.shape[1]

    @pl.when(pl.program_id(0) == 0)
    def _():
        gup_ref[...] = jnp.zeros_like(gup_ref)
        gdown_ref[...] = jnp.zeros_like(gdown_ref)

    two, grad = two_ref[...], grad_ref[...]
    mid = mm(two, up_ref[...])
    back = mm(grad, down_ref[...], NT)
    gate, lin = mid[:, :F], mid[:, F : 2 * F]
    s_gate, s_lin = mid[:, 2 * F : 2 * F + LANES], mid[:, 2 * F + LANES :]
    named = named_ref[...].astype(F32) > 0
    logits = jnp.where(named, s_gate, -1e30)
    odds = jnp.where(named, jnp.exp(logits - jnp.max(logits, axis=1, keepdims=True)), 0.0)
    probs = odds / jnp.sum(odds, axis=1, keepdims=True)
    probs_ref[...] = probs
    mine = mine_ref[...]
    weight = jnp.sum(probs * mine, axis=1, keepdims=True)
    s_back, back = back[:, F:], back[:, :F]
    act_gate, act_s = silu(gate), silu(s_gate)
    acting = act_gate * lin
    gp = jnp.sum(acting * back, axis=1, keepdims=True)
    back = weight * back
    down_in = jnp.concatenate([weight * acting, act_s * s_lin], axis=1).astype(B16)
    mid_grad = jnp.concatenate(
        [back * lin * silu_grad(gate), back * act_gate, s_back * s_lin * silu_grad(s_gate), s_back * act_s], axis=1
    ).astype(B16)
    out_ref[...] = mm(down_in, down_ref[...]).astype(B16)
    part_ref[:, :depth] = mm(mid_grad, up_ref[...], NT).astype(B16)
    part_ref[:, depth:] = (gp * mine).astype(B16)
    gup_ref[...] += mm(two, mid_grad, TN)
    gdown_ref[...] += mm(down_in, grad, TN)


def experts(two, all_grad, gathered, up_w, down_w, mine, F):
    T, depth = two.shape

    def block(width):
        return pl.BlockSpec((BLOCK, width), lambda i: (i, 0))

    return pl.pallas_call(
        functools.partial(expert_kernel, F),
        grid=(T // BLOCK,),
        in_specs=[
            block(depth), block(depth), pl.BlockSpec((BLOCK, LANES), lambda i: (i, depth // LANES)),
            whole(up_w.shape), whole(down_w.shape), whole(mine.shape),
        ],
        out_specs=[block(depth), block(depth + LANES), block(LANES), whole(up_w.shape), whole(down_w.shape)],
        out_shape=[
            jax.ShapeDtypeStruct((T, depth), B16),
            jax.ShapeDtypeStruct((T, depth + LANES), B16),
            jax.ShapeDtypeStruct((T, LANES), F32),
            jax.ShapeDtypeStruct(up_w.shape, F32),
            jax.ShapeDtypeStruct(down_w.shape, F32),
        ],
        compiler_params=params(),
    )(two, all_grad, gathered, up_w, down_w, mine)


def local(
    hidden_in, norm1_gain, w_zx, w_bc, w_dt, conv_x, conv_bc, dt_bias, a_log, d_skip, gate_gain,
    w_out, norm2_gain, router, expert_up, expert_down, shared_up, shared_down, out_grad,
    seq_lengths, routes,
):
    S, H = lax.axis_size("seq"), lax.axis_size("head")
    N = S * H
    s = lax.axis_index("seq")
    g = s * H + lax.axis_index("head")
    R, D = hidden_in.shape
    heads, inner = dt_bias.shape[0], conv_x.shape[1]
    size = inner // heads
    state = w_bc.shape[1] // 2
    width = inner * H
    C = inner // S
    CP = -(-(C + 2) // LANES) * LANES
    E = N // 2
    F = expert_down.shape[1]
    FS = shared_down.shape[0] // N
    per = D // N

    all_grad = lax.all_gather(out_grad.astype(B16), ("seq", "head"), axis=0, tiled=True)
    named = jnp.sum(
        (routes[:, :, None] == jnp.arange(E, dtype=jnp.int32)[None, None, :]).astype(F32), axis=1
    )
    named = jnp.pad(named.astype(B16), ((0, 0), (FS, LANES - FS - E)))
    gain1, gain2 = norm1_gain[None], norm2_gain[None]
    gathered = first_rows(hidden_in, gain1, named, S, H)

    firsts = [min(k * C // size, heads - 2) for k in range(S)]
    first = jnp.minimum(s * C // size, heads - 2)
    channel = jnp.arange(CP)
    masks = jnp.stack(
        [((channel < C) & ((s * C + channel) // size - first == j)).astype(F32) for j in range(2)]
    )

    def mine(values, axis, offset, length):
        return lax.dynamic_slice_in_dim(values, offset, length, axis)

    def channels(values, axis):
        cut = mine(values, axis, s * C, C)
        pads = [(0, 0)] * values.ndim
        pads[axis] = (0, CP - C)
        return jnp.pad(cut, pads)

    def in_free(values):
        return jnp.pad(values, [(0, 0)] * (values.ndim - 1) + [(C, CP - C - 2)])

    in_w = jnp.concatenate(
        [
            mine(w_zx[:, 0], 1, s * C, C), pad_lanes(mine(w_dt, 1, first, 2), CP - C),
            channels(w_zx[:, 1], 1), w_bc,
        ],
        axis=1,
    )
    taps = jnp.concatenate([channels(conv_x, 1), conv_bc], axis=1)
    bias, alog, skip = (mine(v, 0, first, 2) for v in (dt_bias, a_log, d_skip))
    gain = channels(gate_gain, 0)
    out_w = channels(w_out, 0)
    rows = jnp.concatenate(
        [masks, (skip @ masks)[None], gain[None], in_free(jnp.stack([bias, jnp.exp(alog)]))], axis=0
    )
    rows = jnp.pad(rows, ((0, 2), (0, 0)))
    cols = in_free(masks.T)
    ends = jnp.cumsum(seq_lengths)

    pre, z, y, states, part = mixer_forward(ends, gathered, in_w, taps, rows, out_w, state, C)
    two, residual, mixed, inv_gate = second_rows(part, hidden_in, gain2, width, S, H)

    sup = mine(shared_up, 2, g * FS, FS)
    router_w = jnp.pad(router, ((0, 0), (FS, LANES - FS - E)))
    up_w = jnp.concatenate(
        [
            expert_up[0].reshape(D, 2 * F), sup[:, 0], router_w[:, FS:], pad_lanes(sup[:, 1], LANES),
        ],
        axis=1,
    )
    down_w = jnp.concatenate([expert_down[0], mine(shared_down, 0, g * FS, FS), jnp.zeros((LANES - FS, D), B16)], axis=0)
    is_mine = (jnp.arange(LANES) == FS + g // 2).astype(F32)[None]
    out_part, two_part, probs, grad_up_all, grad_down_all = experts(
        two, all_grad, gathered, up_w, down_w, is_mine, F
    )
    out_sum = lax.psum_scatter(out_part, ("seq", "head"), scatter_dimension=0, tiled=True)
    three, grad_res, norm2_part, router_part = third_rows(
        two_part, probs, residual, mixed, inv_gate, out_grad, gain2, router_w, width, S, H
    )
    grad_up = grad_up_all[:, : 2 * F].reshape(expert_up.shape)
    grad_down = grad_down_all[:F].reshape(expert_down.shape)

    one_part, grad_zx_w, grad_bc_w, grad_out_w, tap_part, vec_part = mixer_backward(
        ends, three, gathered, pre, z, y, states, in_w, taps, rows, cols, out_w, state, C
    )
    pieces = (
        norm2_part, tap_part[:4, CP:], tap_part[:4, :C], vec_part[0, :C], vec_part[1, C : C + 2],
        vec_part[2, C : C + 2], masks @ vec_part[3],
    )
    flat = jnp.concatenate([v.reshape(-1) for v in pieces])
    room = -(-flat.shape[0] // (8 * LANES)) * (8 * LANES)
    flat = jnp.pad(flat, (0, room - flat.shape[0])).reshape(8, room // 8)
    tall = -(-per // 16) * 16
    extra = jnp.concatenate([grad_bc_w, router_part], axis=1).reshape(N, per, 2 * state + LANES)
    extra = jnp.pad(extra, ((0, 0), (0, tall - per), (0, 0))).reshape(N * tall, 2 * state + LANES)
    s_up = jnp.concatenate([grad_up_all[:, 2 * F : 2 * F + FS], grad_up_all[:, 2 * F + LANES :][:, :FS]], axis=1)
    s_down = grad_down_all[F : F + FS].reshape(FS, N, per).transpose(1, 0, 2)
    grad_in, extra_sum, norm1_sum, zx_in, wo_in, su_in, sd_in, small = last_rows(
        one_part,
        extra,
        grad_zx_w.reshape(S, D // S, 2 * CP),
        grad_out_w[:C].reshape(C, S, D // S).transpose(1, 0, 2).astype(B16),
        s_up.astype(B16).reshape(N, per, 2 * FS),
        s_down.astype(B16),
        flat, hidden_in, grad_res, gain1, S, H,
    )
    output = residual + out_sum.astype(F32)
    grad_norm1 = norm1_sum.reshape(-1)[:D]
    grad_bc, grad_router = extra_sum[:per, : 2 * state], extra_sum[:per, 2 * state :][:, FS : FS + E]
    zx_in = zx_in.astype(F32)
    grad_zx = jnp.stack([zx_in[:, :, :C], zx_in[:, :, CP : CP + C]], axis=2)
    grad_zx = grad_zx.transpose(1, 2, 0, 3).reshape(D // S, 2, inner)
    grad_w_dt = sum(
        jnp.pad(zx_in[k, :, C : C + 2], ((0, 0), (firsts[k], heads - 2 - firsts[k]))) for k in range(S)
    )
    grad_w_out = wo_in.reshape(inner, D // S).astype(F32)
    grad_shared_up = su_in.reshape(N, per, 2, FS).transpose(1, 2, 0, 3).reshape(per, 2, N * FS).astype(F32)
    grad_shared_down = sd_in.reshape(N * FS, per).astype(F32)

    small = small.reshape(N, room)
    at, found = 0, []
    for v in pieces:
        found.append(small[:, at : at + v.size].reshape((S, H) + v.shape))
        at += v.size
    grad_norm2, grad_conv_bc = found[0].sum((0, 1)).reshape(D), found[1].sum((0, 1))
    grad_conv_x = found[2].transpose(2, 1, 0, 3).reshape(4, width)
    grad_gate_gain = found[3].transpose(1, 0, 2).reshape(width)

    def by_head(v):
        return sum(
            jnp.pad(v[k], ((0, 0), (firsts[k], heads - 2 - firsts[k]))) for k in range(S)
        ).reshape(-1)

    grad_dt_bias, grad_a_log, grad_d_skip = (by_head(v) for v in found[4:])
    return (
        output, grad_in, grad_norm1, grad_zx, grad_bc, grad_w_dt, grad_conv_x, grad_conv_bc, grad_dt_bias,
        grad_a_log, grad_d_skip, grad_gate_gain, grad_w_out, grad_norm2, grad_router, grad_up, grad_down,
        grad_shared_up, grad_shared_down,
    )


def solution(mesh):
    return jax.shard_map(
        local,
        mesh=mesh,
        in_specs=(
            P(("seq", "head"), None),
            P(),
            P(None, None, "head"),
            P(),
            P(None, "head"),
            P(None, "head"),
            P(),
            P("head"),
            P("head"),
            P("head"),
            P("head"),
            P("head", None),
            P(),
            P(),
            P(("seq", "head"), None, None, None),
            P(("seq", "head"), None, None),
            P(),
            P(),
            P(("seq", "head"), None),
            P(),
            P(("seq", "head"), None),
        ),
        out_specs=(
            P(("seq", "head"), None),
            P(("seq", "head"), None),
            P(),
            P("seq", None, "head"),
            P(("seq", "head"), None),
            P("seq", "head"),
            P(),
            P(),
            P(),
            P(),
            P(),
            P(),
            P("head", "seq"),
            P(),
            P(("seq", "head"), None),
            P(("seq", "head"), None, None, None),
            P(("seq", "head"), None, None),
            P(("seq", "head"), None, None),
            P(None, ("seq", "head")),
        ),
        check_vma=False,
    )
```

time: 2120 us -> 592 us (0.28)
  waiting for transfers between devices: 1320 us -> 0.04 us
  Pallas kernels: 0 us -> 460 us
  local copies, waits for them, and re-layouts: 319 us -> 90.6 us
  blocking collectives: 160 us -> 0 us
  matrix products: 141 us -> 1.51 us
  other arithmetic: 125 us -> 23.8 us
    pallas_call x0 -> x7, Pallas kernels: none -> 460 us  [the longest x1 120 us: last_rows(): pl.pallas_call(functools.partial(last_kernel, S, H), out_shape=[jax.Shape...]
    unnamed x16 -> x2, waiting for transfers between devices: 436 us -> 0.03 us
    reduce_scatter x5 -> x1, waiting for transfers between devices: 304 us -> 0.01 us  [local(): lax.psum_scatter(out_part, ('seq', 'head'), scatter_dimension=0, tiled=True)]
    all_to_all x3 -> x0, waiting for transfers between devices: 288 us -> none  [route_rows(): lax.all_to_all(slot_rows, ('seq', 'head'), split_axis=0, concat_axis=0, t...]
    psum x1 -> x0, waiting for transfers between devices: 265 us -> none  [local(): lax.psum((grad_norm1, grad_norm2, widen(grad_conv[:, :inner_local], 1), g...]
    dot_general x44 -> x2, matrix products: 139 us -> 1.51 us  [the longest x1 0.81 us: local(): masks @ vec_part[3]]
    scatter x2 -> x0, local copies, waits for them, and re-layouts: 124 us -> none  [the longest x1 62.2 us: local(): grad_send = jnp.zeros((expert_count, capacity, model_width), jnp.bfloat16...]
    all_to_all x1 -> x0, blocking collectives: 109 us -> none  [route_rows(): lax.all_to_all(slot_rows, ('seq', 'head'), split_axis=0, concat_axis=0, t...]
  transfers between devices with their start and end apart: 17 -> 2, of which waited for: 14 -> 0; matrix products, arithmetic and copies ran while one was open for 14% -> 18% of each run, Pallas kernels for 0% -> 72%
where the time goes in v1:
time: 592 us; the launch traced here: 590 us
  Pallas kernels  460 us (78%)
  local copies, waits for them, and re-layouts  90.6 us (15%)
  other arithmetic  23.8 us (4%)
  between operations  14.5 us (2%)
    pallas_call x1, Pallas kernels, last_rows(): pl.pallas_call(functools.partial(last_kernel, S, H), out_shape=[jax.Shape...  120 us
    pallas_call x1, Pallas kernels, third_rows(): pl.pallas_call(functools.partial(third_kernel, S, H, width), out_shape=[j...  96.9 us
    pallas_call x1, Pallas kernels, second_rows(): pl.pallas_call(functools.partial(second_kernel, S, H, width), out_shape=[...  85.7 us
    pallas_call x1, Pallas kernels, first_rows(): pl.pallas_call(functools.partial(first_kernel, S, H), out_shape=jax.Shape...  59.5 us
    pallas_call x1, Pallas kernels, mixer_backward(): pl.pallas_call(functools.partial(mixer_backward_kernel, ends.shape[0], st...  39.9 us
    pallas_call x1, Pallas kernels, experts(): pl.pallas_call(functools.partial(expert_kernel, F), grid=(T // BLOCK,), i...  35 us
    unnamed x61, local copies, waits for them, and re-layouts  29.8 us
    pallas_call x1, Pallas kernels, mixer_forward(): pl.pallas_call(functools.partial(mixer_forward_kernel, ends.shape[0], sta...  22.7 us
  transfers between devices with their start and end apart: 2, of which 0 were waited for; matrix products, arithmetic and copies ran while one was open for 18% of the time, Pallas kernels for 72%

profile of v1, /device:TPU:0, one launch (start us, length us, event | category | flops | bytes accessed | tf_op | source)
XLA Modules:
  0.0 590.1 jit_solution(11928209135107300874)
XLA Ops:
  7.3 1.8 convert_element_type.157
  9.2 0.8 constant_dynamic-slice_fusion.6
  10.0 1.0 copy.169
  11.0 9.8 %fusion.11 = (bf16[1536,1,768]{2,1,0:T(2,128)(2,1)S(1)}, bf16[1536,1,768]{2,1,0:T(2,128)(2,1)S(1)}) fusion(bf16[1536,2,768]{2,1,0:T(2,128)(2,1)} %param.23), kind=kLoop, calls=%fused_computation.82 | loop fusion | bytes 9437184 | tf_op jit(solution)/shard_map/slice | solution.py:950
  20.8 2.4 constant_dynamic-slice_fusion.5
  23.2 0.8 copy.186
  24.0 0.8 copy.187
  24.8 0.8 dynamic_slice.44
  26.3 1.0 constant_dynamic-slice_fusion.3
  27.3 0.8 pad.167.out_w_ref
  30.0 1.0 copy.148
  31.1 2.9 copy.177
  35.2 0.7 exponential_bitcast_fusion
  37.4 59.5 %shard_map.348.in_ref.named_ref.one_ref = bf16[2048,1664]{1,0:T(8,128)(2,1)} custom-call(f32[64,1536]{1,0:T(8,128)} %in_ref.5, f32[1,1536]{1,0:T(1,128)} %broadcast_in_dim.18.gain_ref, bf16[64,128]{1,0:T(8,128)(2,1)} %pad.160.named_ref), custom_call_target="tpu_custom_call" | custom-call | tf_op jit(solution)/shard_map/pallas_call | solution.py:327
  96.9 0.8 constant_dynamic-slice_fusion.4
  98.3 1.5 fusion.7.w_ref
  99.7 22.7 %shard_map.349 = (f32[2048,384]{1,0:T(8,128)}, f32[2048,128]{1,0:T(8,128)}, f32[2048,128]{1,0:T(8,128)}, f32[8,128,128]{2,1,0:T(8,128)}, bf16[2048,1664]{1,0:T(8,128)(2,1)}) custom-call(s32[4]{0:T(128)} %bitcast.132, bf16[2048,1664]{1,0:T(8,128)(2,1)} %shard_map.348.in_ref.named_ref.one_ref, bf16[1536,512]{1,0:T(8,128)(2,1)} %fusion.7.w_ref, ...), custom_call_target="tpu_custom_call" | custom-call | tf_op jit(solution)/shard_map/pallas_call | solution.py:695
  122.5 85.7 %shard_map.350 = (bf16[2048,1536]{1,0:T(8,128)(2,1)}, f32[64,1536]{1,0:T(8,128)}, f32[64,1536]{1,0:T(8,128)}, f32[64,128]{1,0:T(8,128)}) custom-call(bf16[4,2,2,2,64,1664]{5,4,3,2,1,0:T(8,128)(2,1)} %bitcast.107, f32[64,1536]{1,0:T(8,128)} %in_ref.5, f32[1,1536]{1,0:T(1,128)} %broadcast_in_dim.21.gain_ref), custom_call_target="tpu_custom_call" | custom-call | tf_op jit(solution)/shard_map/pallas_call | solution.py:366
  208.7 3.4 constant_dynamic-slice_fusion
  212.4 1.2 copy-done.3
  213.6 2.1 fusion.5.up_ref
  215.7 1.2 maximum_maximum_fusion.down_ref
  216.9 35.0 %shard_map.351 = (bf16[2048,1536]{1,0:T(8,128)(2,1)}, bf16[2048,1664]{1,0:T(8,128)(2,1)}, f32[2048,128]{1,0:T(8,128)}, f32[1536,768]{1,0:T(8,128)}, f32[384,1536]{1,0:T(8,128)}) custom-call(bf16[2048,1536]{1,0:T(8,128)(2,1)} %get-tuple-element.53.two_ref, bf16[2048,1536]{1,0:T(8,128)(2,1)} %all-gather.2.cloned.1.call-done.grad_ref, ...), custom_call_target="tpu_custom_call" | custom-call | tf_op jit(solution)/shard_map/pallas_call | solution.py:881
  251.9 0.9 pad.168.router_ref
  253.7 96.9 %shard_map.352 = (bf16[2048,1664]{1,0:T(8,128)(2,1)}, f32[64,1536]{1,0:T(8,128)}, f32[1,1536]{1,0:T(1,128)}, bf16[1536,128]{1,0:T(8,128)(2,1)}) custom-call(bf16[4,2,2,2,64,1664]{5,4,3,2,1,0:T(8,128)(2,1)} %bitcast.106, f32[2048,128]{1,0:T(8,128)} %get-tuple-element.56.probs_ref, f32[64,1536]{1,0:T(8,128)} %get-tuple-element.52.res_ref, ...), custom_call_target="tpu_custom_call" | custom-call | tf_op jit(solution)/shard_map/pallas_call | solution.py:423
  350.6 39.9 %shard_map.353 = (bf16[2048,1536]{1,0:T(8,128)(2,1)}, bf16[1536,256]{1,0:T(8,128)(2,1)}, bf16[1536,256]{1,0:T(8,128)(2,1)}, f32[128,1536]{1,0:T(8,128)}, f32[8,384]{1,0:T(8,128)}, /*index=5*/f32[8,128]{1,0:T(8,128)}) custom-call(s32[4]{0:T(128)} %bitcast.133, bf16[2048,1664]{1,0:T(8,128)(2,1)} %get-tuple-element.59.three_ref, ...), custom_call_target="tpu_custom_call" | custom-call | tf_op jit(solution)/shard_map/pallas_call | solution.py:805
  392.0 0.8 convolution_bitcast_fusion
  393.5 0.8 slice_bitcast_fusion.15
  395.0 2.6 convert.20
  397.6 1.1 slice.360
  399.0 0.8 copy.188
  399.9 0.9 slice.361
  401.1 0.8 copy.189
  401.9 1.0 pad_maximum_fusion.1.su_ref
  402.9 1.1 pad_maximum_fusion
  404.0 119.9 %shard_map.354 = (f32[64,1536]{1,0:T(8,128)}, f32[48,384]{1,0:T(8,128)}, f32[16,128]{1,0:T(8,128)}, bf16[8,192,256]{2,1,0:T(8,128)(2,1)}, bf16[8,96,192]{2,1,0:T...) custom-call(bf16[4,2,2,2,64,1536]{5,4,3,2,1,0:T(8,128)(2,1)} %bitcast.109, ...), custom_call_target="tpu_custom_call" | custom-call | tf_op jit(solution)/shard_map/pallas_call | solution.py:554
  524.0 1.1 copy.179
  526.3 1.4 slice.255
  527.7 1.4 slice.292
  530.9 1.3 reshape.312
  532.2 1.4 pad_add_fusion.2
  533.6 1.3 reshape.311
  535.7 1.3 convert_element_type.164
  536.9 1.1 copy-done.2
  538.3 0.9 pad_add_fusion
  539.2 1.6 copy.158
  540.8 1.5 slice_bitcast_fusion.2
  542.5 2.1 copy.163
  544.5 3.3 reshape.325
  547.8 2.2 copy.155
  550.0 3.5 copy.164
  553.5 3.0 reshape.326
  556.5 1.9 bitcast_convert_fusion
  558.4 2.2 copy.159
  560.6 1.8 bitcast_convert_fusion.1
  562.4 1.9 copy.162
  564.3 1.5 reshape.308
  565.8 1.5 copy.153
  567.3 1.6 reshape.309
  570.9 1.4 copy.160
  572.3 3.3 reshape.315
  576.8 3.0 slice_bitcast_fusion
  579.7 1.7 convert_add_fusion
  581.4 1.8 copy.191
  (101 shorter events, 18.7 us)
Async XLA Ops:
  7.2 204.9 %copy-start = (bf16[1024,1536]{1,0:T(8,128)(2,1)S(1)}, bf16[1024,1536]{1,0:T(8,128)(2,1)}, u32[]{:S(2)}) copy-start(bf16[1024,1536]{1,0:T(8,128)(2,1)} %param.38) | copy-start | bytes 9437188
  7.2 209.7 %all-gather.2.cloned.1.call-start = ((), (), s32[]{:S(2)}) async-start(), calls=%async_computation.1 | async-start | bytes 6488064 | tf_op jit(solution)/shard_map/all_gather | solution.py:921
  9.1 570.6 %reduce-scatter.2.cloned.1.call-start = ((), (), s32[]{:S(2)}) async-start(), calls=%async_computation.2 | async-start | bytes 6488064 | tf_op jit(solution)/shard_map/reduce_scatter | solution.py:982
  20.8 4.8 copy-start.12
  20.8 5.4 copy-start.17
  23.2 5.6 copy-start.19
  23.2 6.3 %copy-start.13 = (f32[1536]{0:T(1024)S(1)}, f32[1536]{0:T(1024)}, u32[]{:S(2)}) copy-start(f32[1536]{0:T(1024)} %param.33) | copy-start | bytes 18436
  26.3 8.2 %copy-start.20 = (f32[12]{0:T(128)S(1)}, f32[12]{0:T(128)}, u32[]{:S(2)}) copy-start(f32[12]{0:T(128)} %param.30) | copy-start | bytes 148
  26.3 9.0 %copy-start.18 = (f32[12]{0:T(128)S(1)}, f32[12]{0:T(128)}, u32[]{:S(2)}) copy-start(f32[12]{0:T(128)} %param.29) | copy-start | bytes 148
  37.3 60.3 %copy-start.16 = (f32[4,256]{1,0:T(4,128)S(1)}, f32[4,256]{1,0:T(4,128)}, u32[]{:S(2)}) copy-start(f32[4,256]{1,0:T(4,128)} %param.27) | copy-start | bytes 12292
  37.3 60.9 %copy-start.5 = (bf16[1536,2]{1,0:T(8,128)(2,1)S(1)}, bf16[1536,2]{1,0:T(8,128)(2,1)}, u32[]{:S(2)}) copy-start(bf16[1536,2]{1,0:T(8,128)(2,1)} %copy.169) | copy-start | bytes 18436
  37.3 60.9 %copy-start.6 = (bf16[1536,1,96]{2,0,1:T(8,128)(2,1)S(1)}, bf16[1536,1,96]{2,0,1:T(8,128)(2,1)}, u32[]{:S(2)}) copy-start(bf16[1536,1,96]{2,0,1:T(8,128)(2,1)} %copy.186) | copy-start | bytes 884740
  37.3 60.9 %copy-start.7 = (bf16[1536,1,96]{2,0,1:T(8,128)(2,1)S(1)}, bf16[1536,1,96]{2,0,1:T(8,128)(2,1)}, u32[]{:S(2)}) copy-start(bf16[1536,1,96]{2,0,1:T(8,128)(2,1)} %copy.187) | copy-start | bytes 884740
  37.4 60.9 %copy-start.8 = (bf16[1536,256]{1,0:T(8,128)(2,1)S(1)}, bf16[1536,256]{1,0:T(8,128)(2,1)}, u32[]{:S(2)}) copy-start(bf16[1536,256]{1,0:T(8,128)(2,1)} %param.24) | copy-start | bytes 2359300
  212.1 1.4 copy-start.3
  213.5 2.1 copy-start.9
  350.6 41.4 %copy-start.15 = (f32[1,1536]{1,0:T(1,128)S(1)}, f32[1,1536]{1,0:T(1,128)}, u32[]{:S(2)}) copy-start(f32[1,1536]{1,0:T(1,128)} %get-tuple-element.71) | copy-start | bytes 18436
  399.0 3.9 copy-start.11
  401.0 1.8 copy-start.10
  404.0 125.1 %slice-start = ((s8[4718592]{0:T(1024)(128)(4,1)}), s8[4194304]{0:T(1024)(128)(4,1)S(1)}, s32[]{:S(2)}) async-start(s8[4718592]{0:T(1024)(128)(4,1)} %bitcast.104), calls=%async_computation.3 | async-start | bytes 8388608
  404.0 125.1 %slice-start.1 = ((s8[4718592]{0:T(1024)(128)(4,1)}), s8[524288]{0:T(1024)(128)(4,1)S(1)}, s32[]{:S(2)}) async-start(s8[4718592]{0:T(1024)(128)(4,1)} %bitcast.104), calls=%async_computation.4 | async-start | bytes 1048576
  536.9 1.1 copy-start.2
  572.3 3.9 copy-start.14
  576.2 3.6 copy-start.4
  576.2 7.0 %copy-start.1 = (bf16[1024,1536]{1,0:T(8,128)(2,1)S(1)}, bf16[1024,1536]{1,0:T(8,128)(2,1)}, u32[]{:S(2)}) copy-start(bf16[1024,1536]{1,0:T(8,128)(2,1)} %param.38) | copy-start | bytes 9437188
Sparse Core Ops, SparseCore 0:
  11.5 90.6 all-gather.1
  252.0 141.2 reduce-scatter.1

commit v2 on v1

v2 whole, which is shorter than its diff:
```python
import functools
import jax
import jax.numpy as jnp
from jax import lax
from jax.experimental import pallas as pl
from jax.experimental.pallas import tpu as pltpu
from jax.sharding import PartitionSpec as P

MESH = pl.DeviceIdType.MESH
BLOCK = 256
EPS = 1e-05
LANES = 128
B16 = jnp.bfloat16
F32 = jnp.float32


def mm(left, right, dims=(((1,), (0,)), ((), ()))):
    return lax.dot_general(left, right, dims, preferred_element_type=F32)


NT = (((1,), (1,)), ((), ()))
TN = (((0,), (0,)), ((), ()))


def inverse_rms(values):
    return lax.rsqrt(jnp.mean(values * values, axis=-1, keepdims=True) + EPS)


def rms_back(values, inverse, gain, grad):
    weighted = grad * gain
    inner = jnp.mean(weighted * values, axis=-1, keepdims=True)
    return inverse * weighted - values * inverse**3 * inner


def silu_grad(values):
    sig = jax.nn.sigmoid(values)
    return sig * (1.0 + values * (1.0 - sig))


def pad_lanes(values, width):
    return jnp.pad(values, [(0, 0)] * (values.ndim - 1) + [(0, width - values.shape[-1])])


def hi_lo(values):
    high = values.astype(B16)
    return high, (values - high.astype(F32)).astype(B16)


def sizes(seq_size, head_size):
    return head_size // 2, head_size // 2, seq_size // (head_size // 2)


class Place:
    def __init__(self, seq_size, head_size):
        self.H = head_size
        self.X, self.Y, self.Z = sizes(seq_size, head_size)
        assert self.Z == 4
        seq, head = lax.axis_index("seq"), lax.axis_index("head")
        self.z, self.y = seq // self.Y, seq % self.Y
        self.x, self.c = head // 2, head % 2
        z = self.z
        self.partners = (z, z + 1 - 2 * (z % 2), (z + 2) % 4, 3 - z)

    def at(self, dz=0, dy=0, dx=0, dc=0):
        return (
            self.partners[dz],
            (self.y + dy) % self.Y if dy else self.y,
            (self.x + dx) % self.X if dx else self.x,
            1 - self.c if dc else self.c,
        )

    def dev(self, **where):
        z, y, x, c = self.at(**where)
        return (z * self.Y + y, x * 2 + c)

    def slot(self, **where):
        z, y, x, c = self.at(**where)
        return (z * self.Y + y) * self.H + x * 2 + c

    def peers(self):
        out = [self.dev(dz=1), self.dev(dz=2)]
        out += [self.dev(dy=k) for k in range(1, self.Y)]
        out += [self.dev(dx=k) for k in range(1, self.X)]
        return out + [self.dev(dc=1)]


def greet(peers):
    barrier = pltpu.get_barrier_semaphore()
    for peer in peers:
        pl.semaphore_signal(barrier, inc=1, device_id=peer, device_id_type=MESH)
    pl.semaphore_wait(barrier, len(peers))


class Mail:
    def __init__(self, send, recv):
        self.send, self.recv, self.made = send, recv, []

    def copy(self, src, dst, dev):
        i = len(self.made)
        self.made.append(
            pltpu.make_async_remote_copy(
                src_ref=src, dst_ref=dst, send_sem=self.send.at[i], recv_sem=self.recv.at[i],
                device_id=dev, device_id_type=MESH,
            )
        )
        return self.made[-1]

    def finish(self, count):
        assert len(self.made) == count
        for copy in self.made:
            copy.wait_send()


class Script(list):
    def stage(self):
        self.append([])

    def do(self, action):
        self[-1].append(action)

    def run(self, first=0, last=None):
        for stage in self[first:last]:
            for action in stage:
                action()


def gather_count(S, H):
    X, Y, Z = sizes(S, H)
    return (Z - 1) + 2 * Z * (X + Y - 2) + 2 * Z * (X - 1) * (Y - 1) + X * Y * Z


def gather(pc, mail, x_ref, out_ref, own_sem):
    X, Y, Z = pc.X, pc.Y, pc.Z
    R = x_ref.shape[0]
    half = R // 2
    script = Script()

    def rows(part, **where):
        base = pl.multiple_of(pc.slot(**where) * R, R)
        if part is None:
            return out_ref.at[pl.ds(base, R)]
        return out_ref.at[pl.ds(pl.multiple_of(base + part * half, half), half)]

    def send(src, dst, dev):
        copy = mail.copy(src, dst, dev)
        script.do(copy.start)
        return copy

    x_in, y_in, dga, dgb, sib = {}, {}, {}, {}, []

    def column(dz):
        for part in (0, 1):
            src = x_ref.at[pl.ds(part * half, half)] if dz == 0 else rows(part, dz=dz)
            for k in range(1, X):
                x_in[dz, k, part] = send(src, rows(part, dz=dz), pc.dev(dx=k))
            other = 1 - part
            src = x_ref.at[pl.ds(other * half, half)] if dz == 0 else rows(other, dz=dz)
            for k in range(1, Y):
                y_in[dz, k, other] = send(src, rows(other, dz=dz), pc.dev(dy=k))
        src = x_ref if dz == 0 else rows(None, dz=dz)
        sib.append(send(src, rows(None, dz=dz), pc.dev(dc=1)))

    def onward(dz):
        for k in range(1, X):
            script.do(x_in[dz, k, 0].wait_recv)
            block = rows(0, dz=dz, dx=-k)
            for m in range(1, Y):
                dga[dz, k, m] = send(block, block, pc.dev(dy=m))
        for k in range(1, Y):
            script.do(y_in[dz, k, 1].wait_recv)
            block = rows(1, dz=dz, dy=-k)
            for m in range(1, X):
                dgb[dz, k, m] = send(block, block, pc.dev(dx=m))
        for k in range(1, X):
            script.do(x_in[dz, k, 1].wait_recv)
            block = rows(None, dz=dz, dx=-k)
            sib.append(send(block, block, pc.dev(dc=1)))
        for k in range(1, Y):
            script.do(y_in[dz, k, 0].wait_recv)
            block = rows(None, dz=dz, dy=-k)
            sib.append(send(block, block, pc.dev(dc=1)))

    def corner(dz):
        for k in range(1, X):
            for m in range(1, Y):
                script.do(dga[dz, k, m].wait_recv)
                script.do(dgb[dz, m, k].wait_recv)
                block = rows(None, dz=dz, dx=-k, dy=-m)
                sib.append(send(block, block, pc.dev(dc=1)))

    own = pltpu.make_async_copy(x_ref, rows(None), own_sem)
    script.stage()
    script.do(own.start)
    first = send(x_ref, rows(None), pc.dev(dz=1))
    column(0)
    second = send(x_ref, rows(None), pc.dev(dz=2))
    script.stage()
    script.do(first.wait_recv)
    column(1)
    script.stage()
    onward(0)
    script.stage()
    script.do(second.wait_recv)
    third = send(rows(None, dz=2), rows(None, dz=2), pc.dev(dz=1))
    column(2)
    corner(0)
    script.stage()
    onward(1)
    script.stage()
    script.do(third.wait_recv)
    column(3)
    corner(1)
    script.stage()
    onward(2)
    corner(2)
    script.stage()
    onward(3)
    corner(3)
    for copy in sib:
        script.do(copy.wait_recv)
    script.do(own.wait)
    return script


def scatter_parts(split):
    return (("y", 0), ("x", 1)) if split else (("x", None),)


def scatter_count(S, H, splits=(True,)):
    X, Y, Z = sizes(S, H)
    pieces = sum(len(scatter_parts(split)) for split in splits)
    return len(splits) * (Z + Z - 1) + pieces * Z * (X + Y - 2)


def scatter_scratch(S, H, R, W, split=True):
    X, Y, Z = sizes(S, H)
    out = [pltpu.VMEM((Z, Y, X, R, W), B16), pltpu.VMEM((Z, Y, X, R, W), B16), pltpu.VMEM((Z - 1, R, W), B16)]
    for axis, part in scatter_parts(split):
        rows = R if part is None else R // 2
        first, second = (Y, X) if axis == "y" else (X, Y)
        out += [pltpu.VMEM((Z, first - 1, second, rows, W), B16), pltpu.VMEM((Z, second - 1, rows, W), B16)]
    return out + [pltpu.SemaphoreType.DMA((Z,))]


def accumulate(dst, srcs, rows):
    def action():
        def body(i, carry):
            at = pl.ds(pl.multiple_of(i * 16, 16), 16)
            total = dst.at[at][...].astype(F32)
            for src in srcs:
                total = total + src.at[at][...].astype(F32)
            dst.at[at][...] = total.astype(dst.dtype)
            return carry

        lax.fori_loop(0, rows // 16, body, 0)

    return action


ORDER = (3, 2, 1, 0)


def scatter(pc, mail, jobs):
    X, Y, Z = pc.X, pc.Y, pc.Z
    script = Script()
    own, sib, one, two, zs = {}, {}, {}, {}, {}

    def send(src, dst, dev):
        copy = mail.copy(src, dst, dev)
        script.do(copy.start)
        return copy

    def pieces(o):
        p_ref, total, scratch, split = jobs[o]
        R = p_ref.shape[4]
        for j, (axis, part) in enumerate(scatter_parts(split)):
            rows, size = (pl.ds(0, R), R) if part is None else (pl.ds(part * (R // 2), R // 2), R // 2)
            yield j, axis, rows, size, scratch[3 + 2 * j], scratch[4 + 2 * j]

    def cores(dz):
        for o, (p_ref, total, scratch, split) in enumerate(jobs):
            t0, r0 = scratch[0], scratch[1]
            script.do(own[o, dz].wait)
            script.do(sib[o, dz].wait_recv)
            for yy in range(Y):
                for xx in range(X):
                    script.do(accumulate(t0.at[dz, yy, xx], [r0.at[dz, yy, xx]], p_ref.shape[4]))
            for j, axis, rows, size, r1, r2 in pieces(o):
                for k in range(1, Y if axis == "y" else X):
                    if axis == "y":
                        src, dev = t0.at[dz, pc.at(dy=k)[1], :, rows], pc.dev(dy=k)
                    else:
                        src, dev = t0.at[dz, :, pc.at(dx=k)[2], rows], pc.dev(dx=k)
                    one[o, dz, j, k] = send(src, r1.at[dz, k - 1], dev)

    def firsts(dz):
        for o, (p_ref, total, scratch, split) in enumerate(jobs):
            t0 = scratch[0]
            for j, axis, rows, size, r1, r2 in pieces(o):
                steps = range(1, Y if axis == "y" else X)
                for k in steps:
                    script.do(one[o, dz, j, k].wait_recv)
                for m in range(X if axis == "y" else Y):
                    dst = t0.at[dz, pc.y, m, rows] if axis == "y" else t0.at[dz, m, pc.x, rows]
                    script.do(accumulate(dst, [r1.at[dz, k - 1, m] for k in steps], size))
                for k in range(1, X if axis == "y" else Y):
                    if axis == "y":
                        src, dev = t0.at[dz, pc.y, pc.at(dx=k)[2], rows], pc.dev(dx=k)
                    else:
                        src, dev = t0.at[dz, pc.at(dy=k)[1], pc.x, rows], pc.dev(dy=k)
                    two[o, dz, j, k] = send(src, r2.at[dz, k - 1], dev)

    def seconds(dz):
        for o, (p_ref, total, scratch, split) in enumerate(jobs):
            mine = scratch[0].at[dz, pc.y, pc.x]
            for j, axis, rows, size, r1, r2 in pieces(o):
                steps = range(1, X if axis == "y" else Y)
                for k in steps:
                    script.do(two[o, dz, j, k].wait_recv)
                script.do(accumulate(mine.at[rows], [r2.at[dz, k - 1] for k in steps], size))
            if dz == 2:
                script.do(zs[o, 3].wait_recv)
                script.do(accumulate(mine, [scratch[2].at[0]], p_ref.shape[4]))
            if dz:
                zs[o, dz] = send(mine, scratch[2].at[3 - dz], pc.dev(dz=2 if dz == 2 else 1))

    def last(p_ref, total, scratch):
        def body(i, carry):
            at = pl.ds(pl.multiple_of(i * 16, 16), 16)
            value = scratch[0].at[0, pc.y, pc.x, at][...].astype(F32)
            for k in (1, 2):
                value = value + scratch[2].at[k, at][...].astype(F32)
            total.at[at][...] = value
            return carry

        return lambda: lax.fori_loop(0, p_ref.shape[4] // 16, body, 0)

    script.stage()
    for o, (p_ref, total, scratch, split) in enumerate(jobs):
        for dz in ORDER:
            own[o, dz] = pltpu.make_async_copy(
                p_ref.at[pc.at(dz=dz)[0], :, :, pc.c], scratch[0].at[dz], scratch[-1].at[dz]
            )
            script.do(own[o, dz].start)
    script.stage()
    for dz in ORDER:
        for o, (p_ref, total, scratch, split) in enumerate(jobs):
            sib[o, dz] = send(p_ref.at[pc.at(dz=dz)[0], :, :, 1 - pc.c], scratch[1].at[dz], pc.dev(dc=1))
    script.stage()
    cores(3)
    cores(2)
    script.stage()
    cores(1)
    cores(0)
    script.stage()
    firsts(3)
    script.stage()
    firsts(2)
    seconds(3)
    script.stage()
    firsts(1)
    seconds(2)
    script.stage()
    firsts(0)
    seconds(1)
    script.stage()
    seconds(0)
    for o, (p_ref, total, scratch, split) in enumerate(jobs):
        for dz in (2, 1):
            script.do(zs[o, dz].wait_recv)
        script.do(last(p_ref, total, scratch))
    return script


ANY = pl.BlockSpec(memory_space=pl.ANY)
VMEM = pl.BlockSpec(memory_space=pltpu.VMEM)


def sems(count):
    return [pltpu.SemaphoreType.DMA((count,)), pltpu.SemaphoreType.DMA((count,))]


def talking(cid):
    return pltpu.CompilerParams(collective_id=cid, has_side_effects=True, vmem_limit_bytes=58 * 1024 * 1024)


def blocks(part, S, H):
    X, Y, Z = sizes(S, H)
    return part.reshape(Z, Y, X, 2, part.shape[0] // (S * H), part.shape[1])


def first_kernel(S, H, in_ref, gain_ref, named_ref, out_ref, rows, send, recv, own_sem):
    pc = Place(S, H)
    D = in_ref.shape[1]
    values = in_ref[...]
    rows[:, :D] = (values * inverse_rms(values) * gain_ref[...]).astype(B16)
    rows[:, D:] = named_ref[...]
    mail = Mail(send, recv)
    moves = gather(pc, mail, rows, out_ref, own_sem)
    greet(pc.peers())
    moves.run()
    mail.finish(gather_count(S, H))


def first_rows(hidden_in, gain, named, S, H):
    R, D = hidden_in.shape
    W = D + LANES
    return pl.pallas_call(
        functools.partial(first_kernel, S, H),
        out_shape=jax.ShapeDtypeStruct((S * H * R, W), B16),
        in_specs=[VMEM] * 3,
        out_specs=ANY,
        scratch_shapes=[pltpu.VMEM((R, W), B16), *sems(gather_count(S, H)), pltpu.SemaphoreType.DMA],
        compiler_params=talking(1),
    )(hidden_in, gain, named)


def second_kernel(S, H, width, p_ref, in_ref, gain_ref, out_ref, res_ref, mixed_ref, inv_ref, total, rows, *rest):
    scratch, (send, recv, own_sem) = rest[:-3], rest[-3:]
    pc = Place(S, H)
    D = in_ref.shape[1]
    mail = Mail(send, recv)
    sums = scatter(pc, mail, [(p_ref, total, scratch, True)])
    moves = gather(pc, mail, rows, out_ref, own_sem)
    sums.run(0, 1)
    greet(pc.peers())
    sums.run(1)
    mixed = total[:, :D]
    square = jnp.sum(total[:, D:], axis=1, keepdims=True)
    inv = lax.rsqrt(square / width + EPS)
    residual = in_ref[...] + inv * mixed
    rows[...] = (residual * inverse_rms(residual) * gain_ref[...]).astype(B16)
    moves.run(0, 1)
    mixed_ref[...] = mixed
    res_ref[...] = residual
    inv_ref[...] = jnp.broadcast_to(inv, inv_ref.shape)
    moves.run(1)
    mail.finish(scatter_count(S, H) + gather_count(S, H))


def second_rows(part, hidden_in, gain, width, S, H):
    R, D = hidden_in.shape
    count = scatter_count(S, H) + gather_count(S, H)
    return pl.pallas_call(
        functools.partial(second_kernel, S, H, width),
        out_shape=[
            jax.ShapeDtypeStruct((S * H * R, D), B16),
            jax.ShapeDtypeStruct((R, D), F32),
            jax.ShapeDtypeStruct((R, D), F32),
            jax.ShapeDtypeStruct((R, LANES), F32),
        ],
        in_specs=[ANY, VMEM, VMEM],
        out_specs=[ANY, VMEM, VMEM, VMEM],
        scratch_shapes=[
            pltpu.VMEM((R, D + LANES), F32), pltpu.VMEM((R, D), B16), *scatter_scratch(S, H, R, D + LANES),
            *sems(count), pltpu.SemaphoreType.DMA,
        ],
        compiler_params=talking(2),
    )(blocks(part, S, H), hidden_in, gain)


def third_kernel(
    S, H, width, p_ref, probs_ref, res_ref, mixed_ref, inv_ref, grad_ref, gain_ref, router_ref,
    out_ref, gres_ref, gnorm_ref, grouter_ref, total, rows, probs, *rest,
):
    scratch, (send, recv, own_sem, probs_sem) = rest[:-4], rest[-4:]
    pc = Place(S, H)
    R, D = res_ref.shape
    mail = Mail(send, recv)
    sums = scatter(pc, mail, [(p_ref, total, scratch, True)])
    moves = gather(pc, mail, rows, out_ref, own_sem)
    fetch = pltpu.make_async_copy(probs_ref.at[pl.ds(pl.multiple_of(pc.slot() * R, R), R)], probs, probs_sem)
    fetch.start()
    sums.run(0, 1)
    greet(pc.peers())
    sums.run(1)
    fetch.wait()
    p = probs[...]
    gp = total[:, D:]
    glogits = (p * (gp - jnp.sum(p * gp, axis=1, keepdims=True))).astype(B16)
    gtwo = total[:, :D] + mm(glogits, router_ref[...], NT)
    residual = res_ref[...]
    inv_two = inverse_rms(residual)
    gain = gain_ref[...]
    gres = grad_ref[...] + rms_back(residual, inv_two, gain, gtwo)
    inv = inv_ref[:, 0:1]
    cross = jnp.sum(gres * mixed_ref[...], axis=1, keepdims=True) * (inv * inv * inv) / width
    high, low = hi_lo(cross)
    lane = lax.broadcasted_iota(jnp.int32, (R, LANES), 1)
    rows[:, :D] = (inv * gres).astype(B16)
    rows[:, D:] = jnp.where(lane == 0, high.astype(F32), jnp.where(lane == 1, low.astype(F32), 0.0)).astype(B16)
    moves.run(0, 1)
    gres_ref[...] = gres
    gnorm_ref[...] = jnp.sum(gtwo * residual * inv_two, axis=0, keepdims=True)
    grouter_ref[...] = mm((residual * inv_two * gain).astype(B16), glogits, TN).astype(B16)
    moves.run(1)
    mail.finish(scatter_count(S, H) + gather_count(S, H))


def third_rows(part, probs, residual, mixed, inv_gate, out_grad, gain, router, width, S, H):
    R, D = residual.shape
    count = scatter_count(S, H) + gather_count(S, H)
    return pl.pallas_call(
        functools.partial(third_kernel, S, H, width),
        out_shape=[
            jax.ShapeDtypeStruct((S * H * R, D + LANES), B16),
            jax.ShapeDtypeStruct((R, D), F32),
            jax.ShapeDtypeStruct((1, D), F32),
            jax.ShapeDtypeStruct((D, LANES), B16),
        ],
        in_specs=[ANY, ANY] + [VMEM] * 6,
        out_specs=[ANY, VMEM, VMEM, VMEM],
        scratch_shapes=[
            pltpu.VMEM((R, D + LANES), F32), pltpu.VMEM((R, D + LANES), B16), pltpu.VMEM((R, LANES), F32),
            *scatter_scratch(S, H, R, D + LANES), *sems(count), pltpu.SemaphoreType.DMA, pltpu.SemaphoreType.DMA,
        ],
        compiler_params=talking(3),
    )(blocks(part, S, H), probs, residual, mixed, inv_gate, out_grad, gain, router)


def last_kernel(
    S, H, state, p_ref, e_ref, zx_ref, wo_ref, taps_ref, vec_ref, norms_ref, in_ref, gres_ref, gain_ref,
    gin_ref, extra_ref, sums_ref, each_ref, zx_out, wo_out, total, small, small_in, *rest,
):
    half = len(rest) - 6
    main, extra = rest[: half - 6], rest[half - 6 : half]
    send, recv, group_send, group_recv, local_sem, own_sem = rest[half:]
    pc = Place(S, H)
    seq, head = lax.axis_index("seq"), lax.axis_index("head")
    mail = Mail(send, recv)
    sums = scatter(pc, mail, [(p_ref, total, main, True), (e_ref, extra_ref, extra, False)])
    moves = gather(pc, mail, small, small_in, own_sem)
    group = []
    for m in range(1, S):
        to = (seq + m) % S
        for j, (src, dst) in enumerate(((zx_ref, zx_out), (wo_ref, wo_out))):
            group.append(
                pltpu.make_async_remote_copy(
                    src_ref=src.at[to], dst_ref=dst.at[seq], send_sem=group_send.at[j, m],
                    recv_sem=group_recv.at[j, m], device_id=(to, head), device_id_type=MESH,
                )
            )
    stay = [
        pltpu.make_async_copy(src.at[seq], dst.at[seq], local_sem.at[j])
        for j, (src, dst) in enumerate(((zx_ref, zx_out), (wo_ref, wo_out)))
    ]
    sums.run(0, 1)
    D = in_ref.shape[1]
    line = 0
    small[...] = jnp.zeros_like(small)
    for r in range(2):
        for j in range(D // LANES):
            small[line : line + 1, :] = norms_ref[r : r + 1, j * LANES : (j + 1) * LANES]
            line += 1
    wide = taps_ref.shape[1] - 2 * state
    for r in range(4):
        for j in range(2 * state // LANES):
            small[line : line + 1, :] = taps_ref[r : r + 1, wide + j * LANES : wide + (j + 1) * LANES]
            line += 1
    small[line : line + 4, :] = taps_ref[0:4, :wide]
    small[line + 4 : line + 8, :] = vec_ref[0:4, :]
    peers = pc.peers()
    barrier = pltpu.get_barrier_semaphore()
    for peer in peers:
        pl.semaphore_signal(barrier, inc=1, device_id=peer, device_id_type=MESH)
    for m in range(1, S):
        pl.semaphore_signal(barrier, inc=1, device_id=((seq + m) % S, head), device_id_type=MESH)
    pl.semaphore_wait(barrier, len(peers) + S - 1)
    sums.run(1, 3)
    moves.run(0, 1)
    for copy in stay + group:
        copy.start()
    sums.run(3, 4)
    moves.run(1, 2)
    for k in range(4, 9):
        sums.run(k, k + 1)
        if k < 8:
            moves.run(k - 2, k - 1)
    values, gone = in_ref[...], total[...]
    inv = inverse_rms(values)
    gin_ref[...] = gres_ref[...] + rms_back(values, inv, gain_ref[...], gone)
    moves.run(6)
    rows = small.shape[0]

    def add(k, value):
        return value + small_in[pl.ds(pl.multiple_of(k * rows, rows), line), :]

    sums_ref[...] = lax.fori_loop(0, S * H, add, jnp.zeros(sums_ref.shape, F32))
    for k in range(S * H):
        each_ref[k] = small_in[k * rows + line : k * rows + line + 8, :]
    for copy in group:
        copy.wait()
    for copy in stay:
        copy.wait()
    mail.finish(scatter_count(S, H, (True, False)) + gather_count(S, H))


def last_rows(part, extra, zx, wo, taps, vec, norms, hidden_in, grad_res, gain, state, S, H):
    R, D = hidden_in.shape
    N = S * H
    line = 2 * (D // LANES) + 4 * (2 * state // LANES)
    assert line % 8 == 0 and vec.shape[1] == LANES
    rows = -(-(line + 8) // 16) * 16
    tall = extra.shape[0] // N
    count = scatter_count(S, H, (True, False)) + gather_count(S, H)
    return pl.pallas_call(
        functools.partial(last_kernel, S, H, state),
        out_shape=[
            jax.ShapeDtypeStruct((R, D), F32),
            jax.ShapeDtypeStruct((tall, extra.shape[1]), F32),
            jax.ShapeDtypeStruct((line, LANES), F32),
            jax.ShapeDtypeStruct((N, 8, LANES), F32),
            jax.ShapeDtypeStruct(zx.shape, zx.dtype),
            jax.ShapeDtypeStruct(wo.shape, wo.dtype),
        ],
        in_specs=[ANY] * 4 + [VMEM] * 6,
        out_specs=[VMEM] * 4 + [ANY] * 2,
        scratch_shapes=[
            pltpu.VMEM((R, D), F32), pltpu.VMEM((rows, LANES), F32), pltpu.VMEM((N * rows, LANES), F32),
            *scatter_scratch(S, H, R, D), *scatter_scratch(S, H, tall, extra.shape[1], False), *sems(count),
            pltpu.SemaphoreType.DMA((2, S)), pltpu.SemaphoreType.DMA((2, S)), pltpu.SemaphoreType.DMA((2,)),
            pltpu.SemaphoreType.DMA,
        ],
        compiler_params=talking(4),
    )(blocks(part, S, H), blocks(extra, S, H), zx, wo, taps, vec, norms, hidden_in, grad_res, gain)


def seg_of(pos, ends_ref, count):
    found = jnp.zeros(pos.shape, jnp.int32)
    for k in range(count):
        found = found + (pos >= ends_ref[k]).astype(jnp.int32)
    return jnp.where(pos < 0, -1, found)


def exact(left, right):
    return jnp.dot(left, right, precision=lax.Precision.HIGHEST, preferred_element_type=F32)


def silu(values):
    return values / (1.0 + jnp.exp(-values))


def softplus(values):
    return jnp.maximum(values, 0.0) + jnp.log1p(jnp.exp(-jnp.abs(values)))


class Block:
    def __init__(self, i, pre, ext, z, taps_ref, rows_ref, ends_ref, count, state, C):
        n = BLOCK
        pos = i * n + lax.broadcasted_iota(jnp.int32, (n, 1), 0)
        pos_row = i * n + lax.broadcasted_iota(jnp.int32, (1, n), 1)
        seg, seg_row = seg_of(pos, ends_ref, count), seg_of(pos_row, ends_ref, count)
        self.joined = {k: ((pos >= k) & (seg_of(pos - k, ends_ref, count) == seg)).astype(F32) for k in (1, 2, 3)}
        self.later = {k: (seg_of(pos + k, ends_ref, count) == seg).astype(F32) for k in (1, 2, 3)}
        conv = taps_ref[3:4, :] * pre
        for k in (1, 2, 3):
            conv = conv + taps_ref[3 - k : 4 - k, :] * ext[8 - k : 8 - k + n, :] * self.joined[k]
        act = silu(conv)
        cp = act.shape[1] - 2 * state
        self.conv = conv
        self.x, self.b, self.c = act[:, :cp], act[:, cp : cp + state].astype(B16), act[:, cp + state :].astype(B16)
        self.m = [rows_ref[j : j + 1, :] for j in range(2)]
        self.skip, self.gain = rows_ref[2:3, :], rows_ref[3:4, :]
        self.C = C
        self.dtr = z + rows_ref[4:5, :]
        self.dt = softplus(self.dtr)
        self.decay = rows_ref[5:6, :]
        self.rate = -self.dt * self.decay
        row, col = lax.broadcasted_iota(jnp.int32, (n, n), 0), lax.broadcasted_iota(jnp.int32, (n, n), 1)
        lower = row >= col
        self.row, self.col = row, col
        logdec = exact(lower.astype(F32), self.rate)
        log_row = logdec.T
        linked = lower & (seg == seg_row)
        self.decays = [
            jnp.exp(jnp.where(linked, logdec[:, C + j : C + j + 1] - log_row[C + j : C + j + 1, :], -1e30)) for j in range(2)
        ]
        scores = mm(self.c, self.b, NT)
        self.mats = [(scores * d).astype(B16) for d in self.decays]
        before = jnp.where(i == 0, -1, seg_of(jnp.full((1, 1), i * n - 1, jnp.int32), ends_ref, count))
        final = seg_of(jnp.full((1, 1), i * n + n - 1, jnp.int32), ends_ref, count)
        last = logdec[n - 1 : n, :]
        self.carry = self.spread(jnp.where(seg == before, jnp.exp(logdec), 0.0))
        self.tail = self.spread(jnp.where(seg == final, jnp.exp(last - logdec), 0.0))
        self.keep = self.spread(jnp.where(final == before, jnp.exp(last), 0.0))
        self.dtc = self.spread(self.dt)
        self.xt = (self.dtc * self.x).astype(B16)
        self.low = [m.astype(B16) for m in self.m]
        self.xts = [self.xt * low for low in self.low]
        self.tail_xt = (self.tail * self.xt.astype(F32)).astype(B16)

    def spread(self, values):
        return values[:, self.C : self.C + 1] * self.m[0] + values[:, self.C + 1 : self.C + 2] * self.m[1]

    def inner(self):
        return mm(self.mats[0], self.xts[0]) + mm(self.mats[1], self.xts[1])


def mixer_forward_kernel(
    S, H, count, state, C, ends_ref, in_ref, w_ref, taps_ref, rows_ref, out_w_ref, grad_ref,
    pre_ref, z_ref, y_ref, st_ref, part_ref, all_ref, held, ext, send, recv, own_sem,
):
    i = pl.program_id(0)
    pc = Place(S, H)
    mail = Mail(send, recv)
    moves = gather(pc, mail, grad_ref, all_ref, own_sem)
    ready = pl.num_programs(0) - 1

    @pl.when(i == 0)
    def _():
        greet(pc.peers())
        moves.run(0, 1)

    for step, stage in ((2, 1), (3, 2), (4, 3), (5, 4), (6, 5)):

        @pl.when(i == step)
        def _():
            moves.run(stage, stage + 1)

    depth = w_ref.shape[0]
    n, cp = BLOCK, z_ref.shape[1]

    @pl.when(i == 0)
    def _():
        held[...] = jnp.zeros_like(held)
        ext[0:8, :] = jnp.zeros((8, ext.shape[1]), F32)

    made = mm(in_ref[:, :depth], w_ref[...])
    z = made[:, :cp]
    pre = made[:, cp:]
    z_ref[...], pre_ref[...] = z, pre
    ext[8 : 8 + n, :] = pre
    blk = Block(i, pre, ext, z, taps_ref, rows_ref, ends_ref, count, state, C)
    ext[0:8, :] = pre[n - 8 :, :]
    st = held[...]
    st_ref[0] = st
    y = blk.inner() + blk.carry * mm(blk.c, st.astype(B16))
    held[...] = blk.keep * st + mm(blk.b, blk.tail_xt, TN)
    y = y + blk.skip * blk.x
    y_ref[...] = y
    gated = y * silu(z)
    part_ref[:, :depth] = mm((gated * blk.gain).astype(B16), out_w_ref[...]).astype(B16)
    high, rest = hi_lo(jnp.sum(gated * gated, axis=1, keepdims=True))
    lane = lax.broadcasted_iota(jnp.int32, (n, LANES), 1)
    part_ref[:, depth:] = jnp.where(lane == 0, high.astype(F32), jnp.where(lane == 1, rest.astype(F32), 0.0)).astype(B16)

    @pl.when(i == ready)
    def _():
        moves.run(6)
        mail.finish(gather_count(S, H))


def whole(shape):
    return pl.BlockSpec(shape, lambda i: (0,) * len(shape))


def params():
    return pltpu.CompilerParams(dimension_semantics=("arbitrary",), vmem_limit_bytes=60 * 1024 * 1024)


def mixer_forward(ends, gathered, in_w, taps, rows, out_w, grad, state, C, S, H):
    T, depth = gathered.shape[0], in_w.shape[0]
    cp, nb = out_w.shape[0], gathered.shape[0] // BLOCK
    conv_width = cp + 2 * state

    def block(width):
        return pl.BlockSpec((BLOCK, width), lambda i: (i, 0))

    return pl.pallas_call(
        functools.partial(mixer_forward_kernel, S, H, ends.shape[0], state, C),
        grid=(nb,),
        in_specs=[
            pl.BlockSpec(memory_space=pltpu.SMEM), block(gathered.shape[1]), whole(in_w.shape), whole(taps.shape),
            whole(rows.shape), whole(out_w.shape), VMEM,
        ],
        out_specs=[
            block(conv_width), block(cp), block(cp),
            pl.BlockSpec((1, state, cp), lambda i: (i, 0, 0)), block(depth + LANES), ANY,
        ],
        out_shape=[
            jax.ShapeDtypeStruct((T, conv_width), F32),
            jax.ShapeDtypeStruct((T, cp), F32),
            jax.ShapeDtypeStruct((T, cp), F32),
            jax.ShapeDtypeStruct((nb, state, cp), F32),
            jax.ShapeDtypeStruct((T, depth + LANES), B16),
            jax.ShapeDtypeStruct((T, depth), B16),
        ],
        scratch_shapes=[
            pltpu.VMEM((state, cp), F32), pltpu.VMEM((BLOCK + 8, conv_width), F32), *sems(gather_count(S, H)),
            pltpu.SemaphoreType.DMA,
        ],
        compiler_params=talking(5),
    )(ends, gathered, in_w, taps, rows, out_w, grad)


def mixer_backward_kernel(
    S, H, count, state, C, ends_ref, three_ref, one_ref, pre_ref, halo_ref, z_ref, y_ref, st_ref,
    w_ref, taps_ref, rows_ref, cols_ref, out_w_ref, p_ref, sh_ref, res_ref,
    part_ref, gzx_ref, gbc_ref, gout_ref, gtaps_ref, gvec_ref, gnorm_ref, sh_out, output_ref,
    held, ext, gext, gw_ref, total, *rest,
):
    step = pl.program_id(0)
    i = pl.num_programs(0) - 1 - step
    depth = w_ref.shape[0]
    n, cp = BLOCK, z_ref.shape[1]

    scratch, (send, recv, sh_send, sh_recv, sh_sem) = rest[:-5], rest[-5:]
    pc = Place(S, H)
    N, me = S * H, pc.slot()
    mail = Mail(send, recv)
    sums = scatter(pc, mail, [(p_ref, total, scratch, True)])
    stay = pltpu.make_async_copy(sh_ref.at[me], sh_out.at[me], sh_sem)

    def to_all(function, first, last):
        def body(m, carry):
            to = (me + m) % N
            function(
                pltpu.make_async_remote_copy(
                    src_ref=sh_ref.at[to], dst_ref=sh_out.at[me], send_sem=sh_send.at[m], recv_sem=sh_recv.at[m],
                    device_id=(to // H, to % H), device_id_type=MESH,
                )
            )
            return carry

        lax.fori_loop(first, last, body, 0)

    @pl.when(step == 0)
    def _():
        sums.run(0, 1)
        stay.start()
        barrier = pltpu.get_barrier_semaphore()

        def hello(m, carry):
            to = (me + m) % N
            pl.semaphore_signal(barrier, inc=1, device_id=(to // H, to % H), device_id_type=MESH)
            return carry

        lax.fori_loop(1, N, hello, 0)
        pl.semaphore_wait(barrier, N - 1)
        sums.run(1, 2)

    for when, stage in ((1, 2), (2, 3), (3, 4), (4, 5), (5, 6), (6, 7)):

        @pl.when(step == when)
        def _():
            sums.run(stage, stage + 1)

    @pl.when(step == 1)
    def _():
        to_all(lambda copy: copy.start(), 1, N)

    @pl.when(step == 0)
    def _():
        gnorm_ref[...] = jnp.zeros_like(gnorm_ref)
        held[...] = jnp.zeros_like(held)
        gext[n : n + 8, :] = jnp.zeros((8, gext.shape[1]), F32)
        gw_ref[...] = jnp.zeros_like(gw_ref)
        gout_ref[...] = jnp.zeros_like(gout_ref)
        gtaps_ref[...] = jnp.zeros_like(gtaps_ref)
        gvec_ref[...] = jnp.zeros_like(gvec_ref)

    pre, z, y = pre_ref[...], z_ref[...], y_ref[...]
    ext[0:8, :] = jnp.where(i == 0, 0.0, halo_ref[...])
    ext[8 : 8 + n, :] = pre
    blk = Block(i, pre, ext, z, taps_ref, rows_ref, ends_ref, count, state, C)
    three = three_ref[:, :depth]
    pg = mm(three, out_w_ref[...], NT)
    cross = jnp.sum(three_ref[:, depth:].astype(F32), axis=1, keepdims=True)
    act_z = silu(z)
    gated = y * act_z
    gout_ref[...] += mm((gated * blk.gain).astype(B16), three, TN)
    grad_gated = pg * blk.gain - gated * cross
    gy = grad_gated * act_z
    gz = grad_gated * y * silu_grad(z)
    st = st_ref[0]
    st_low, grad = st.astype(B16), held[...]
    grad_low = grad.astype(B16)
    gy_low = gy.astype(B16)
    y_all = blk.inner() + blk.carry * mm(blk.c, st_low)
    back = sum(mm(blk.mats[j], gy_low * blk.low[j], TN) for j in range(2))
    gate = (blk.carry * gy_low.astype(F32)).astype(B16)
    tail_back = blk.tail * mm(blk.b, grad_low)
    pull = sum(mm(gy_low, blk.xts[j], NT) * blk.decays[j] for j in range(2)).astype(B16)
    g_c = mm(pull, blk.b) + mm(gate, st_low, NT)
    g_b = mm(pull, blk.c, TN) + mm(blk.tail_xt, grad_low, NT)
    held[...] = blk.keep * grad + mm(blk.c, gate, TN)
    g_xt = back + tail_back
    xt = blk.xt.astype(F32)
    cols = cols_ref[...]
    after = exact(gy_low.astype(F32) * y_all - xt * back, cols)
    used = exact(xt * tail_back, cols)
    through = exact(jnp.broadcast_to(blk.keep * jnp.sum(grad * st, axis=0, keepdims=True), (8, cp)), cols)[0:1, :]
    g_rate = (
        exact((blk.row <= blk.col).astype(F32), after) + exact((blk.row > blk.col).astype(F32), used) + through
    )
    g_dt = exact(g_xt * blk.x, cols) - g_rate * blk.decay
    g_dtr = g_dt / (1.0 + jnp.exp(-blk.dtr))
    g_x = g_xt * blk.dtc + blk.skip * gy
    for r, v in enumerate((pg * gated, g_dtr, g_rate * blk.rate, gy * blk.x)):
        gvec_ref[r : r + 1, :] += jnp.sum(v, axis=0, keepdims=True)
    gconv = jnp.concatenate([g_x, g_b, g_c], axis=1) * silu_grad(blk.conv)
    gext[0:n, :] = gconv
    gpre = taps_ref[3:4, :] * gconv
    gtaps_ref[3:4, :] += jnp.sum(gconv * pre, axis=0, keepdims=True)
    for k in (1, 2, 3):
        gpre = gpre + taps_ref[3 - k : 4 - k, :] * gext[k : n + k, :] * blk.later[k]
        gtaps_ref[3 - k : 4 - k, :] += jnp.sum(gconv * ext[8 - k : 8 - k + n, :] * blk.joined[k], axis=0, keepdims=True)
    gext[n : n + 8, :] = gconv[0:8, :]
    made = jnp.concatenate([gz + g_dtr, gpre], axis=1).astype(B16)
    one = one_ref[:, :depth]
    part = mm(made, w_ref[...], NT)
    part_ref[...] = part.astype(B16)
    gnorm_ref[...] += jnp.sum(part * one.astype(F32), axis=0, keepdims=True)
    gw_ref[...] += mm(made, one, TN)

    @pl.when(i == 0)
    def _():
        gzx_ref[...] = gw_ref[: 2 * cp, :].astype(B16)
        gbc_ref[...] = gw_ref[2 * cp :, :].astype(B16)
        gvec_ref[3:4, :] = exact(gvec_ref[...], cols)[3:4, :]
        sums.run(8)
        output_ref[...] = res_ref[...] + total[...]
        to_all(lambda copy: copy.wait(), 1, N)
        stay.wait()
        mail.finish(scatter_count(S, H))


def mixer_backward(ends, three, one, pre, z, y, states, in_w, taps, rows, cols, out_w, out_part, shared, residual, state, C, S, H):
    T, depth = three.shape[0], in_w.shape[0]
    cp, nb = out_w.shape[0], T // BLOCK
    conv_width = cp + 2 * state
    R = residual.shape[0]

    def block(width):
        return pl.BlockSpec((BLOCK, width), lambda k: (nb - 1 - k, 0))

    def halo(k):
        return (jnp.maximum((nb - 1 - k) * (BLOCK // 8) - 1, 0), 0)

    return pl.pallas_call(
        functools.partial(mixer_backward_kernel, S, H, ends.shape[0], state, C),
        grid=(nb,),
        in_specs=[
            pl.BlockSpec(memory_space=pltpu.SMEM), block(three.shape[1]), block(one.shape[1]), block(conv_width),
            pl.BlockSpec((8, conv_width), halo), block(cp), block(cp),
            pl.BlockSpec((1, state, cp), lambda k: (nb - 1 - k, 0, 0)),
            whole(in_w.shape), whole(taps.shape), whole(rows.shape), whole(cols.shape), whole(out_w.shape),
            ANY, ANY, whole(residual.shape),
        ],
        out_specs=[
            block(depth), whole((2 * cp, depth)), whole((2 * state, depth)), whole(out_w.shape), whole((8, conv_width)),
            whole((8, cp)), whole((1, depth)), ANY, whole(residual.shape),
        ],
        out_shape=[
            jax.ShapeDtypeStruct((T, depth), B16),
            jax.ShapeDtypeStruct((2 * cp, depth), B16),
            jax.ShapeDtypeStruct((2 * state, depth), B16),
            jax.ShapeDtypeStruct(out_w.shape, F32),
            jax.ShapeDtypeStruct((8, conv_width), F32),
            jax.ShapeDtypeStruct((8, cp), F32),
            jax.ShapeDtypeStruct((1, depth), F32),
            jax.ShapeDtypeStruct(shared.shape, shared.dtype),
            jax.ShapeDtypeStruct(residual.shape, F32),
        ],
        scratch_shapes=[
            pltpu.VMEM((state, cp), F32),
            pltpu.VMEM((BLOCK + 8, conv_width), F32),
            pltpu.VMEM((BLOCK + 8, conv_width), F32),
            pltpu.VMEM((in_w.shape[1], depth), F32),
            pltpu.VMEM(residual.shape, F32),
            *scatter_scratch(S, H, R, depth),
            *sems(scatter_count(S, H)),
            *sems(S * H),
            pltpu.SemaphoreType.DMA,
        ],
        compiler_params=talking(6),
    )(ends, three, one, pre, pre, z, y, states, in_w, taps, rows, cols, out_w, blocks(out_part, S, H), shared, residual)


def expert_kernel(
    F, FS, two_ref, grad_ref, named_ref, up_ref, down_ref, mine_ref,
    out_ref, part_ref, probs_ref, gup_ref, gdown_ref, gsh_ref, gs_ref,
):
    depth = two_ref.shape[1]

    @pl.when(pl.program_id(0) == 0)
    def _():
        gup_ref[...] = jnp.zeros_like(gup_ref)
        gdown_ref[...] = jnp.zeros_like(gdown_ref)
        gs_ref[...] = jnp.zeros_like(gs_ref)

    two, grad = two_ref[...], grad_ref[...]
    mid = mm(two, up_ref[...])
    back = mm(grad, down_ref[...], NT)
    gate, lin = mid[:, :F], mid[:, F : 2 * F]
    s_gate, s_lin = mid[:, 2 * F : 2 * F + LANES], mid[:, 2 * F + LANES :]
    named = named_ref[...].astype(F32) > 0
    logits = jnp.where(named, s_gate, -1e30)
    odds = jnp.where(named, jnp.exp(logits - jnp.max(logits, axis=1, keepdims=True)), 0.0)
    probs = odds / jnp.sum(odds, axis=1, keepdims=True)
    probs_ref[...] = probs
    mine = mine_ref[...]
    weight = jnp.sum(probs * mine, axis=1, keepdims=True)
    s_back, back = back[:, F:], back[:, :F]
    act_gate, act_s = silu(gate), silu(s_gate)
    acting = act_gate * lin
    gp = jnp.sum(acting * back, axis=1, keepdims=True)
    back = weight * back
    down_in = jnp.concatenate([weight * acting, act_s * s_lin], axis=1).astype(B16)
    mid_grad = jnp.concatenate(
        [back * lin * silu_grad(gate), back * act_gate, s_back * s_lin * silu_grad(s_gate), s_back * act_s], axis=1
    ).astype(B16)
    out_ref[...] = mm(down_in, down_ref[...]).astype(B16)
    part_ref[:, :depth] = mm(mid_grad, up_ref[...], NT).astype(B16)
    part_ref[:, depth:] = (gp * mine).astype(B16)
    gup_ref[...] += mm(two, mid_grad[:, : 2 * F], TN)
    gdown_ref[...] += mm(down_in[:, :F], grad, TN)
    gs_ref[: 2 * LANES, :] += mm(mid_grad[:, 2 * F :], two, TN)
    gs_ref[2 * LANES :, :] += mm(down_in[:, F:], grad, TN)

    @pl.when(pl.program_id(0) == pl.num_programs(0) - 1)
    def _():
        for k in range(3):
            gsh_ref[k] = gs_ref[k * LANES : k * LANES + gsh_ref.shape[1], :].astype(B16)


def experts(two, all_grad, gathered, up_w, down_w, mine, F, FS):
    T, depth = two.shape
    tall = -(-FS // 16) * 16

    def block(width):
        return pl.BlockSpec((BLOCK, width), lambda i: (i, 0))

    return pl.pallas_call(
        functools.partial(expert_kernel, F, FS),
        grid=(T // BLOCK,),
        in_specs=[
            block(depth), block(depth), pl.BlockSpec((BLOCK, LANES), lambda i: (i, depth // LANES)),
            whole(up_w.shape), whole(down_w.shape), whole(mine.shape),
        ],
        out_specs=[
            block(depth), block(depth + LANES), block(LANES), whole((depth, 2 * F)), whole((F, depth)),
            whole((3, tall, depth)),
        ],
        out_shape=[
            jax.ShapeDtypeStruct((T, depth), B16),
            jax.ShapeDtypeStruct((T, depth + LANES), B16),
            jax.ShapeDtypeStruct((T, LANES), F32),
            jax.ShapeDtypeStruct((depth, 2 * F), F32),
            jax.ShapeDtypeStruct((F, depth), F32),
            jax.ShapeDtypeStruct((3, tall, depth), B16),
        ],
        scratch_shapes=[pltpu.VMEM((3 * LANES, depth), F32)],
        compiler_params=params(),
    )(two, all_grad, gathered, up_w, down_w, mine)


def local(
    hidden_in, norm1_gain, w_zx, w_bc, w_dt, conv_x, conv_bc, dt_bias, a_log, d_skip, gate_gain,
    w_out, norm2_gain, router, expert_up, expert_down, shared_up, shared_down, out_grad,
    seq_lengths, routes,
):
    S, H = lax.axis_size("seq"), lax.axis_size("head")
    N = S * H
    s = lax.axis_index("seq")
    g = s * H + lax.axis_index("head")
    R, D = hidden_in.shape
    heads, inner = dt_bias.shape[0], conv_x.shape[1]
    size = inner // heads
    state = w_bc.shape[1] // 2
    width = inner * H
    C = inner // S
    CP = -(-(C + 2) // LANES) * LANES
    E = N // 2
    F = expert_down.shape[1]
    FS = shared_down.shape[0] // N
    per = D // N

    named = jnp.sum(
        (routes[:, :, None] == jnp.arange(E, dtype=jnp.int32)[None, None, :]).astype(F32), axis=1
    )
    named = jnp.pad(named.astype(B16), ((0, 0), (FS, LANES - FS - E)))
    gain1, gain2 = norm1_gain[None], norm2_gain[None]
    gathered = first_rows(hidden_in, gain1, named, S, H)

    firsts = [min(k * C // size, heads - 2) for k in range(S)]
    first = jnp.minimum(s * C // size, heads - 2)
    channel = jnp.arange(CP)
    masks = jnp.stack(
        [((channel < C) & ((s * C + channel) // size - first == j)).astype(F32) for j in range(2)]
    )

    def mine(values, axis, offset, length):
        return lax.dynamic_slice_in_dim(values, offset, length, axis)

    def channels(values, axis):
        cut = mine(values, axis, s * C, C)
        pads = [(0, 0)] * values.ndim
        pads[axis] = (0, CP - C)
        return jnp.pad(cut, pads)

    def in_free(values):
        return jnp.pad(values, [(0, 0)] * (values.ndim - 1) + [(C, CP - C - 2)])

    zx_w = mine(w_zx, 2, s * C, C)
    in_w = jnp.concatenate(
        [
            zx_w[:, 0], pad_lanes(mine(w_dt, 1, first, 2), CP - C), pad_lanes(zx_w[:, 1], CP), w_bc,
        ],
        axis=1,
    )
    taps = jnp.concatenate([channels(conv_x, 1), conv_bc], axis=1)
    bias, alog, skip = (mine(v, 0, first, 2) for v in (dt_bias, a_log, d_skip))
    gain = channels(gate_gain, 0)
    out_w = channels(w_out, 0)
    rows = jnp.concatenate(
        [masks, (skip @ masks)[None], gain[None], in_free(jnp.stack([bias, jnp.exp(alog)]))], axis=0
    )
    rows = jnp.pad(rows, ((0, 2), (0, 0)))
    cols = in_free(masks.T)
    ends = jnp.cumsum(seq_lengths)

    pre, z, y, states, part, all_grad = mixer_forward(
        ends, gathered, in_w, taps, rows, out_w, out_grad.astype(B16), state, C, S, H
    )
    two, residual, mixed, inv_gate = second_rows(part, hidden_in, gain2, width, S, H)

    sup = mine(shared_up, 2, g * FS, FS)
    router_w = jnp.pad(router, ((0, 0), (FS, LANES - FS - E)))
    up_w = jnp.concatenate(
        [
            expert_up[0].reshape(D, 2 * F), sup[:, 0], router_w[:, FS:], pad_lanes(sup[:, 1], LANES),
        ],
        axis=1,
    )
    down_w = jnp.concatenate([expert_down[0], mine(shared_down, 0, g * FS, FS), jnp.zeros((LANES - FS, D), B16)], axis=0)
    is_mine = (jnp.arange(LANES) == FS + g // 2).astype(F32)[None]
    out_part, two_part, probs, grad_up, grad_down, grad_shared = experts(
        two, all_grad, gathered, up_w, down_w, is_mine, F, FS
    )
    three, grad_res, norm2_part, router_part = third_rows(
        two_part, probs, residual, mixed, inv_gate, out_grad, gain2, router_w, width, S, H
    )
    tall_s = grad_shared.shape[1]
    shared = grad_shared.reshape(3 * tall_s, N, per).transpose(1, 0, 2)
    one_part, grad_zx_w, grad_bc_w, grad_out_w, tap_part, vec_part, norm1_part, sh_in, output = mixer_backward(
        ends, three, gathered, pre, z, y, states, in_w, taps, rows, cols, out_w, out_part, shared, residual,
        state, C, S, H,
    )
    tall = -(-per // 16) * 16
    extra = jnp.concatenate([grad_bc_w.T, router_part], axis=1).reshape(N, per, 2 * state + LANES)
    extra = jnp.pad(extra, ((0, 0), (0, tall - per), (0, 0))).reshape(N * tall, 2 * state + LANES)
    cut = -(-(C + 2) // 16) * 16
    zx_rows = jnp.concatenate([grad_zx_w[:cut], grad_zx_w[CP : CP + C]], axis=0)
    zx_rows = jnp.pad(zx_rows, ((0, -(cut + C) % 16), (0, 0)))
    wo_rows = jnp.pad(grad_out_w[:C].astype(B16), ((0, -C % 16), (0, 0)))

    def by_seq(values):
        return values.reshape(values.shape[0], S, D // S).transpose(1, 0, 2)

    grad_in, extra_sum, sums, singles, zx_in, wo_in = last_rows(
        one_part, extra, by_seq(zx_rows), by_seq(wo_rows), tap_part, vec_part,
        jnp.concatenate([norm1_part, norm2_part], axis=0), hidden_in, grad_res, gain1, state, S, H,
    )
    grad_bc, grad_router = extra_sum[:per, : 2 * state], extra_sum[:per, 2 * state :][:, FS : FS + E]
    grad_zx = jnp.stack([zx_in[:, :C], zx_in[:, cut : cut + C]], axis=0)
    grad_zx = grad_zx.transpose(3, 0, 1, 2).reshape(D // S, 2, inner).astype(F32)
    pick = jnp.asarray(
        [[[float(firsts[k] + j == h) for h in range(heads)] for j in range(2)] for k in range(S)], F32
    )
    exactly = lax.Precision.HIGHEST
    grad_w_dt = jnp.einsum("kjd,kjh->dh", zx_in[:, C : C + 2].astype(F32), pick, precision=exactly)
    grad_w_out = wo_in[:, :C].reshape(inner, D // S).astype(F32)
    sh_in = sh_in.reshape(N, 3, tall_s, per)[:, :, :FS]
    grad_shared_up = sh_in[:, :2].transpose(3, 1, 0, 2).reshape(per, 2, N * FS).astype(F32)
    grad_shared_down = sh_in[:, 2].reshape(N * FS, per).astype(F32)
    lines = D // LANES
    grad_norm1 = sums[:lines].reshape(D) / norm1_gain
    grad_norm2 = sums[lines : 2 * lines].reshape(D)
    grad_conv_bc = sums[2 * lines :].reshape(4, 2 * state)
    singles = singles.reshape(S, H, 8, LANES)
    by_channel = singles[:, :, :5, :C].transpose(2, 1, 0, 3).reshape(5, width)
    grad_conv_x, grad_gate_gain = by_channel[:4], by_channel[4]
    by_head = jnp.einsum("kgrj,kjh->rgh", singles[:, :, 5:, C : C + 2], pick, precision=exactly).reshape(3, heads * H)
    grad_dt_bias, grad_a_log, grad_d_skip = by_head[0], by_head[1], by_head[2]
    grad_up, grad_down = grad_up.reshape(expert_up.shape), grad_down.reshape(expert_down.shape)
    return (
        output, grad_in, grad_norm1, grad_zx, grad_bc, grad_w_dt, grad_conv_x, grad_conv_bc, grad_dt_bias,
        grad_a_log, grad_d_skip, grad_gate_gain, grad_w_out, grad_norm2, grad_router, grad_up, grad_down,
        grad_shared_up, grad_shared_down,
    )


def solution(mesh):
    return jax.shard_map(
        local,
        mesh=mesh,
        in_specs=(
            P(("seq", "head"), None),
            P(),
            P(None, None, "head"),
            P(),
            P(None, "head"),
            P(None, "head"),
            P(),
            P("head"),
            P("head"),
            P("head"),
            P("head"),
            P("head", None),
            P(),
            P(),
            P(("seq", "head"), None, None, None),
            P(("seq", "head"), None, None),
            P(),
            P(),
            P(("seq", "head"), None),
            P(),
            P(("seq", "head"), None),
        ),
        out_specs=(
            P(("seq", "head"), None),
            P(("seq", "head"), None),
            P(),
            P("seq", None, "head"),
            P(("seq", "head"), None),
            P("seq", "head"),
            P(),
            P(),
            P(),
            P(),
            P(),
            P(),
            P("head", "seq"),
            P(),
            P(("seq", "head"), None),
            P(("seq", "head"), None, None, None),
            P(("seq", "head"), None, None),
            P(("seq", "head"), None, None),
            P(None, ("seq", "head")),
        ),
        check_vma=False,
    )
```

time: 592 us -> 493 us (0.83)
  Pallas kernels: 460 us -> 423 us
  local copies, waits for them, and re-layouts: 90.6 us -> 54.4 us
  between operations: 14.5 us -> 1.18 us
  other arithmetic: 23.8 us -> 12 us
    unnamed x61, local copies, waits for them, and re-layouts: 29.8 us -> 12 us
    pallas_call x1, Pallas kernels: 96.9 us -> 83.1 us  [third_rows(): pl.pallas_call(functools.partial(third_kernel, S, H, width), out_shape=[j...]
    pallas_call x1, Pallas kernels: 59.5 us -> 46.1 us  [first_rows(): pl.pallas_call(functools.partial(first_kernel, S, H), out_shape=jax.Shape...]
    slice x11 -> x13, local copies, waits for them, and re-layouts: 15.6 us -> 10.1 us  [the longest x1 4.42 us: local(): zx_w[:, 0]]
    reshape x10 -> x9, local copies, waits for them, and re-layouts: 13.8 us -> 11.3 us  [the longest x1 5.3 us: local(): grad_up.reshape(expert_up.shape)]
  transfers between devices with their start and end apart: 2 -> 0, of which waited for: 0 -> 0; matrix products, arithmetic and copies ran while one was open for 18% -> 0% of each run, Pallas kernels for 72% -> 0%
where the time goes in v2:
time: 493 us; the launch traced here: 492 us
  Pallas kernels  423 us (86%)
  local copies, waits for them, and re-layouts  54.4 us (11%)
  other arithmetic  12 us (2%)
    pallas_call x1, Pallas kernels, third_rows(): pl.pallas_call(functools.partial(third_kernel, S, H, width), out_shape=[j...  83.1 us
    pallas_call x1, Pallas kernels, second_rows(): pl.pallas_call(functools.partial(second_kernel, S, H, width), out_shape=[...  82.1 us
    pallas_call x1, Pallas kernels, last_rows(): pl.pallas_call(functools.partial(last_kernel, S, H, state), out_shape=[ja...  66.9 us
    pallas_call x1, Pallas kernels, mixer_backward(): pl.pallas_call(functools.partial(mixer_backward_kernel, S, H, ends.shape[...  65.2 us
    pallas_call x1, Pallas kernels, first_rows(): pl.pallas_call(functools.partial(first_kernel, S, H), out_shape=jax.Shape...  46.1 us
    pallas_call x1, Pallas kernels, mixer_forward(): pl.pallas_call(functools.partial(mixer_forward_kernel, S, H, ends.shape[0...  45.2 us
    pallas_call x1, Pallas kernels, experts(): pl.pallas_call(functools.partial(expert_kernel, F, FS), grid=(T // BLOCK,...  34.5 us
    unnamed x61, local copies, waits for them, and re-layouts  12 us

profile of v2, /device:TPU:0, one launch (start us, length us, event | category | flops | bytes accessed | tf_op | source)
XLA Modules:
  0.0 491.8 jit_solution(14760353350997607483)
XLA Ops:
  0.7 1.0 constant_dynamic-slice_fusion.6
  1.9 4.4 constant_dynamic-slice_fusion.1
  6.5 1.5 fusion.7.w_ref
  8.4 0.8 dynamic_slice.34
  9.2 0.6 pad.50.rows_ref
  9.8 1.0 constant_dynamic-slice_fusion.4
  10.8 0.8 pad.51.out_w_ref
  11.6 0.8 constant_dynamic-slice_fusion.5
  12.3 1.3 select_maximum_fusion.taps_ref
  13.6 0.6 broadcast_in_dim.18.gain_ref
  14.2 0.7 convert_reduce_fusion
  15.0 0.7 pad.44.named_ref
  15.7 46.1 %shard_map.357.in_ref.named_ref.one_ref = bf16[2048,1664]{1,0:T(8,128)(2,1)} custom-call(f32[64,1536]{1,0:T(8,128)} %in_ref.5, f32[1,1536]{1,0:T(1,128)} %broadcast_in_dim.18.gain_ref, bf16[64,128]{1,0:T(8,128)(2,1)} %pad.44.named_ref), custom_call_target="tpu_custom_call" | custom-call | tf_op jit(solution)/shard_map/pallas_call | solution.py:408
  61.8 1.3 reduce-window.9
  63.1 0.7 convert_element_type.97.grad_ref
  63.8 45.2 %shard_map.358 = (f32[2048,384]{1,0:T(8,128)}, f32[2048,128]{1,0:T(8,128)}, f32[2048,128]{1,0:T(8,128)}, f32[8,128,128]{2,1,0:T(8,128)}, bf16[2048,1664]{1,0:T(8,128)(2,1)}, /*index=5*/bf16[2048,1536]{1,0:T(8,128)(2,1)}) custom-call(s32[4]{0:T(128)} %bitcast.106, bf16[2048,1664]{1,0:T(8,128)(2,1)} %shard_map.357.in_ref.named_ref.one_ref, ...), custom_call_target="tpu_custom_call" | custom-call | tf_op jit(solution)/shard_map/pallas_call | solution.py:769
  109.1 0.6 broadcast_in_dim.21.gain_ref
  109.7 82.1 %shard_map.359 = (bf16[2048,1536]{1,0:T(8,128)(2,1)}, f32[64,1536]{1,0:T(8,128)}, f32[64,1536]{1,0:T(8,128)}, f32[64,128]{1,0:T(8,128)}) custom-call(bf16[4,2,2,2,64,1664]{5,4,3,2,1,0:T(8,128)(2,1)} %bitcast.87, f32[64,1536]{1,0:T(8,128)} %in_ref.5, f32[1,1536]{1,0:T(1,128)} %broadcast_in_dim.21.gain_ref), custom_call_target="tpu_custom_call" | custom-call | tf_op jit(solution)/shard_map/pallas_call | solution.py:444
  192.3 3.4 constant_dynamic-slice_fusion
  195.6 1.0 copy_bitcast_fusion.2
  196.6 1.0 copy.123
  197.8 1.8 copy.151
  199.6 2.1 fusion.5.up_ref
  201.8 1.2 maximum_maximum_fusion.down_ref
  203.1 34.5 %shard_map.360 = (bf16[2048,1536]{1,0:T(8,128)(2,1)}, bf16[2048,1664]{1,0:T(8,128)(2,1)}, f32[2048,128]{1,0:T(8,128)}, f32[1536,512]{1,0:T(8,128)}, f32[256,1536]{1,0:T(8,128)}, /*index=5*/bf16[3,32,1536]{2,1,0:T(8,128)(2,1)}) custom-call(bf16[2048,1536]{1,0:T(8,128)(2,1)} %get-tuple-element.55.two_ref, bf16[2048,1536]{1,0:T(8,128)(2,1)} %get-tuple-element.56.grad_ref, ...), custom_call_target="tpu_custom_call" | custom-call | tf_op jit(solution)/shard_map/pallas_call | solution.py:1034
  237.6 0.9 pad.52.router_ref
  238.5 83.1 %shard_map.361 = (bf16[2048,1664]{1,0:T(8,128)(2,1)}, f32[64,1536]{1,0:T(8,128)}, f32[1,1536]{1,0:T(1,128)}, bf16[1536,128]{1,0:T(8,128)(2,1)}) custom-call(bf16[4,2,2,2,64,1664]{5,4,3,2,1,0:T(8,128)(2,1)} %bitcast.86, f32[2048,128]{1,0:T(8,128)} %get-tuple-element.58.probs_ref, f32[64,1536]{1,0:T(8,128)} %get-tuple-element.59.res_ref, ...), custom_call_target="tpu_custom_call" | custom-call | tf_op jit(solution)/shard_map/pallas_call | solution.py:503
  321.6 0.8 reshape.226
  322.4 1.2 copy.163
  323.7 0.7 pad.54.cols_ref
  324.4 65.2 %shard_map.362 = (bf16[2048,1536]{1,0:T(8,128)(2,1)}, bf16[256,1536]{1,0:T(8,128)(2,1)}, bf16[256,1536]{1,0:T(8,128)(2,1)}, f32[128,1536]{1,0:T(8,128)}, f32[8,3...) custom-call(s32[4]{0:T(128)} %bitcast.107, ...), custom_call_target="tpu_custom_call" | custom-call | tf_op jit(solution)/shard_map/pallas_call | solution.py:940
  389.6 1.3 pad_maximum_fusion.2.norms_ref
  390.9 1.0 slice.90
  391.9 1.0 slice.91
  393.0 0.6 reshape.228
  393.6 1.1 copy.162
  395.0 1.4 copy.127
  396.4 1.1 slice.127
  397.8 0.8 copy.164
  398.6 66.9 %shard_map.363 = (f32[64,1536]{1,0:T(8,128)}, f32[48,384]{1,0:T(8,128)}, f32[32,128]{1,0:T(8,128)}, f32[32,8,128]{2,1,0:T(8,128)}, bf16[8,208,192]{2,1,0:T(8,128)(2,1)}, /*index=5*/bf16[8,96,192]{2,1,0:T(8,128)(2,1)}) custom-call(bf16[4,2,2,2,64,1536]{5,4,3,2,1,0:T(8,128)(2,1)} %bitcast.91, bf16[4,2,2,2,48,384]{5,4,3,2,1,0:T(8,128)(2,1)} %bitcast.92, ...), custom_call_target="tpu_custom_call" | custom-call | tf_op jit(solution)/shard_map/pallas_call | solution.py:606
  465.5 1.2 slice_bitcast_fusion.1
  466.9 1.5 copy.135
  468.5 1.1 copy.136
  469.6 0.7 slice.100
  470.4 0.7 squeeze.35
  471.6 0.6 squeeze.32
  472.2 0.6 squeeze.33
  472.7 0.6 squeeze.34
  473.3 0.6 slice.96
  474.0 0.7 copy.137
  474.7 0.8 slice.97
  475.5 0.8 convolution_bitcast_fusion
  476.3 0.6 bitcast_divide_fusion
  476.9 0.6 reshape.232
  477.5 0.6 slice_bitcast_fusion.2
  478.2 1.2 copy.149
  479.6 0.7 reshape.239
  480.3 1.1 copy.138
  481.3 1.0 slice.120
  482.3 0.6 copy.150
  482.9 1.1 reshape.240
  484.0 5.3 %reshape.234 = f32[1,1536,2,256]{3,2,1,0:T(2,128)} reshape(f32[1536,512]{1,0:T(8,128)} %get-tuple-element.86) | data formatting | bytes 6291456 | tf_op jit(solution)/shard_map/reshape | solution.py:1186
  489.3 0.7 copy.168
  490.1 1.8 copy.169
  (81 shorter events, 3.6 us)
Async XLA Ops:
  0.7 201.1 %copy-start = (bf16[1024,1536]{1,0:T(8,128)(2,1)S(1)}, bf16[1024,1536]{1,0:T(8,128)(2,1)}, u32[]{:S(2)}) copy-start(bf16[1024,1536]{1,0:T(8,128)(2,1)} %param.39) | copy-start | bytes 9437188
  1.9 4.6 copy-start.5
  6.5 1.6 copy-start.20
  6.5 1.5 copy-start.21
  6.5 1.7 copy-start.22
  6.5 7.1 %copy-start.15 = (f32[1536]{0:T(1024)S(1)}, f32[1536]{0:T(1024)}, u32[]{:S(2)}) copy-start(f32[1536]{0:T(1024)} %param.23) | copy-start | bytes 18436
  15.7 47.4 %copy-start.2 = (f32[64,1536]{1,0:T(8,128)S(1)}, f32[64,1536]{1,0:T(8,128)}, u32[]{:S(2)}) copy-start(f32[64,1536]{1,0:T(8,128)} %grad_ref.1) | copy-start | bytes 1179652
  63.8 45.2 %copy-start.17 = (f32[1536]{0:T(1024)S(1)}, f32[1536]{0:T(1024)}, u32[]{:S(2)}) copy-start(f32[1536]{0:T(1024)} %param.34) | copy-start | bytes 18436
  197.6 1.9 copy-start.3
  197.7 1.9 copy-start.4
  199.6 2.2 copy-start.6
  238.5 83.1 %copy-start.13 = (bf16[3,32,1536]{2,1,0:T(8,128)(2,1)S(1)}, bf16[3,32,1536]{2,1,0:T(8,128)(2,1)}, u32[]{:S(2)}) copy-start(bf16[3,32,1536]{2,1,0:T(8,128)(2,1)} %get-tuple-element.68) | copy-start | bytes 884740
  324.4 65.2 %copy-start.19 = (f32[1,1536]{1,0:T(1,128)S(1)}, f32[1,1536]{1,0:T(1,128)}, u32[]{:S(2)}) copy-start(f32[1,1536]{1,0:T(1,128)} %get-tuple-element.78) | copy-start | bytes 18436
  392.9 1.8 copy-start.10
  392.9 2.0 copy-start.8
  466.7 1.7 copy-start.11
  466.9 2.7 copy-start.12
  466.9 4.4 copy-start.18
  468.4 4.9 %copy-start.14 = (f32[48,384]{1,0:T(8,128)S(1)}, f32[48,384]{1,0:T(8,128)}, u32[]{:S(2)}) copy-start(f32[48,384]{1,0:T(8,128)} %get-tuple-element.83) | copy-start | bytes 221188
  468.4 7.1 %copy-start.23 = (f32[8,2,12]{2,0,1:T(8,128)S(1)}, f32[8,2,12]{2,0,1:T(8,128)}, u32[]{:S(2)}) copy-start(f32[8,2,12]{2,0,1:T(8,128)} %constant.74.clone) | copy-start | bytes 2308
  468.4 7.9 %copy-start.16 = (f32[32,128]{1,0:T(8,128)S(1)}, f32[32,128]{1,0:T(8,128)}, u32[]{:S(2)}) copy-start(f32[32,128]{1,0:T(8,128)} %get-tuple-element.81) | copy-start | bytes 49156
  468.4 9.7 %copy-start.7 = (bf16[32,96,48]{2,1,0:T(8,128)(2,1)S(1)}, bf16[32,96,48]{2,1,0:T(8,128)(2,1)}, u32[]{:S(2)}) copy-start(bf16[32,96,48]{2,1,0:T(8,128)(2,1)} %get-tuple-element.88) | copy-start | bytes 884740
  484.0 5.3 %copy-start.9 = (f32[64,1536]{1,0:T(8,128)S(1)}, f32[64,1536]{1,0:T(8,128)}, u32[]{:S(2)}) copy-start(f32[64,1536]{1,0:T(8,128)} %get-tuple-element.220) | copy-start | bytes 1179652
  484.0 7.8 %copy-start.1 = (bf16[1024,1536]{1,0:T(8,128)(2,1)S(1)}, bf16[1024,1536]{1,0:T(8,128)(2,1)}, u32[]{:S(2)}) copy-start(bf16[1024,1536]{1,0:T(8,128)(2,1)} %param.39) | copy-start | bytes 9437188

commit v3 on v2

v3 whole, which is shorter than its diff:
```python
import functools
import jax
import jax.numpy as jnp
from jax import lax
from jax.experimental import pallas as pl
from jax.experimental.pallas import tpu as pltpu
from jax.sharding import PartitionSpec as P

MESH = pl.DeviceIdType.MESH
BLOCK = 256
EPS = 1e-05
LANES = 128
B16 = jnp.bfloat16
F32 = jnp.float32


def mm(left, right, dims=(((1,), (0,)), ((), ()))):
    return lax.dot_general(left, right, dims, preferred_element_type=F32)


NT = (((1,), (1,)), ((), ()))
TN = (((0,), (0,)), ((), ()))


def inverse_rms(values):
    return lax.rsqrt(jnp.mean(values * values, axis=-1, keepdims=True) + EPS)


def rms_back(values, inverse, gain, grad):
    weighted = grad * gain
    inner = jnp.mean(weighted * values, axis=-1, keepdims=True)
    return inverse * weighted - values * inverse**3 * inner


def silu_grad(values):
    sig = jax.nn.sigmoid(values)
    return sig * (1.0 + values * (1.0 - sig))


def pad_lanes(values, width):
    return jnp.pad(values, [(0, 0)] * (values.ndim - 1) + [(0, width - values.shape[-1])])


def hi_lo(values):
    high = values.astype(B16)
    return high, (values - high.astype(F32)).astype(B16)


def sizes(seq_size, head_size):
    return head_size // 2, head_size // 2, seq_size // (head_size // 2)


class Place:
    def __init__(self, seq_size, head_size):
        self.H = head_size
        self.X, self.Y, self.Z = sizes(seq_size, head_size)
        assert self.Z == 4
        seq, head = lax.axis_index("seq"), lax.axis_index("head")
        self.z, self.y = seq // self.Y, seq % self.Y
        self.x, self.c = head // 2, head % 2
        z = self.z
        self.partners = (z, z + 1 - 2 * (z % 2), (z + 2) % 4, 3 - z)

    def at(self, dz=0, dy=0, dx=0, dc=0):
        return (
            self.partners[dz],
            (self.y + dy) % self.Y if dy else self.y,
            (self.x + dx) % self.X if dx else self.x,
            1 - self.c if dc else self.c,
        )

    def dev(self, **where):
        z, y, x, c = self.at(**where)
        return (z * self.Y + y, x * 2 + c)

    def slot(self, **where):
        z, y, x, c = self.at(**where)
        return (z * self.Y + y) * self.H + x * 2 + c

    def partner(self, dz):
        return (self.z // 2 + dz // 2) % 2 * 2 + (self.z + dz) % 2

    def peers(self, direct=False):
        out = [self.dev(dz=k) for k in range(1, 4 if direct else 3)]
        out += [self.dev(dy=k) for k in range(1, self.Y)]
        out += [self.dev(dx=k) for k in range(1, self.X)]
        return out + [self.dev(dc=1)]


def greet(peers):
    barrier = pltpu.get_barrier_semaphore()
    for peer in peers:
        pl.semaphore_signal(barrier, inc=1, device_id=peer, device_id_type=MESH)
    pl.semaphore_wait(barrier, len(peers))


class Mail:
    def __init__(self, send, recv):
        self.send, self.recv, self.made = send, recv, []

    def copy(self, src, dst, dev):
        i = len(self.made)
        self.made.append(
            pltpu.make_async_remote_copy(
                src_ref=src, dst_ref=dst, send_sem=self.send.at[i], recv_sem=self.recv.at[i],
                device_id=dev, device_id_type=MESH,
            )
        )
        return self.made[-1]

    def finish(self, count):
        assert len(self.made) == count
        for copy in self.made:
            copy.wait_send()


class Script(list):
    def stage(self):
        self.append([])

    def do(self, action):
        self[-1].append(action)

    def run(self, first=0, last=None):
        for stage in self[first:last]:
            for action in stage:
                action()


def gather_count(S, H):
    X, Y, Z = sizes(S, H)
    return (Z - 1) + 2 * Z * (X + Y - 2) + 2 * Z * (X - 1) * (Y - 1) + X * Y * Z


def gather(pc, mail, x_ref, out_ref, own_sem, planes=False):
    X, Y, Z = pc.X, pc.Y, pc.Z
    R = x_ref.shape[0]
    half = R // 2
    script = Script()

    def rows(part, **where):
        base = pl.multiple_of(pc.slot(**where) * R, R)
        if part is None:
            return out_ref.at[pl.ds(base, R)]
        return out_ref.at[pl.ds(pl.multiple_of(base + part * half, half), half)]

    def send(src, dst, dev):
        copy = mail.copy(src, dst, dev)
        script.do(copy.start)
        return copy

    x_in, y_in, dga, dgb = {}, {}, {}, {}
    sib = {dz: [] for dz in range(Z)}

    def column(dz):
        for part in (0, 1):
            src = x_ref.at[pl.ds(part * half, half)] if dz == 0 else rows(part, dz=dz)
            for k in range(1, X):
                x_in[dz, k, part] = send(src, rows(part, dz=dz), pc.dev(dx=k))
            other = 1 - part
            src = x_ref.at[pl.ds(other * half, half)] if dz == 0 else rows(other, dz=dz)
            for k in range(1, Y):
                y_in[dz, k, other] = send(src, rows(other, dz=dz), pc.dev(dy=k))
        src = x_ref if dz == 0 else rows(None, dz=dz)
        sib[dz].append(send(src, rows(None, dz=dz), pc.dev(dc=1)))

    def onward(dz):
        for k in range(1, X):
            script.do(x_in[dz, k, 0].wait_recv)
            block = rows(0, dz=dz, dx=-k)
            for m in range(1, Y):
                dga[dz, k, m] = send(block, block, pc.dev(dy=m))
        for k in range(1, Y):
            script.do(y_in[dz, k, 1].wait_recv)
            block = rows(1, dz=dz, dy=-k)
            for m in range(1, X):
                dgb[dz, k, m] = send(block, block, pc.dev(dx=m))
        for k in range(1, X):
            script.do(x_in[dz, k, 1].wait_recv)
            block = rows(None, dz=dz, dx=-k)
            sib[dz].append(send(block, block, pc.dev(dc=1)))
        for k in range(1, Y):
            script.do(y_in[dz, k, 0].wait_recv)
            block = rows(None, dz=dz, dy=-k)
            sib[dz].append(send(block, block, pc.dev(dc=1)))

    def corner(dz):
        for k in range(1, X):
            for m in range(1, Y):
                script.do(dga[dz, k, m].wait_recv)
                script.do(dgb[dz, m, k].wait_recv)
                block = rows(None, dz=dz, dx=-k, dy=-m)
                sib[dz].append(send(block, block, pc.dev(dc=1)))

    own = pltpu.make_async_copy(x_ref, rows(None), own_sem)
    script.stage()
    script.do(own.start)
    first = send(x_ref, rows(None), pc.dev(dz=1))
    column(0)
    second = send(x_ref, rows(None), pc.dev(dz=2))
    script.stage()
    script.do(first.wait_recv)
    column(1)
    script.stage()
    onward(0)
    script.stage()
    corner(0)
    script.stage()
    script.do(second.wait_recv)
    third = send(rows(None, dz=2), rows(None, dz=2), pc.dev(dz=1))
    column(2)
    script.stage()
    onward(1)
    script.stage()
    script.do(third.wait_recv)
    column(3)
    script.stage()
    corner(1)
    for dz in (2, 3):
        script.stage()
        onward(dz)
        script.stage()
        corner(dz)
    if not planes:
        for dz in range(Z):
            for copy in sib[dz]:
                script.do(copy.wait_recv)
        script.do(own.wait)
        return script
    for dz in range(Z):
        script.stage()
        for copy in sib[dz]:
            script.do(copy.wait_recv)
        if dz == 0:
            script.do(own.wait)
    return script


def scatter_parts(split):
    return (("y", 0), ("x", 1)) if split else (("x", None),)


def scatter_count(S, H, splits=(True,)):
    X, Y, Z = sizes(S, H)
    pieces = sum(len(scatter_parts(split)) for split in splits)
    return len(splits) * (Z + Z - 1) + pieces * Z * (X + Y - 2)


def sum_scratch(S, H, R, W, split=True):
    X, Y, Z = sizes(S, H)
    out = [pltpu.VMEM((Z, Y, X, R, W), B16), pltpu.VMEM((Z - 1, R, W), B16)]
    for axis, part in scatter_parts(split):
        rows = R if part is None else R // 2
        first, second = (Y, X) if axis == "y" else (X, Y)
        out += [pltpu.VMEM((Z, first - 1, second, rows, W), B16), pltpu.VMEM((Z, second - 1, rows, W), B16)]
    return out


def scatter_scratch(S, H, R, W, split=True):
    X, Y, Z = sizes(S, H)
    return [pltpu.VMEM((Z, Y, X, R, W), B16), *sum_scratch(S, H, R, W, split), pltpu.SemaphoreType.DMA((Z,))]


def accumulate(dst, srcs, rows):
    def action():
        def body(i, carry):
            at = pl.ds(pl.multiple_of(i * 16, 16), 16)
            total = dst.at[at][...].astype(F32)
            for src in srcs:
                total = total + src.at[at][...].astype(F32)
            dst.at[at][...] = total.astype(dst.dtype)
            return carry

        lax.fori_loop(0, rows // 16, body, 0)

    return action


ORDER = (3, 2, 1, 0)


class Sum:
    def __init__(self, pc, mail, script, cell, theirs, buffers, R, split=True, direct=False, ends=None):
        self.ends = ends
        self.pc, self.mail, self.script, self.cell, self.theirs = pc, mail, script, cell, theirs
        self.r0, self.r3, self.buffers, self.R, self.split, self.direct = buffers[0], buffers[1], buffers[2:], R, split, direct
        self.sib, self.one, self.two, self.zs = {}, {}, {}, {}

    def send(self, src, dst, dev):
        copy = self.mail.copy(src, dst, dev)
        self.script.do(copy.start)
        return copy

    def pieces(self):
        R = self.R
        for j, (axis, part) in enumerate(scatter_parts(self.split)):
            rows, size = (pl.ds(0, R), R) if part is None else (pl.ds(part * (R // 2), R // 2), R // 2)
            yield j, axis, rows, size, self.buffers[2 * j], self.buffers[2 * j + 1]

    def across(self, dz):
        self.sib[dz] = self.send(self.theirs(dz), self.r0.at[dz], self.pc.dev(dc=1))

    def cores(self, dz):
        pc, whole = self.pc, pl.ds(0, self.R)
        self.script.do(self.sib[dz].wait_recv)
        for yy in range(pc.Y):
            for xx in range(pc.X):
                self.script.do(accumulate(self.cell(dz, yy, xx, whole), [self.r0.at[dz, yy, xx]], self.R))
        for j, axis, rows, size, r1, r2 in self.pieces():
            for k in range(1, pc.Y if axis == "y" else pc.X):
                if axis == "y":
                    src, dev = self.cell(dz, pc.at(dy=k)[1], slice(None), rows), pc.dev(dy=k)
                else:
                    src, dev = self.cell(dz, slice(None), pc.at(dx=k)[2], rows), pc.dev(dx=k)
                self.one[dz, j, k] = self.send(src, r1.at[dz, k - 1], dev)

    def firsts(self, dz):
        pc = self.pc
        for j, axis, rows, size, r1, r2 in self.pieces():
            steps = range(1, pc.Y if axis == "y" else pc.X)
            for k in steps:
                self.script.do(self.one[dz, j, k].wait_recv)
            for m in range(pc.X if axis == "y" else pc.Y):
                dst = self.cell(dz, pc.y, m, rows) if axis == "y" else self.cell(dz, m, pc.x, rows)
                self.script.do(accumulate(dst, [r1.at[dz, k - 1, m] for k in steps], size))
            for k in range(1, pc.X if axis == "y" else pc.Y):
                if axis == "y":
                    src, dev = self.cell(dz, pc.y, pc.at(dx=k)[2], rows), pc.dev(dx=k)
                else:
                    src, dev = self.cell(dz, pc.at(dy=k)[1], pc.x, rows), pc.dev(dy=k)
                self.two[dz, j, k] = self.send(src, r2.at[dz, k - 1], dev)

    def seconds(self, dz):
        pc = self.pc
        for j, axis, rows, size, r1, r2 in self.pieces():
            steps = range(1, pc.X if axis == "y" else pc.Y)
            for k in steps:
                self.script.do(self.two[dz, j, k].wait_recv)
            mine = self.cell(dz, pc.y, pc.x, rows)
            self.script.do(accumulate(mine, [r2.at[dz, k - 1] for k in steps], size))
        mine = self.cell(dz, pc.y, pc.x, pl.ds(0, self.R))
        if self.ends is not None:
            self.homeward(dz, mine)
            return
        if self.direct:
            if dz:
                self.zs[dz] = self.send(mine, self.r3.at[dz - 1], pc.dev(dz=dz))
            return
        if dz == 2:
            self.script.do(self.zs[3].wait_recv)
            self.script.do(accumulate(mine, [self.r3.at[0]], self.R))
        if dz:
            self.zs[dz] = self.send(mine, self.r3.at[3 - dz], pc.dev(dz=2 if dz == 2 else 1))

    def homeward(self, plane, mine):
        pc, (zsend, zrecv) = self.pc, self.ends
        at = (pc.z - plane + 3) % 4
        copy = pltpu.make_async_remote_copy(
            src_ref=mine, dst_ref=self.r3.at[at], send_sem=zsend.at[plane], recv_sem=zrecv.at[at],
            device_id=(plane * pc.Y + pc.y, pc.x * 2 + pc.c), device_id_type=MESH,
        )
        self.zs[plane] = copy

        def start():
            @pl.when(pc.z != plane)
            def _():
                copy.start()

        self.script.do(start)

    def home(self, total):
        pc, (zsend, zrecv) = self.pc, self.ends
        mine = self.cell(pc.z, pc.y, pc.x, pl.ds(0, self.R))
        copies = [
            pltpu.make_async_remote_copy(
                src_ref=mine, dst_ref=self.r3.at[k], send_sem=zsend.at[0], recv_sem=zrecv.at[k],
                device_id=pc.dev(dz=1), device_id_type=MESH,
            )
            for k in range(3)
        ]

        def body(i, carry):
            at = pl.ds(pl.multiple_of(i * 16, 16), 16)
            value = mine.at[at][...].astype(F32)
            for k in range(3):
                value = value + self.r3.at[k, at][...].astype(F32)
            total.at[at][...] = value
            return carry

        def sent():
            for plane in range(4):

                @pl.when(pc.z != plane)
                def _():
                    self.zs[plane].wait_send()

        for copy in copies:
            self.script.do(copy.wait_recv)
        self.script.do(lambda: lax.fori_loop(0, self.R // 16, body, 0))
        self.script.do(sent)

    def last(self, total):
        ends = (1, 2, 3) if self.direct else (2, 1)
        slots = (0, 1, 2) if self.direct else (1, 2)
        for dz in ends:
            self.script.do(self.zs[dz].wait_recv)
        pc, mine = self.pc, self.cell(0, self.pc.y, self.pc.x, pl.ds(0, self.R))

        def body(i, carry):
            at = pl.ds(pl.multiple_of(i * 16, 16), 16)
            value = mine.at[at][...].astype(F32)
            for k in slots:
                value = value + self.r3.at[k, at][...].astype(F32)
            total.at[at][...] = value
            return carry

        self.script.do(lambda: lax.fori_loop(0, self.R // 16, body, 0))


def scatter(pc, mail, jobs):
    script = Script()
    own, sums = {}, []

    def make(p_ref, t0, scratch, split):
        return Sum(
            pc, mail, script, lambda dz, yy, xx, rows: t0.at[dz, yy, xx, rows],
            lambda dz: p_ref.at[pc.at(dz=dz)[0], :, :, 1 - pc.c], scratch[1:-1], p_ref.shape[4], split,
        )

    for p_ref, total, scratch, split in jobs:
        sums.append(make(p_ref, scratch[0], scratch, split))
    script.stage()
    for o, (p_ref, total, scratch, split) in enumerate(jobs):
        for dz in ORDER:
            own[o, dz] = pltpu.make_async_copy(
                p_ref.at[pc.at(dz=dz)[0], :, :, pc.c], scratch[0].at[dz], scratch[-1].at[dz]
            )
            script.do(own[o, dz].start)
    script.stage()
    for dz in ORDER:
        for each in sums:
            each.across(dz)

    def cores(dz):
        for o, each in enumerate(sums):
            script.do(own[o, dz].wait)
            each.cores(dz)

    script.stage()
    cores(3)
    cores(2)
    script.stage()
    cores(1)
    cores(0)
    script.stage()
    for dz in ORDER:
        if dz < 3:
            script.stage()
        for each in sums:
            each.firsts(dz)
        if dz < 3:
            for each in sums:
                each.seconds(dz + 1)
    script.stage()
    for each, (p_ref, total, scratch, split) in zip(sums, jobs):
        each.seconds(0)
        each.last(total)
    return script


ANY = pl.BlockSpec(memory_space=pl.ANY)
VMEM = pl.BlockSpec(memory_space=pltpu.VMEM)


def sems(count):
    return [pltpu.SemaphoreType.DMA((count,)), pltpu.SemaphoreType.DMA((count,))]


def talking(cid):
    return pltpu.CompilerParams(collective_id=cid, has_side_effects=True, vmem_limit_bytes=60 * 1024 * 1024)


def blocks(part, S, H):
    X, Y, Z = sizes(S, H)
    return part.reshape(Z, Y, X, 2, part.shape[0] // (S * H), part.shape[1])


def first_kernel(S, H, in_ref, gain_ref, named_ref, out_ref, rows, send, recv, own_sem):
    pc = Place(S, H)
    D = in_ref.shape[1]
    values = in_ref[...]
    rows[:, :D] = (values * inverse_rms(values) * gain_ref[...]).astype(B16)
    rows[:, D:] = named_ref[...]
    mail = Mail(send, recv)
    moves = gather(pc, mail, rows, out_ref, own_sem)
    greet(pc.peers())
    moves.run()
    mail.finish(gather_count(S, H))


def first_rows(hidden_in, gain, named, S, H):
    R, D = hidden_in.shape
    W = D + LANES
    return pl.pallas_call(
        functools.partial(first_kernel, S, H),
        out_shape=jax.ShapeDtypeStruct((S * H * R, W), B16),
        in_specs=[VMEM] * 3,
        out_specs=ANY,
        scratch_shapes=[pltpu.VMEM((R, W), B16), *sems(gather_count(S, H)), pltpu.SemaphoreType.DMA],
        compiler_params=talking(1),
    )(hidden_in, gain, named)


def seg_of(pos, ends_ref, count):
    found = jnp.zeros(pos.shape, jnp.int32)
    for k in range(count):
        found = found + (pos >= ends_ref[k]).astype(jnp.int32)
    return jnp.where(pos < 0, -1, found)


def exact(left, right):
    return jnp.dot(left, right, precision=lax.Precision.HIGHEST, preferred_element_type=F32)


def silu(values):
    return values / (1.0 + jnp.exp(-values))


def softplus(values):
    return jnp.maximum(values, 0.0) + jnp.log1p(jnp.exp(-jnp.abs(values)))


class Block:
    def __init__(self, i, pre, ext, z, taps_ref, rows_ref, ends_ref, count, state, C):
        n = BLOCK
        pos = i * n + lax.broadcasted_iota(jnp.int32, (n, 1), 0)
        pos_row = i * n + lax.broadcasted_iota(jnp.int32, (1, n), 1)
        seg, seg_row = seg_of(pos, ends_ref, count), seg_of(pos_row, ends_ref, count)
        self.joined = {k: ((pos >= k) & (seg_of(pos - k, ends_ref, count) == seg)).astype(F32) for k in (1, 2, 3)}
        self.later = {k: (seg_of(pos + k, ends_ref, count) == seg).astype(F32) for k in (1, 2, 3)}
        conv = taps_ref[3:4, :] * pre
        for k in (1, 2, 3):
            conv = conv + taps_ref[3 - k : 4 - k, :] * ext[8 - k : 8 - k + n, :] * self.joined[k]
        act = silu(conv)
        cp = act.shape[1] - 2 * state
        self.conv = conv
        self.x, self.b, self.c = act[:, :cp], act[:, cp : cp + state].astype(B16), act[:, cp + state :].astype(B16)
        self.m = [rows_ref[j : j + 1, :] for j in range(2)]
        self.skip, self.gain = rows_ref[2:3, :], rows_ref[3:4, :]
        self.C = C
        self.dtr = z + rows_ref[4:5, :]
        self.dt = softplus(self.dtr)
        self.decay = rows_ref[5:6, :]
        self.rate = -self.dt * self.decay
        row, col = lax.broadcasted_iota(jnp.int32, (n, n), 0), lax.broadcasted_iota(jnp.int32, (n, n), 1)
        lower = row >= col
        self.row, self.col = row, col
        logdec = exact(lower.astype(F32), self.rate)
        log_row = logdec.T
        linked = lower & (seg == seg_row)
        self.decays = [
            jnp.exp(jnp.where(linked, logdec[:, C + j : C + j + 1] - log_row[C + j : C + j + 1, :], -1e30)) for j in range(2)
        ]
        scores = mm(self.c, self.b, NT)
        self.mats = [(scores * d).astype(B16) for d in self.decays]
        before = jnp.where(i == 0, -1, seg_of(jnp.full((1, 1), i * n - 1, jnp.int32), ends_ref, count))
        final = seg_of(jnp.full((1, 1), i * n + n - 1, jnp.int32), ends_ref, count)
        last = logdec[n - 1 : n, :]
        self.carry = self.spread(jnp.where(seg == before, jnp.exp(logdec), 0.0))
        self.tail = self.spread(jnp.where(seg == final, jnp.exp(last - logdec), 0.0))
        self.keep = self.spread(jnp.where(final == before, jnp.exp(last), 0.0))
        self.dtc = self.spread(self.dt)
        self.xt = (self.dtc * self.x).astype(B16)
        self.low = [m.astype(B16) for m in self.m]
        self.xts = [self.xt * low for low in self.low]
        self.tail_xt = (self.tail * self.xt.astype(F32)).astype(B16)

    def spread(self, values):
        return values[:, self.C : self.C + 1] * self.m[0] + values[:, self.C + 1 : self.C + 2] * self.m[1]

    def inner(self):
        return mm(self.mats[0], self.xts[0]) + mm(self.mats[1], self.xts[1])


def mixer_forward_kernel(
    S, H, count, state, C, ends_ref, in_ref, w_ref, taps_ref, rows_ref, out_w_ref, grad_ref,
    pre_ref, z_ref, y_ref, st_ref, part_ref, all_ref, held, ext, send, recv, own_sem,
):
    i = pl.program_id(0)
    pc = Place(S, H)
    mail = Mail(send, recv)
    moves = gather(pc, mail, grad_ref, all_ref, own_sem)
    ready = pl.num_programs(0) - 1

    @pl.when(i == 0)
    def _():
        greet(pc.peers())
        moves.run(0, 1)

    for step, stage, until in ((1, 1, 2), (2, 2, 3), (3, 3, 5), (4, 5, 7), (5, 7, 9), (6, 9, 11)):

        @pl.when(i == step)
        def _():
            moves.run(stage, until)

    depth = w_ref.shape[0]
    n, cp = BLOCK, z_ref.shape[1]

    @pl.when(i == 0)
    def _():
        held[...] = jnp.zeros_like(held)
        ext[0:8, :] = jnp.zeros((8, ext.shape[1]), F32)

    made = mm(in_ref[:, :depth], w_ref[...])
    z = made[:, :cp]
    pre = made[:, cp:]
    z_ref[...], pre_ref[...] = z, pre
    ext[8 : 8 + n, :] = pre
    blk = Block(i, pre, ext, z, taps_ref, rows_ref, ends_ref, count, state, C)
    ext[0:8, :] = pre[n - 8 :, :]
    st = held[...]
    st_ref[0] = st
    y = blk.inner() + blk.carry * mm(blk.c, st.astype(B16))
    held[...] = blk.keep * st + mm(blk.b, blk.tail_xt, TN)
    y = y + blk.skip * blk.x
    y_ref[...] = y
    gated = y * silu(z)
    part_ref[:, :depth] = mm((gated * blk.gain).astype(B16), out_w_ref[...]).astype(B16)
    high, rest = hi_lo(jnp.sum(gated * gated, axis=1, keepdims=True))
    lane = lax.broadcasted_iota(jnp.int32, (n, LANES), 1)
    part_ref[:, depth:] = jnp.where(lane == 0, high.astype(F32), jnp.where(lane == 1, rest.astype(F32), 0.0)).astype(B16)

    @pl.when(i == ready)
    def _():
        moves.run(11)
        mail.finish(gather_count(S, H))


def whole(shape):
    return pl.BlockSpec(shape, lambda i: (0,) * len(shape))


def params():
    return pltpu.CompilerParams(dimension_semantics=("arbitrary",), vmem_limit_bytes=60 * 1024 * 1024)


def mixer_forward(ends, gathered, in_w, taps, rows, out_w, grad, state, C, S, H):
    T, depth = gathered.shape[0], in_w.shape[0]
    cp, nb = out_w.shape[0], gathered.shape[0] // BLOCK
    conv_width = cp + 2 * state

    def block(width):
        return pl.BlockSpec((BLOCK, width), lambda i: (i, 0))

    return pl.pallas_call(
        functools.partial(mixer_forward_kernel, S, H, ends.shape[0], state, C),
        grid=(nb,),
        in_specs=[
            pl.BlockSpec(memory_space=pltpu.SMEM), block(gathered.shape[1]), whole(in_w.shape), whole(taps.shape),
            whole(rows.shape), whole(out_w.shape), VMEM,
        ],
        out_specs=[
            block(conv_width), block(cp), block(cp),
            pl.BlockSpec((1, state, cp), lambda i: (i, 0, 0)), block(depth + LANES), ANY,
        ],
        out_shape=[
            jax.ShapeDtypeStruct((T, conv_width), F32),
            jax.ShapeDtypeStruct((T, cp), F32),
            jax.ShapeDtypeStruct((T, cp), F32),
            jax.ShapeDtypeStruct((nb, state, cp), F32),
            jax.ShapeDtypeStruct((T, depth + LANES), B16),
            jax.ShapeDtypeStruct((T, depth), B16),
        ],
        scratch_shapes=[
            pltpu.VMEM((state, cp), F32), pltpu.VMEM((BLOCK + 8, conv_width), F32), *sems(gather_count(S, H)),
            pltpu.SemaphoreType.DMA,
        ],
        compiler_params=talking(5),
    )(ends, gathered, in_w, taps, rows, out_w, grad)


def mixer_backward_kernel(
    S, H, beside, count, state, C, ends_ref, three_ref, one_ref, pre_ref, halo_ref, z_ref, y_ref, st_ref,
    w_ref, taps_ref, rows_ref, cols_ref, out_w_ref, p_ref, sh_ref, res_ref, gres_ref, in_ref, gain_ref, norm2_ref, router_ref,
    sh_out, output_ref, gin_ref, extra_ref, small_out, zx_out, wo_out,
    held, ext, gext, gw_ref, gout_ref, gtaps_ref, gvec_ref, gnorm_ref, total, parts, extra, zx_ref, wo_ref, small, joint,
    *rest,
):
    step = pl.program_id(0)
    i = pl.num_programs(0) - 1 - step
    depth = w_ref.shape[0]
    n, cp = BLOCK, z_ref.shape[1]

    n1, n2 = 8 if beside else 0, 6
    scratch, main, side = rest[:n1], rest[n1 : n1 + n2], rest[n1 + n2 : n1 + n2 + 4]
    send, recv, sh_send, sh_recv, send2, recv2, zsend, zrecv, group_send, group_recv, sh_sem, local_sem = rest[n1 + n2 + 4 :]
    pc = Place(S, H)
    X, Y, Z = pc.X, pc.Y, pc.Z
    N, me, R = S * H, pc.slot(), res_ref.shape[0]
    seq, head = lax.axis_index("seq"), lax.axis_index("head")
    mail = Mail(send, recv)
    sums = scatter(pc, mail, [(p_ref, total, scratch, True)]) if beside else Script([[] for _ in range(9)])

    mail2 = Mail(send2, recv2)
    acts = Script()
    ones = Sum(
        pc, mail2, acts, lambda dz, yy, xx, rows: parts.at[dz, yy, xx, pc.c, rows], lambda dz: parts.at[dz, :, :, 1 - pc.c],
        main, R, ends=(zsend, zrecv),
    )
    for dz in range(Z):
        acts.stage()
        ones.across(dz)
        acts.stage()
        ones.cores(dz)
        acts.stage()
        ones.firsts(dz)
        acts.stage()
        ones.seconds(dz)
    acts.stage()
    ones.home(total)
    tall = extra.shape[4]
    sides = Script()
    other = Sum(
        pc, mail2, sides, lambda dz, yy, xx, rows: extra.at[pc.at(dz=dz)[0], yy, xx, pc.c, rows],
        lambda dz: extra.at[pc.at(dz=dz)[0], :, :, 1 - pc.c],
        side, tall, split=False, direct=True,
    )
    sides.stage()
    for dz in ORDER:
        other.across(dz)
    sides.stage()
    for dz in ORDER:
        other.cores(dz)
    sides.stage()
    for dz in ORDER:
        other.firsts(dz)
    sides.stage()
    for dz in ORDER:
        other.seconds(dz)
    other.last(extra_ref)
    group, keep_here, column, row = [], [], [], []
    for j, (src, dst) in enumerate(((zx_ref, zx_out), (wo_ref, wo_out))):
        keep_here.append(pltpu.make_async_copy(src.at[seq], dst.at[seq], local_sem.at[j]))
        for m in range(1, S):
            to = (seq + m) % S
            group.append(
                pltpu.make_async_remote_copy(
                    src_ref=src.at[to], dst_ref=dst.at[seq], send_sem=group_send.at[j, m],
                    recv_sem=group_recv.at[j, m], device_id=(to, head), device_id_type=MESH,
                )
            )
    for m in range(1, S):
        column.append(
            pltpu.make_async_remote_copy(
                src_ref=small.at[seq], dst_ref=small.at[seq], send_sem=group_send.at[2, m], recv_sem=group_recv.at[2, m],
                device_id=((seq + m) % S, head), device_id_type=MESH,
            )
        )
    for m in range(1, H):
        row.append(
            pltpu.make_async_remote_copy(
                src_ref=joint, dst_ref=small_out.at[head], send_sem=group_send.at[3, m], recv_sem=group_recv.at[3, m],
                device_id=(seq, (head + m) % H), device_id_type=MESH,
            )
        )
    keep_joint = pltpu.make_async_copy(joint, small_out.at[head], local_sem.at[2])
    total_steps = Y * Z
    before = {k: [] for k in range(total_steps)}
    for k, stage in ((2, 2), (3, 3), (4, 4), (5, 5), (6, 6), (7, 7)):
        before[k].append((sums, stage))
    final_acts = []
    for dz in (3, 2, 1, 0):
        for late, stage in ((0, 0), (1, 1), (3, 2), (4, 3)):
            k = (Z - dz) * Y + late
            if k < total_steps:
                before[k].append((acts, 4 * dz + stage))
    final_acts = [(acts, 4 * dz + stage) for dz, stage in ((0, 0), (3, 3), (2, 2), (2, 3), (1, 1), (1, 2), (0, 1), (1, 3), (0, 2), (0, 3))]
    final_acts = [entry for entry in final_acts if all(entry not in before[k] for k in before)]
    stay = pltpu.make_async_copy(sh_ref.at[me], sh_out.at[me], sh_sem)

    def to_all(function, first, last):
        def body(m, carry):
            to = (me + m) % N
            function(
                pltpu.make_async_remote_copy(
                    src_ref=sh_ref.at[to], dst_ref=sh_out.at[me], send_sem=sh_send.at[m], recv_sem=sh_recv.at[m],
                    device_id=(to // H, to % H), device_id_type=MESH,
                )
            )
            return carry

        lax.fori_loop(first, last, body, 0)

    @pl.when(step == 0)
    def _():
        sums.run(0, 1)
        stay.start()
        barrier = pltpu.get_barrier_semaphore()

        def hello(m, carry):
            to = (me + m) % N
            pl.semaphore_signal(barrier, inc=1, device_id=(to // H, to % H), device_id_type=MESH)
            return carry

        lax.fori_loop(1, N, hello, 0)
        pl.semaphore_wait(barrier, N - 1)
        sums.run(1, 2)

    for at in range(1, total_steps):
        if before[at]:

            @pl.when(step == at)
            def _():
                for script, stage in before[at]:
                    script.run(stage, stage + 1)

    @pl.when(step == 1)
    def _():
        to_all(lambda copy: copy.start(), 1, N)

    @pl.when(step == 0)
    def _():
        gnorm_ref[...] = jnp.zeros_like(gnorm_ref)
        held[...] = jnp.zeros_like(held)
        gext[n : n + 8, :] = jnp.zeros((8, gext.shape[1]), F32)
        gw_ref[...] = jnp.zeros_like(gw_ref)
        extra[...] = jnp.zeros_like(extra)
        zx_ref[...] = jnp.zeros_like(zx_ref)
        wo_ref[...] = jnp.zeros_like(wo_ref)
        gout_ref[...] = jnp.zeros_like(gout_ref)
        gtaps_ref[...] = jnp.zeros_like(gtaps_ref)
        gvec_ref[...] = jnp.zeros_like(gvec_ref)

    pre, z, y = pre_ref[...], z_ref[...], y_ref[...]
    ext[0:8, :] = jnp.where(i == 0, 0.0, halo_ref[...])
    ext[8 : 8 + n, :] = pre
    blk = Block(i, pre, ext, z, taps_ref, rows_ref, ends_ref, count, state, C)
    three = three_ref[:, :depth]
    pg = mm(three, out_w_ref[...], NT)
    cross = jnp.sum(three_ref[:, depth:].astype(F32), axis=1, keepdims=True)
    act_z = silu(z)
    gated = y * act_z
    gout_ref[...] += mm((gated * blk.gain).astype(B16), three, TN)
    grad_gated = pg * blk.gain - gated * cross
    gy = grad_gated * act_z
    gz = grad_gated * y * silu_grad(z)
    st = st_ref[0]
    st_low, grad = st.astype(B16), held[...]
    grad_low = grad.astype(B16)
    gy_low = gy.astype(B16)
    y_all = blk.inner() + blk.carry * mm(blk.c, st_low)
    back = sum(mm(blk.mats[j], gy_low * blk.low[j], TN) for j in range(2))
    gate = (blk.carry * gy_low.astype(F32)).astype(B16)
    tail_back = blk.tail * mm(blk.b, grad_low)
    pull = sum(mm(gy_low, blk.xts[j], NT) * blk.decays[j] for j in range(2)).astype(B16)
    g_c = mm(pull, blk.b) + mm(gate, st_low, NT)
    g_b = mm(pull, blk.c, TN) + mm(blk.tail_xt, grad_low, NT)
    held[...] = blk.keep * grad + mm(blk.c, gate, TN)
    g_xt = back + tail_back
    xt = blk.xt.astype(F32)
    cols = cols_ref[...]
    after = exact(gy_low.astype(F32) * y_all - xt * back, cols)
    used = exact(xt * tail_back, cols)
    through = exact(jnp.broadcast_to(blk.keep * jnp.sum(grad * st, axis=0, keepdims=True), (8, cp)), cols)[0:1, :]
    g_rate = (
        exact((blk.row <= blk.col).astype(F32), after) + exact((blk.row > blk.col).astype(F32), used) + through
    )
    g_dt = exact(g_xt * blk.x, cols) - g_rate * blk.decay
    g_dtr = g_dt / (1.0 + jnp.exp(-blk.dtr))
    g_x = g_xt * blk.dtc + blk.skip * gy
    for r, v in enumerate((pg * gated, g_dtr, g_rate * blk.rate, gy * blk.x)):
        gvec_ref[r : r + 1, :] += jnp.sum(v, axis=0, keepdims=True)
    gconv = jnp.concatenate([g_x, g_b, g_c], axis=1) * silu_grad(blk.conv)
    gext[0:n, :] = gconv
    gpre = taps_ref[3:4, :] * gconv
    gtaps_ref[3:4, :] += jnp.sum(gconv * pre, axis=0, keepdims=True)
    for k in (1, 2, 3):
        gpre = gpre + taps_ref[3 - k : 4 - k, :] * gext[k : n + k, :] * blk.later[k]
        gtaps_ref[3 - k : 4 - k, :] += jnp.sum(gconv * ext[8 - k : 8 - k + n, :] * blk.joined[k], axis=0, keepdims=True)
    gext[n : n + 8, :] = gconv[0:8, :]
    made = jnp.concatenate([gz + g_dtr, gpre], axis=1).astype(B16)
    one = one_ref[:, :depth]
    part = mm(made, w_ref[...], NT)
    part_low = part.astype(B16)
    for xx in range(X):
        for cc in range(2):
            at = slice((xx * 2 + cc) * R, (xx * 2 + cc + 1) * R)
            parts[i // Y, i % Y, xx, cc] = part_low[at]
    gnorm_ref[...] += jnp.sum(part * one.astype(F32), axis=0, keepdims=True)
    gw_ref[...] += mm(made, one, TN)

    @pl.when(i == 0)
    def _():
        acts.run(0, 1)
        line = 0
        for ref in (gnorm_ref, norm2_ref):
            for j in range(depth // LANES):
                small[seq, line : line + 1, :] = ref[0:1, j * LANES : (j + 1) * LANES]
                line += 1
        for r in range(4):
            for j in range(2 * state // LANES):
                small[seq, line : line + 1, :] = gtaps_ref[r : r + 1, cp + j * LANES : cp + (j + 1) * LANES]
                line += 1
        small[seq, line : line + 4, :] = gtaps_ref[0:4, :cp]
        small[seq, line + 4 : line + 7, :] = gvec_ref[0:3, :]
        small[seq, line + 7 : line + 8, :] = exact(gvec_ref[...], cols)[3:4, :]
        for copy in column:
            copy.start()
        wide = depth // S
        cut = zx_ref.shape[1]
        for t in range(S):
            at = slice(t * wide, (t + 1) * wide)
            zx_ref[t, :, :wide] = gw_ref[:cut, at].astype(B16)
            zx_ref[t, :, wide:] = gw_ref[cp : cp + cut, at].astype(B16)
            wo_ref[t] = gout_ref[: wo_ref.shape[1], at].astype(B16)
        for copy in keep_here + group:
            copy.start()
        for script, stage in final_acts[1:5]:
            script.run(stage, stage + 1)
        per = depth // N
        bc = gw_ref[2 * cp :, :].T
        router = router_ref[...].astype(F32)
        for t in range(N):
            at = slice(t * per, (t + 1) * per)
            where = (t // (Y * X * 2), t // (X * 2) % Y, t // 2 % X, t % 2)
            extra[(*where, slice(0, per), slice(0, 2 * state))] = bc[at].astype(B16)
            extra[(*where, slice(0, per), slice(2 * state, 2 * state + LANES))] = router[at].astype(B16)
        sides.run(0, 1)
        for script, stage in final_acts[5:7]:
            script.run(stage, stage + 1)
        sides.run(1, 2)
        for copy in column:
            copy.wait_recv()
        joint[0:line, :] = functools.reduce(jnp.add, [small[t, 0:line, :] for t in range(S)])
        for t in range(S):
            joint[line + 8 * t : line + 8 * t + 8, :] = small[t, line : line + 8, :]
        keep_joint.start()
        for copy in row:
            copy.start()
        for script, stage in final_acts[7:]:
            script.run(stage, stage + 1)
        sides.run(2, 3)
        sums.run(8)
        output_ref[...] = res_ref[...] + total[...] if beside else res_ref[...]
        sides.run(3)
        acts.run(4 * Z)
        values, gone = in_ref[...], total[...]
        gin_ref[...] = gres_ref[...] + rms_back(values, inverse_rms(values), gain_ref[...], gone)
        for copy in row:
            copy.wait()
        for copy in column:
            copy.wait_send()
        keep_joint.wait()
        to_all(lambda copy: copy.wait(), 1, N)
        for copy in keep_here + group:
            copy.wait()
        stay.wait()
        mail.finish(scatter_count(S, H) if beside else 0)
        mail2.finish(scatter_count(S, H) - 3 + scatter_count(S, H, (False,)))


def mixer_backward(
    ends, three, one, pre, z, y, states, in_w, taps, rows, cols, out_w, out_part, shared, residual, grad_res, hidden_in, gain,
    norm2, router_part, state, C, S, H,
):
    T, depth = three.shape[0], in_w.shape[0]
    cp, nb = out_w.shape[0], T // BLOCK
    conv_width = cp + 2 * state
    R, N = residual.shape[0], S * H
    X, Y, Z = sizes(S, H)
    line = 2 * (depth // LANES) + 4 * (2 * state // LANES)
    tall = -(-(depth // N) // 16) * 16
    zx_rows = -(-(C + 2) // 16) * 16
    beside = Y == 2
    wo_rows = -(-C // 16) * 16
    assert line % 8 == 0 and cp == LANES and R * H == BLOCK
    sent = scatter_count(S, H) - 3 + scatter_count(S, H, (False,))

    def block(width, kept=2):
        return pl.BlockSpec((BLOCK, width), lambda k: (nb - 1 - k, 0), pipeline_mode=pl.Buffered(kept))

    kept = 2 if beside else 1

    def halo(k):
        return (jnp.maximum((nb - 1 - k) * (BLOCK // 8) - 1, 0), 0)

    return pl.pallas_call(
        functools.partial(mixer_backward_kernel, S, H, beside, ends.shape[0], state, C),
        grid=(nb,),
        in_specs=[
            pl.BlockSpec(memory_space=pltpu.SMEM), block(three.shape[1]), block(one.shape[1], kept), block(conv_width, kept),
            pl.BlockSpec((8, conv_width), halo), block(cp), block(cp),
            pl.BlockSpec((1, state, cp), lambda k: (nb - 1 - k, 0, 0)),
            VMEM, VMEM, VMEM, VMEM, VMEM, ANY, ANY, VMEM, VMEM, VMEM, VMEM, VMEM, VMEM,
        ],
        out_specs=[ANY, VMEM, VMEM, VMEM, ANY, ANY, ANY],
        out_shape=[
            jax.ShapeDtypeStruct(shared.shape, shared.dtype),
            jax.ShapeDtypeStruct((R, depth), F32),
            jax.ShapeDtypeStruct((R, depth), F32),
            jax.ShapeDtypeStruct((tall, 2 * state + LANES), F32),
            jax.ShapeDtypeStruct((H, line + 8 * S, LANES), F32),
            jax.ShapeDtypeStruct((S, zx_rows, 2 * (depth // S)), B16),
            jax.ShapeDtypeStruct((S, wo_rows, depth // S), B16),
        ],
        scratch_shapes=[
            pltpu.VMEM((state, cp), F32),
            pltpu.VMEM((BLOCK + 8, conv_width), F32),
            pltpu.VMEM((BLOCK + 8, conv_width), F32),
            pltpu.VMEM((in_w.shape[1], depth), F32),
            pltpu.VMEM(out_w.shape, F32),
            pltpu.VMEM((8, conv_width), F32),
            pltpu.VMEM((8, cp), F32),
            pltpu.VMEM((1, depth), F32),
            pltpu.VMEM((R, depth), F32),
            pltpu.VMEM((Z, Y, X, 2, R, depth), B16),
            pltpu.VMEM((Z, Y, X, 2, tall, 2 * state + LANES), B16),
            pltpu.VMEM((S, zx_rows, 2 * (depth // S)), B16),
            pltpu.VMEM((S, wo_rows, depth // S), B16),
            pltpu.VMEM((S, line + 8, LANES), F32),
            pltpu.VMEM((line + 8 * S, LANES), F32),
            *(scatter_scratch(S, H, R, depth) if beside else []),
            *sum_scratch(S, H, R, depth),
            *sum_scratch(S, H, tall, 2 * state + LANES, False),
            *sems(scatter_count(S, H)),
            *sems(N),
            *sems(sent),
            pltpu.SemaphoreType.DMA((4,)), pltpu.SemaphoreType.DMA((3,)),
            pltpu.SemaphoreType.DMA((4, S)), pltpu.SemaphoreType.DMA((4, S)),
            pltpu.SemaphoreType.DMA, pltpu.SemaphoreType.DMA((3,)),
        ],
        compiler_params=talking(6),
    )(
        ends, three, one, pre, pre, z, y, states, in_w, taps, rows, cols, out_w, blocks(out_part, S, H), shared, residual,
        grad_res, hidden_in, gain, norm2, router_part,
    )


def expert_block(F, two, grad, named, mine, up_ref, down_ref, gup_ref, gdown_ref, gs_ref):
    mid = mm(two, up_ref[...])
    back = mm(grad, down_ref[...], NT)
    gate, lin = mid[:, :F], mid[:, F : 2 * F]
    s_gate, s_lin = mid[:, 2 * F : 2 * F + LANES], mid[:, 2 * F + LANES :]
    named = named.astype(F32) > 0
    logits = jnp.where(named, s_gate, -1e30)
    odds = jnp.where(named, jnp.exp(logits - jnp.max(logits, axis=1, keepdims=True)), 0.0)
    probs = odds / jnp.sum(odds, axis=1, keepdims=True)
    weight = jnp.sum(probs * mine, axis=1, keepdims=True)
    s_back, back = back[:, F:], back[:, :F]
    act_gate, act_s = silu(gate), silu(s_gate)
    acting = act_gate * lin
    gp = jnp.sum(acting * back, axis=1, keepdims=True)
    back = weight * back
    down_in = jnp.concatenate([weight * acting, act_s * s_lin], axis=1).astype(B16)
    mid_grad = jnp.concatenate(
        [back * lin * silu_grad(gate), back * act_gate, s_back * s_lin * silu_grad(s_gate), s_back * act_s], axis=1
    ).astype(B16)
    gup_ref[...] += mm(two, mid_grad[:, : 2 * F], TN)
    gdown_ref[...] += mm(down_in[:, :F], grad, TN)
    gs_ref[: 2 * LANES, :] += mm(mid_grad[:, 2 * F :], two, TN)
    gs_ref[2 * LANES :, :] += mm(down_in[:, F:], grad, TN)
    out = mm(down_in, down_ref[...]).astype(B16)
    part = mm(mid_grad, up_ref[...], NT).astype(B16)
    return out, part, (gp * mine).astype(B16), probs


def expert_kernel(
    S, H, F, width, p_ref, in_ref, gain_ref, grad_ref, named_ref, up_ref, down_ref, mine_ref, router_ref, ograd_ref,
    rows_ref, res_ref, gres_ref, gnorm_ref, grouter_ref, out_ref, gup_out, gdown_ref, gsh_ref,
    gup_ref, total, rows, two, grads, names, parts, stage_out, probs, gs_ref, *rest,
):
    buffers, (send1, recv1, send2, recv2, own_sem, load_sem, name_sem, grad_sem, out_sem) = rest[:-9], rest[-9:]
    pc = Place(S, H)
    X, Y, Z = pc.X, pc.Y, pc.Z
    R, D = in_ref.shape
    n = BLOCK
    mail1, mail2 = Mail(send1, recv1), Mail(send2, recv2)

    def cell(dz, yy, xx, rows):
        return parts.at[dz, yy, xx, pc.c, rows]

    sums = Script()
    first = Sum(
        pc, mail1, sums, cell, lambda dz: p_ref.at[pc.at(dz=dz)[0], :, :, 1 - pc.c], buffers, R
    )
    own = {
        dz: pltpu.make_async_copy(p_ref.at[pc.at(dz=dz)[0], :, :, pc.c], parts.at[dz, :, :, pc.c], load_sem.at[dz])
        for dz in ORDER
    }
    for copy in own.values():
        copy.start()
    sums.stage()
    for dz in ORDER:
        first.across(dz)
    for dz in ORDER:
        sums.do(own[dz].wait)
        first.cores(dz)
    for dz in ORDER:
        first.firsts(dz)
        if dz < 3:
            first.seconds(dz + 1)
    first.seconds(0)
    first.last(total)

    moves = gather(pc, mail2, rows, two, own_sem, planes=True)
    acts = Script()
    second = Sum(pc, mail2, acts, cell, lambda dz: parts.at[dz, :, :, 1 - pc.c], buffers, R, direct=True)
    for dz in range(Z):
        acts.stage()
        second.across(dz)
        acts.stage()
        second.cores(dz)
        acts.stage()
        second.firsts(dz)
        acts.stage()
        second.seconds(dz)
    acts.stage()
    second.last(total)

    def seq_of(k):
        return pc.partner(k // Y) * Y + k % Y

    def loads(k, slot):
        at = pl.ds(pl.multiple_of(seq_of(k) * n, n), n)
        return [
            pltpu.make_async_copy(grad_ref.at[at], grads.at[slot], grad_sem.at[slot]),
            pltpu.make_async_copy(named_ref.at[at, pl.ds(D, LANES)], names.at[slot], name_sem.at[slot]),
        ]

    def store(k, slot):
        at = pl.ds(pl.multiple_of(seq_of(k) * n, n), n)
        return pltpu.make_async_copy(stage_out.at[slot], out_ref.at[at], out_sem.at[slot])

    for copy in loads(0, 0):
        copy.start()
    gup_ref[...] = jnp.zeros_like(gup_ref)
    gdown_ref[...] = jnp.zeros_like(gdown_ref)
    gs_ref[...] = jnp.zeros_like(gs_ref)
    greet(pc.peers(direct=True))
    sums.run()
    gain = gain_ref[...]
    mixed = total[:, :D]
    square = jnp.sum(total[:, D:], axis=1, keepdims=True)
    inv = lax.rsqrt(square / width + EPS)
    residual = in_ref[...] + inv * mixed
    res_ref[...] = residual
    rows[...] = (residual * inverse_rms(residual) * gain).astype(B16)
    gres_ref[...] = mixed
    cube = inv * inv * inv / width
    moves.run(0, 5)
    for copy in mail1.made:
        copy.wait_send()
    moves.run(12, 13)

    count = Y * Z
    before = {k: [] for k in range(count)}
    after = []
    for dz in range(Z):
        for late, stage in ((0, 0), (1, 1), (3, 2), (4, 3)):
            k = (dz + 1) * Y + late
            before.get(k, after).append((acts, 4 * dz + stage))
    after = [(acts, 4 * dz + stage) for dz, stage in ((3, 0), (1, 2), (1, 3), (2, 2), (3, 1), (2, 3), (3, 2), (3, 3))]
    after = [entry for entry in after if all(entry not in before[k] for k in before)]
    for k, stage in (
        (0, 5), (1, 6), (1, 7), (Y, 8), (Y, 13), (Y + 1, 9), (Y + 1, 10), (2 * Y, 11), (2 * Y, 14), (3 * Y, 15),
    ):
        before[k].append((moves, stage))
    mine = mine_ref[...]

    def step(k, carry):
        for at in range(count):
            if before[at]:

                @pl.when(k == at)
                def _():
                    for script, stage in before[at]:
                        script.run(stage, stage + 1)

        slot = k % 2

        @pl.when(k + 1 < count)
        def _():
            for copy in loads(k + 1, 1 - slot):
                copy.start()

        for copy in loads(k, slot):
            copy.wait()
        block = two[pl.ds(pl.multiple_of(seq_of(k) * n, n), n), :]
        out, part, gp, chance = expert_block(
            F, block, grads[slot], names[slot], mine, up_ref, down_ref, gup_ref, gdown_ref, gs_ref
        )
        for xx in range(X):
            for cc in range(2):
                at = slice((xx * 2 + cc) * R, (xx * 2 + cc + 1) * R)
                parts[k // Y, k % Y, xx, cc, :, :D] = part[at]
                parts[k // Y, k % Y, xx, cc, :, D:] = gp[at]

        @pl.when(k == pc.y)
        def _():
            probs[...] = chance

        @pl.when(k >= 2)
        def _():
            store(k - 2, slot).wait()

        stage_out[slot] = out
        store(k, slot).start()
        return carry

    lax.fori_loop(0, count, step, 0)
    for script, stage in after[:1]:
        script.run(stage, stage + 1)
    for k in range(2):
        gup_out[0, :, k, :] = gup_ref[:, k * F : (k + 1) * F]
    for script, stage in after[1:]:
        script.run(stage, stage + 1)
    for k in range(3):
        gsh_ref[k] = gs_ref[k * LANES : k * LANES + gsh_ref.shape[1], :].astype(B16)
    head = lax.axis_index("head")
    p = probs[pl.ds(pl.multiple_of(head * R, R), R), :]
    acts.run(4 * Z)
    gp = total[:, D:]
    glogits = (p * (gp - jnp.sum(p * gp, axis=1, keepdims=True))).astype(B16)
    gtwo = total[:, :D] + mm(glogits, router_ref[...], NT)
    residual = res_ref[...]
    inv_two = inverse_rms(residual)
    mixed = gres_ref[...]
    gres = ograd_ref[...] + rms_back(residual, inv_two, gain, gtwo)
    cross = jnp.sum(gres * mixed, axis=1, keepdims=True) * cube
    high, low = hi_lo(cross)
    lane = lax.broadcasted_iota(jnp.int32, (R, LANES), 1)
    rows_ref[:, :D] = (inv * gres).astype(B16)
    rows_ref[:, D:] = jnp.where(lane == 0, high.astype(F32), jnp.where(lane == 1, low.astype(F32), 0.0)).astype(B16)
    gres_ref[...] = gres
    gnorm_ref[...] = jnp.sum(gtwo * residual * inv_two, axis=0, keepdims=True)
    grouter_ref[...] = mm((residual * inv_two * gain).astype(B16), glogits, TN).astype(B16)
    for k in (count - 2, count - 1):
        store(k, k % 2).wait()
    mail2.finish(gather_count(S, H) + scatter_count(S, H))


def experts(part, hidden_in, gain, all_grad, gathered, up_w, down_w, mine, router, out_grad, F, FS, width, S, H):
    R, D = hidden_in.shape
    X, Y, Z = sizes(S, H)
    T, W = S * H * R, D + LANES
    tall = -(-FS // 16) * 16
    assert R * H == BLOCK
    return pl.pallas_call(
        functools.partial(expert_kernel, S, H, F, width),
        out_shape=[
            jax.ShapeDtypeStruct((R, W), B16),
            jax.ShapeDtypeStruct((R, D), F32),
            jax.ShapeDtypeStruct((R, D), F32),
            jax.ShapeDtypeStruct((1, D), F32),
            jax.ShapeDtypeStruct((D, LANES), B16),
            jax.ShapeDtypeStruct((T, D), B16),
            jax.ShapeDtypeStruct((1, D, 2, F), F32),
            jax.ShapeDtypeStruct((F, D), F32),
            jax.ShapeDtypeStruct((3, tall, D), B16),
        ],
        in_specs=[ANY, VMEM, VMEM, ANY, ANY] + [VMEM] * 5,
        out_specs=[VMEM] * 5 + [ANY] + [VMEM] * 3,
        scratch_shapes=[
            pltpu.VMEM((D, 2 * F), F32), pltpu.VMEM((R, W), F32), pltpu.VMEM((R, D), B16), pltpu.VMEM((T, D), B16),
            pltpu.VMEM((2, BLOCK, D), B16), pltpu.VMEM((2, BLOCK, LANES), B16),
            pltpu.VMEM((Z, Y, X, 2, R, W), B16), pltpu.VMEM((2, BLOCK, D), B16), pltpu.VMEM((BLOCK, LANES), F32),
            pltpu.VMEM((3 * LANES, D), F32), *sum_scratch(S, H, R, W),
            *sems(scatter_count(S, H)), *sems(scatter_count(S, H) + gather_count(S, H)),
            pltpu.SemaphoreType.DMA, pltpu.SemaphoreType.DMA((Z,)), pltpu.SemaphoreType.DMA((2,)),
            pltpu.SemaphoreType.DMA((2,)), pltpu.SemaphoreType.DMA((2,)),
        ],
        compiler_params=talking(2),
    )(blocks(part, S, H), hidden_in, gain, all_grad, gathered, up_w, down_w, mine, router, out_grad)


def third_kernel(S, H, rows_ref, out_ref, send, recv, own_sem):
    pc = Place(S, H)
    mail = Mail(send, recv)
    moves = gather(pc, mail, rows_ref, out_ref, own_sem)
    greet(pc.peers())
    moves.run()
    mail.finish(gather_count(S, H))


def third_rows(rows, S, H):
    R, W = rows.shape
    return pl.pallas_call(
        functools.partial(third_kernel, S, H),
        out_shape=jax.ShapeDtypeStruct((S * H * R, W), B16),
        in_specs=[VMEM],
        out_specs=ANY,
        scratch_shapes=[*sems(gather_count(S, H)), pltpu.SemaphoreType.DMA],
        compiler_params=talking(3),
    )(rows)


def finish_kernel(
    S, H, C, FS, state, zx_ref, wo_ref, sh_ref, small_ref, pick_ref, gain_ref,
    zx_out, dt_out, wo_out, up_out, down_out, norm1_out, norm2_out, taps_out, bc_out, gate_out, heads_out,
):
    wide = wo_ref.shape[2]
    heads = dt_out.shape[1]
    dt = jnp.zeros(dt_out.shape, F32)
    for t in range(S):
        turned = zx_ref[t].astype(F32).T
        at = slice(t * C, (t + 1) * C)
        zx_out[:, 0, at] = turned[:wide, :C]
        zx_out[:, 1, at] = turned[wide:, :C]
        dt = dt + exact(turned[:wide, :], pick_ref[t, : turned.shape[1], :])
        wo_out[at, :] = wo_ref[t, :C, :].astype(F32)
    dt_out[...] = dt
    N, tall, per = sh_ref.shape[0], sh_ref.shape[1] // 3, sh_ref.shape[2]
    for k in range(2):
        rows = sh_ref[:, k * tall : (k + 1) * tall, :].astype(F32)[:, :FS, :]
        up_out[:, k, :] = rows.reshape(N * FS, per).T
    down_out[...] = sh_ref[:, 2 * tall :, :].astype(F32)[:, :FS, :].reshape(N * FS, per)
    lines = gain_ref.shape[1] // LANES
    total = small_ref[0, : 2 * lines + 4 * (2 * state // LANES), :]
    for h in range(1, H):
        total = total + small_ref[h, : total.shape[0], :]
    for j in range(lines):
        at = slice(j * LANES, (j + 1) * LANES)
        norm1_out[:, at] = total[j : j + 1, :] / gain_ref[:, at]
        norm2_out[:, at] = total[lines + j : lines + j + 1, :]
    line = 2 * lines
    for r in range(4):
        for j in range(2 * state // LANES):
            bc_out[r : r + 1, j * LANES : (j + 1) * LANES] = total[line : line + 1, :]
            line += 1
    for h in range(H):
        by_head = jnp.zeros((8, heads), F32)
        for t in range(S):
            ours = small_ref[h, line + 8 * t : line + 8 * t + 8, :]
            at = slice((h * S + t) * C, (h * S + t + 1) * C)
            taps_out[:, at] = ours[0:4, :C]
            gate_out[:, at] = ours[4:5, :C]
            by_head = by_head + exact(ours, pick_ref[t])
        for r in range(3):
            heads_out[r : r + 1, h * heads : (h + 1) * heads] = by_head[5 + r : 6 + r, :]


def finish(zx, wo, shared, small, pick, gain, C, FS, state, S, H):
    N, per, wide, heads, D = shared.shape[0], shared.shape[2], wo.shape[2], pick.shape[2], gain.shape[1]
    shapes = (
        (wide, 2, S * C), (wide, heads), (S * C, wide), (per, 2, N * FS), (N * FS, per), (1, D), (1, D), (4, S * H * C),
        (4, 2 * state), (1, S * H * C), (3, H * heads),
    )
    return pl.pallas_call(
        functools.partial(finish_kernel, S, H, C, FS, state),
        out_shape=[jax.ShapeDtypeStruct(shape, F32) for shape in shapes],
        in_specs=[VMEM] * 6,
        out_specs=[VMEM] * len(shapes),
        compiler_params=pltpu.CompilerParams(vmem_limit_bytes=56 * 1024 * 1024),
    )(zx, wo, shared, small, pick, gain)


def local(
    hidden_in, norm1_gain, w_zx, w_bc, w_dt, conv_x, conv_bc, dt_bias, a_log, d_skip, gate_gain,
    w_out, norm2_gain, router, expert_up, expert_down, shared_up, shared_down, out_grad,
    seq_lengths, routes,
):
    S, H = lax.axis_size("seq"), lax.axis_size("head")
    N = S * H
    s = lax.axis_index("seq")
    g = s * H + lax.axis_index("head")
    R, D = hidden_in.shape
    heads, inner = dt_bias.shape[0], conv_x.shape[1]
    size = inner // heads
    state = w_bc.shape[1] // 2
    width = inner * H
    C = inner // S
    CP = -(-(C + 2) // LANES) * LANES
    E = N // 2
    F = expert_down.shape[1]
    FS = shared_down.shape[0] // N
    per = D // N

    named = jnp.sum(
        (routes[:, :, None] == jnp.arange(E, dtype=jnp.int32)[None, None, :]).astype(F32), axis=1
    )
    named = jnp.pad(named.astype(B16), ((0, 0), (FS, LANES - FS - E)))
    gain1, gain2 = norm1_gain[None], norm2_gain[None]
    gathered = first_rows(hidden_in, gain1, named, S, H)

    firsts = [min(k * C // size, heads - 2) for k in range(S)]
    first = jnp.minimum(s * C // size, heads - 2)
    channel = jnp.arange(CP)
    masks = jnp.stack(
        [((channel < C) & ((s * C + channel) // size - first == j)).astype(F32) for j in range(2)]
    )

    def mine(values, axis, offset, length):
        return lax.dynamic_slice_in_dim(values, offset, length, axis)

    def channels(values, axis):
        cut = mine(values, axis, s * C, C)
        pads = [(0, 0)] * values.ndim
        pads[axis] = (0, CP - C)
        return jnp.pad(cut, pads)

    def in_free(values):
        return jnp.pad(values, [(0, 0)] * (values.ndim - 1) + [(C, CP - C - 2)])

    zx_w = mine(w_zx, 2, s * C, C)
    in_w = jnp.concatenate(
        [
            zx_w[:, 0], pad_lanes(mine(w_dt, 1, first, 2), CP - C), pad_lanes(zx_w[:, 1], CP), w_bc,
        ],
        axis=1,
    )
    taps = jnp.concatenate([channels(conv_x, 1), conv_bc], axis=1)
    bias, alog, skip = (mine(v, 0, first, 2) for v in (dt_bias, a_log, d_skip))
    gain = channels(gate_gain, 0)
    out_w = channels(w_out, 0)
    rows = jnp.concatenate(
        [masks, (skip @ masks)[None], gain[None], in_free(jnp.stack([bias, jnp.exp(alog)]))], axis=0
    )
    rows = jnp.pad(rows, ((0, 2), (0, 0)))
    cols = in_free(masks.T)
    ends = jnp.cumsum(seq_lengths)

    pre, z, y, states, part, all_grad = mixer_forward(
        ends, gathered, in_w, taps, rows, out_w, out_grad.astype(B16), state, C, S, H
    )

    sup = mine(shared_up, 2, g * FS, FS)
    router_w = jnp.pad(router, ((0, 0), (FS, LANES - FS - E)))
    up_w = jnp.concatenate(
        [
            expert_up[0].reshape(D, 2 * F), sup[:, 0], router_w[:, FS:], pad_lanes(sup[:, 1], LANES),
        ],
        axis=1,
    )
    down_w = jnp.concatenate([expert_down[0], mine(shared_down, 0, g * FS, FS), jnp.zeros((LANES - FS, D), B16)], axis=0)
    is_mine = (jnp.arange(LANES) == FS + g // 2).astype(F32)[None]
    rows_three, residual, grad_res, norm2_part, router_part, out_part, grad_up, grad_down, grad_shared = experts(
        part, hidden_in, gain2, all_grad, gathered, up_w, down_w, is_mine, router_w, out_grad, F, FS, width, S, H
    )
    three = third_rows(rows_three, S, H)

    tall_s = grad_shared.shape[1]
    shared = grad_shared.reshape(3 * tall_s, N, per).transpose(1, 0, 2)
    sh_in, output, grad_in, extra_sum, small, zx_in, wo_in = mixer_backward(
        ends, three, gathered, pre, z, y, states, in_w, taps, rows, cols, out_w, out_part, shared, residual,
        grad_res, hidden_in, gain1, norm2_part, router_part, state, C, S, H,
    )
    if H > 4:
        output = output + lax.psum_scatter(out_part, ("seq", "head"), scatter_dimension=0, tiled=True).astype(F32)
    grad_bc, grad_router = extra_sum[:per, : 2 * state], extra_sum[:per, 2 * state :][:, FS : FS + E]
    pick = jnp.asarray(
        [[[float(c >= C and firsts[k] + c - C == h) for h in range(heads)] for c in range(LANES)] for k in range(S)], F32
    ) * (jnp.arange(LANES) < C + 2).astype(F32)[None, :, None]
    grad_zx, grad_w_dt, grad_w_out, grad_shared_up, grad_shared_down, *found = finish(
        zx_in, wo_in, sh_in, small, pick, gain1, C, FS, state, S, H
    )
    grad_norm1, grad_norm2, grad_conv_x, grad_conv_bc, grad_gate_gain, by_head = found
    grad_norm1, grad_norm2, grad_gate_gain = (v.reshape(-1) for v in (grad_norm1, grad_norm2, grad_gate_gain))
    grad_dt_bias, grad_a_log, grad_d_skip = by_head[0], by_head[1], by_head[2]
    return (
        output, grad_in, grad_norm1, grad_zx, grad_bc, grad_w_dt, grad_conv_x, grad_conv_bc, grad_dt_bias,
        grad_a_log, grad_d_skip, grad_gate_gain, grad_w_out, grad_norm2, grad_router, grad_up, grad_down[None],
        grad_shared_up, grad_shared_down,
    )


def solution(mesh):
    return jax.shard_map(
        local,
        mesh=mesh,
        in_specs=(
            P(("seq", "head"), None),
            P(),
            P(None, None, "head"),
            P(),
            P(None, "head"),
            P(None, "head"),
            P(),
            P("head"),
            P("head"),
            P("head"),
            P("head"),
            P("head", None),
            P(),
            P(),
            P(("seq", "head"), None, None, None),
            P(("seq", "head"), None, None),
            P(),
            P(),
            P(("seq", "head"), None),
            P(),
            P(("seq", "head"), None),
        ),
        out_specs=(
            P(("seq", "head"), None),
            P(("seq", "head"), None),
            P(),
            P("seq", None, "head"),
            P(("seq", "head"), None),
            P("seq", "head"),
            P(),
            P(),
            P(),
            P(),
            P(),
            P(),
            P("head", "seq"),
            P(),
            P(("seq", "head"), None),
            P(("seq", "head"), None, None, None),
            P(("seq", "head"), None, None),
            P(("seq", "head"), None, None),
            P(None, ("seq", "head")),
        ),
        check_vma=False,
    )
```

time: 493 us -> 440 us (0.89)
  Pallas kernels: 423 us -> 386 us
  local copies, waits for them, and re-layouts: 54.4 us -> 39.3 us
    pallas_call x5 -> x4, Pallas kernels: 332 us -> 295 us  [the longest x1 130 us: experts(): pl.pallas_call(functools.partial(expert_kernel, S, H, F, width), out_shap...]
    reshape x7 -> x0, local copies, waits for them, and re-layouts: 9.36 us -> none  [the longest x1 5.3 us: local(): grad_up.reshape(expert_up.shape)]
    slice x12 -> x0, local copies, waits for them, and re-layouts: 5.71 us -> none  [the longest x2 1.98 us: local(): zx_rows = jnp.concatenate([grad_zx_w[:cut], grad_zx_w[CP:CP + C]], axis=0)]
    unnamed x61 -> x49, local copies, waits for them, and re-layouts: 12 us -> 17.5 us
where the time goes in v3:
time: 440 us; the launch traced here: 439 us
  Pallas kernels  386 us (88%)
  local copies, waits for them, and re-layouts  39.3 us (9%)
  other arithmetic  12.3 us (3%)
    pallas_call x1, Pallas kernels, experts(): pl.pallas_call(functools.partial(expert_kernel, S, H, F, width), out_shap...  130 us
    pallas_call x1, Pallas kernels, mixer_backward(): pl.pallas_call(functools.partial(mixer_backward_kernel, S, H, beside, end...  114 us
    pallas_call x1, Pallas kernels, first_rows(): pl.pallas_call(functools.partial(first_kernel, S, H), out_shape=jax.Shape...  47.4 us
    pallas_call x1, Pallas kernels, third_rows(): pl.pallas_call(functools.partial(third_kernel, S, H), out_shape=jax.Shape...  44.9 us
    pallas_call x1, Pallas kernels, mixer_forward(): pl.pallas_call(functools.partial(mixer_forward_kernel, S, H, ends.shape[0...  43.5 us
    unnamed x49, local copies, waits for them, and re-layouts  17.5 us

profile of v3, /device:TPU:0, one launch (start us, length us, event | category | flops | bytes accessed | tf_op | source)
XLA Modules:
  0.0 438.9 jit_solution(4602760517356916865)
XLA Ops:
  0.7 0.0 copy-start
  0.7 1.0 constant_dynamic-slice_fusion.6
  1.7 0.3 copy.100
  1.9 0.0 copy-start.6
  1.9 4.5 %constant_dynamic-slice_fusion.1 = (bf16[1536,1,96]{2,1,0:T(2,128)(2,1)S(1)}, bf16[1536,1,96]{2,1,0:T(2,128)(2,1)S(1)}) fusion(bf16[1536,2,768]{2,1,0:T(2,128)(2,1)} %param.24, s32[]{:T(128)S(6)} %select_n.41, s32[]{:T(128)S(6)} %add.86), kind=kLoop, calls=%fused_computation.26 | loop fusion | bytes 1179656 | tf_op jit(solution)/shard_map/slice | solution.py:1407
  6.5 0.0 copy-start.15
  6.5 0.0 copy-start.16
  6.5 0.0 copy-start.17
  6.5 0.0 copy-start.13
  6.5 0.1 copy_bitcast_fusion.3
  6.6 1.5 fusion.7.w_ref
  8.1 0.1 exponential_bitcast_fusion
  8.2 0.1 select_maximum_fusion.1
  8.3 0.2 fusion.10
  8.5 0.8 dynamic_slice.34
  9.3 0.6 pad.50.rows_ref
  9.9 1.0 constant_dynamic-slice_fusion.4
  10.9 0.8 pad.51.out_w_ref
  11.6 0.8 constant_dynamic-slice_fusion.5
  12.4 1.3 select_maximum_fusion.taps_ref
  13.7 0.6 broadcast_in_dim.22.gain_ref
  14.3 0.7 convert_reduce_fusion
  15.0 0.1 copy.86
  15.1 0.7 pad.44.named_ref
  15.8 47.4 %shard_map.357.in_ref.named_ref.one_ref = bf16[2048,1664]{1,0:T(8,128)(2,1)} custom-call(f32[64,1536]{1,0:T(8,128)} %in_ref.5, f32[1,1536]{1,0:T(1,128)} %broadcast_in_dim.22.gain_ref, bf16[64,128]{1,0:T(8,128)(2,1)} %pad.44.named_ref), custom_call_target="tpu_custom_call" | custom-call | tf_op jit(solution)/shard_map/pallas_call | solution.py:504
  63.2 0.7 reduce-window.9
  63.9 0.7 convert_element_type.72.grad_ref
  64.6 43.5 %shard_map.358 = (f32[2048,384]{1,0:T(8,128)}, f32[2048,128]{1,0:T(8,128)}, f32[2048,128]{1,0:T(8,128)}, f32[8,128,128]{2,1,0:T(8,128)}, bf16[2048,1664]{1,0:T(8,128)(2,1)}, /*index=5*/bf16[2048,1536]{1,0:T(8,128)(2,1)}) custom-call(s32[4]{0:T(128)} %bitcast.46, bf16[2048,1664]{1,0:T(8,128)(2,1)} %shard_map.357.in_ref.named_ref.one_ref, ...), custom_call_target="tpu_custom_call" | custom-call | tf_op jit(solution)/shard_map/pallas_call | solution.py:655
  108.1 0.5 compare_convert_fusion.1.mine_ref
  108.6 3.3 constant_dynamic-slice_fusion
  111.9 1.0 copy_bitcast_fusion.1
  112.9 1.0 copy.90
  113.9 0.0 copy-start.2
  114.0 0.0 copy-start.3
  114.0 0.1 pad_slice_fusion
  114.1 1.8 copy.105
  115.9 0.0 copy-start.7
  115.9 2.1 fusion.5.up_ref
  118.0 0.1 pad.57.clone
  118.1 1.2 maximum_maximum_fusion.down_ref
  119.4 0.9 pad.52.router_ref
  120.3 0.6 broadcast_in_dim.25.gain_ref
  120.9 129.8 %shard_map.359 = (bf16[64,1664]{1,0:T(8,128)(2,1)}, f32[64,1536]{1,0:T(8,128)}, f32[64,1536]{1,0:T(8,128)}, f32[1,1536]{1,0:T(1,128)}, bf16[1536,128]{1,0:T(8,12...) custom-call(bf16[4,2,2,2,64,1664]{5,4,3,2,1,0:T(8,128)(2,1)} %bitcas, ...), custom_call_target="tpu_custom_call" | custom-call | tf_op jit(solution)/shard_map/pallas_call | solution.py:1248
  250.7 44.9 %shard_map.360.three_ref = bf16[2048,1664]{1,0:T(8,128)(2,1)} custom-call(bf16[64,1664]{1,0:T(8,128)(2,1)} %get-tuple-element.54.rows_ref), custom_call_target="tpu_custom_call" | custom-call | tf_op jit(solution)/shard_map/pallas_call | solution.py:1287
  295.6 0.8 reshape.182
  296.4 1.2 copy.111
  297.6 0.1 copy.91
  297.7 0.7 pad.54.cols_ref
  298.5 113.9 %shard_map.361 = (bf16[32,96,48]{2,1,0:T(8,128)(2,1)}, f32[64,1536]{1,0:T(8,128)}, f32[64,1536]{1,0:T(8,128)}, f32[48,384]{1,0:T(8,128)}, f32[4,96,128]{2,1,0:T(...) custom-call(s32[4]{0:T(128)} %bitcast.47, bf16[2048,1664]{1,0:T(8,128)(2,1)} %shard_map.360.three_ref, ...), custom_call_target="tpu_custom_call" | custom-call | tf_op jit(solution)/shard_map/pallas_call | solution.py:987
  412.4 0.9 broadcast_multiply_fusion.pick_ref
  413.3 6.6 %shard_map.362 = (f32[192,2,768]{2,1,0:T(2,128)}, f32[192,12]{1,0:T(8,128)}, f32[768,192]{1,0:T(8,128)}, f32[48,2,1024]{2,1,0:T(2,128)}, f32[1024,48]{1,0:T(8,12...) custom-call(bf16[8,112,384]{2,1,0:T(8,128)(2,1)} %get-tuple-element., ...), custom_call_target="tpu_custom_call" | custom-call | tf_op jit(solution)/shard_map/pallas_call | solution.py:1348
  419.9 2.2 copy.95
  422.1 1.9 copy.97
  424.0 1.6 copy.94
  425.6 1.3 reduce
  426.9 1.3 reduce.1
  428.2 1.3 slice_bitcast_fusion
  429.6 0.6 slice.37
  430.2 0.1 slice.41
  430.3 0.7 copy.96
  430.9 0.7 copy.116
  431.7 0.7 copy.117
  432.4 5.4 %copy.118 = f32[1,1536,2,256]{3,2,1,0:T(2,128)} copy(f32[1,1536,2,256]{3,2,1,0:T(2,128)} %get-tuple-element.229) | data formatting | bytes 6291456
  437.8 1.1 copy.119
  (36 shorter events, 0.1 us)
Async XLA Ops:
  0.7 117.4 %copy-start = (bf16[1024,1536]{1,0:T(8,128)(2,1)S(1)}, bf16[1024,1536]{1,0:T(8,128)(2,1)}, u32[]{:S(2)}) copy-start(bf16[1024,1536]{1,0:T(8,128)(2,1)} %param.39) | copy-start | bytes 9437188
  1.9 4.7 %copy-start.6 = (bf16[1536,256]{1,0:T(8,128)(2,1)S(1)}, bf16[1536,256]{1,0:T(8,128)(2,1)}, u32[]{:S(2)}) copy-start(bf16[1536,256]{1,0:T(8,128)(2,1)} %param.25) | copy-start | bytes 2359300
  6.5 1.6 copy-start.15
  6.5 1.6 copy-start.16
  6.5 1.8 copy-start.17
  6.5 7.2 %copy-start.13 = (f32[1536]{0:T(1024)S(1)}, f32[1536]{0:T(1024)}, u32[]{:S(2)}) copy-start(f32[1536]{0:T(1024)} %param.23) | copy-start | bytes 18436
  15.8 47.4 %copy-start.18 = (s32[4]{0:T(128)S(1)}, s32[4]{0:T(128)}, u32[]{:S(2)}) copy-start(s32[4]{0:T(128)} %param.41) | copy-start | bytes 52
  15.8 48.1 %copy-start.5 = (f32[64,1536]{1,0:T(8,128)S(1)}, f32[64,1536]{1,0:T(8,128)}, u32[]{:S(2)}) copy-start(f32[64,1536]{1,0:T(8,128)} %ograd_ref.1) | copy-start | bytes 1179652
  113.9 1.9 copy-start.2
  114.0 1.9 copy-start.3
  115.9 2.3 copy-start.7
  115.9 4.4 %copy-start.14 = (f32[1536]{0:T(1024)S(1)}, f32[1536]{0:T(1024)}, u32[]{:S(2)}) copy-start(f32[1536]{0:T(1024)} %param.34) | copy-start | bytes 18436
  250.7 44.9 %copy-start.11 = (bf16[3,32,1536]{2,1,0:T(8,128)(2,1)S(1)}, bf16[3,32,1536]{2,1,0:T(8,128)(2,1)}, u32[]{:S(2)}) copy-start(bf16[3,32,1536]{2,1,0:T(8,128)(2,1)} %get-tuple-element.60) | copy-start | bytes 884740
  298.5 114.0 %copy-start.8 = (f32[8,128,12]{2,1,0:T(8,128)S(1)}, f32[8,128,12]{2,1,0:T(8,128)}, u32[]{:S(2)}) copy-start(f32[8,128,12]{2,1,0:T(8,128)} %constant.101) | copy-start | bytes 147460
  412.4 17.2 %copy-start.12 = (f32[48,384]{1,0:T(8,128)S(1)}, f32[48,384]{1,0:T(8,128)}, u32[]{:S(2)}) copy-start(f32[48,384]{1,0:T(8,128)} %get-tuple-element.73) | copy-start | bytes 221188
  412.4 18.5 %copy-start.10 = (f32[64,1536]{1,0:T(8,128)S(1)}, f32[64,1536]{1,0:T(8,128)}, u32[]{:S(2)}) copy-start(f32[64,1536]{1,0:T(8,128)} %get-tuple-element.214) | copy-start | bytes 1179652
  413.3 18.3 %copy-start.9 = (f32[64,1536]{1,0:T(8,128)S(1)}, f32[64,1536]{1,0:T(8,128)}, u32[]{:S(2)}) copy-start(f32[64,1536]{1,0:T(8,128)} %get-tuple-element.215) | copy-start | bytes 1179652
  432.4 5.4 %copy-start.4 = (f32[256,1536]{1,0:T(8,128)S(1)}, f32[256,1536]{1,0:T(8,128)}, u32[]{:S(2)}) copy-start(f32[256,1536]{1,0:T(8,128)} %get-tuple-element.82) | copy-start | bytes 4718596
  432.4 6.5 %copy-start.1 = (bf16[1024,1536]{1,0:T(8,128)(2,1)S(1)}, bf16[1024,1536]{1,0:T(8,128)(2,1)}, u32[]{:S(2)}) copy-start(bf16[1024,1536]{1,0:T(8,128)(2,1)} %param.39) | copy-start | bytes 9437188

commit v4 on v3

--- a/solution.py
+++ b/solution.py
@@ -1,6 +1,7 @@
 import functools
 import jax
 import jax.numpy as jnp
+import numpy as np
 from jax import lax
 from jax.experimental import pallas as pl
 from jax.experimental.pallas import tpu as pltpu
@@ -584,17 +585,47 @@
 
 def mixer_forward_kernel(
     S, H, count, state, C, ends_ref, in_ref, w_ref, taps_ref, rows_ref, out_w_ref, grad_ref,
-    pre_ref, z_ref, y_ref, st_ref, part_ref, all_ref, held, ext, send, recv, own_sem,
+    pre_ref, z_ref, y_ref, st_ref, total_ref, all_ref, held, ext, parts, *rest,
 ):
     i = pl.program_id(0)
     pc = Place(S, H)
+    buffers, (send, recv, zsend, zrecv, own_sem) = rest[:-5], rest[-5:]
+    X, Y, Z = pc.X, pc.Y, pc.Z
+    R = grad_ref.shape[0]
     mail = Mail(send, recv)
     moves = gather(pc, mail, grad_ref, all_ref, own_sem)
-    ready = pl.num_programs(0) - 1
+    acts = Script()
+    sums = Sum(
+        pc, mail, acts, lambda dz, yy, xx, rows: parts.at[dz, yy, xx, pc.c, rows], lambda dz: parts.at[dz, :, :, 1 - pc.c],
+        buffers, R, ends=(zsend, zrecv),
+    )
+    for dz in range(Z):
+        acts.stage()
+        sums.across(dz)
+        acts.stage()
+        sums.cores(dz)
+        acts.stage()
+        sums.firsts(dz)
+        acts.stage()
+        sums.seconds(dz)
+    acts.stage()
+    sums.home(total_ref)
+    ready = Y * Z - 1
+    before = {k: [] for k in range(Y * Z)}
+    for dz in range(Z):
+        for late, stage in ((0, 0), (1, 1), (3, 2), (4, 3)):
+            k = (dz + 1) * Y + late
+            if k <= ready:
+                before[k].append((acts, 4 * dz + stage))
+    final_acts = [
+        (acts, 4 * dz + stage)
+        for dz, stage in ((3, 0), (0, 3), (1, 2), (1, 3), (2, 1), (2, 2), (3, 1), (2, 3), (3, 2), (3, 3))
+    ]
+    final_acts = [entry for entry in final_acts if all(entry not in before[k] for k in before)]
 
     @pl.when(i == 0)
     def _():
-        greet(pc.peers())
+        greet(pc.peers(direct=True))
         moves.run(0, 1)
 
     for step, stage, until in ((1, 1, 2), (2, 2, 3), (3, 3, 5), (4, 5, 7), (5, 7, 9), (6, 9, 11)):
@@ -602,6 +633,14 @@
         @pl.when(i == step)
         def _():
             moves.run(stage, until)
+
+    for at in range(1, Y * Z):
+        if before[at]:
+
+            @pl.when(i == at)
+            def _():
+                for script, stage in before[at]:
+                    script.run(stage, stage + 1)
 
     depth = w_ref.shape[0]
     n, cp = BLOCK, z_ref.shape[1]
@@ -625,15 +664,25 @@
     y = y + blk.skip * blk.x
     y_ref[...] = y
     gated = y * silu(z)
-    part_ref[:, :depth] = mm((gated * blk.gain).astype(B16), out_w_ref[...]).astype(B16)
+    part = mm((gated * blk.gain).astype(B16), out_w_ref[...]).astype(B16)
     high, rest = hi_lo(jnp.sum(gated * gated, axis=1, keepdims=True))
     lane = lax.broadcasted_iota(jnp.int32, (n, LANES), 1)
-    part_ref[:, depth:] = jnp.where(lane == 0, high.astype(F32), jnp.where(lane == 1, rest.astype(F32), 0.0)).astype(B16)
+    tail = jnp.where(lane == 0, high.astype(F32), jnp.where(lane == 1, rest.astype(F32), 0.0)).astype(B16)
+    for xx in range(X):
+        for cc in range(2):
+            at = slice((xx * 2 + cc) * R, (xx * 2 + cc + 1) * R)
+            parts[i // Y, i % Y, xx, cc, :, :depth] = part[at]
+            parts[i // Y, i % Y, xx, cc, :, depth:] = tail[at]
 
     @pl.when(i == ready)
     def _():
+        for script, stage in final_acts[:4]:
+            script.run(stage, stage + 1)
         moves.run(11)
-        mail.finish(gather_count(S, H))
+        for script, stage in final_acts[4:]:
+            script.run(stage, stage + 1)
+        acts.run(4 * Z)
+        mail.finish(gather_count(S, H) + scatter_count(S, H) - 3)
 
 
 def whole(shape):
@@ -646,6 +695,8 @@
 
 def mixer_forward(ends, gathered, in_w, taps, rows, out_w, grad, state, C, S, H):
     T, depth = gathered.shape[0], in_w.shape[0]
+    X, Y, Z = sizes(S, H)
+    R = grad.shape[0]
     cp, nb = out_w.shape[0], gathered.shape[0] // BLOCK
     conv_width = cp + 2 * state
 
@@ -661,19 +712,21 @@
         ],
         out_specs=[
             block(conv_width), block(cp), block(cp),
-            pl.BlockSpec((1, state, cp), lambda i: (i, 0, 0)), block(depth + LANES), ANY,
+            pl.BlockSpec((1, state, cp), lambda i: (i, 0, 0)), VMEM, ANY,
         ],
         out_shape=[
             jax.ShapeDtypeStruct((T, conv_width), F32),
             jax.ShapeDtypeStruct((T, cp), F32),
             jax.ShapeDtypeStruct((T, cp), F32),
             jax.ShapeDtypeStruct((nb, state, cp), F32),
-            jax.ShapeDtypeStruct((T, depth + LANES), B16),
+            jax.ShapeDtypeStruct((R, depth + LANES), F32),
             jax.ShapeDtypeStruct((T, depth), B16),
         ],
         scratch_shapes=[
-            pltpu.VMEM((state, cp), F32), pltpu.VMEM((BLOCK + 8, conv_width), F32), *sems(gather_count(S, H)),
-            pltpu.SemaphoreType.DMA,
+            pltpu.VMEM((state, cp), F32), pltpu.VMEM((BLOCK + 8, conv_width), F32),
+            pltpu.VMEM((Z, Y, X, 2, R, depth + LANES), B16), *sum_scratch(S, H, R, depth + LANES),
+            *sems(gather_count(S, H) + scatter_count(S, H) - 3),
+            pltpu.SemaphoreType.DMA((4,)), pltpu.SemaphoreType.DMA((3,)), pltpu.SemaphoreType.DMA,
         ],
         compiler_params=talking(5),
     )(ends, gathered, in_w, taps, rows, out_w, grad)
@@ -681,8 +734,8 @@
 
 def mixer_backward_kernel(
     S, H, beside, count, state, C, ends_ref, three_ref, one_ref, pre_ref, halo_ref, z_ref, y_ref, st_ref,
-    w_ref, taps_ref, rows_ref, cols_ref, out_w_ref, p_ref, sh_ref, res_ref, gres_ref, in_ref, gain_ref, norm2_ref, router_ref,
-    sh_out, output_ref, gin_ref, extra_ref, small_out, zx_out, wo_out,
+    w_ref, taps_ref, rows_ref, cols_ref, out_w_ref, p_ref, res_ref, gres_ref, in_ref, gain_ref, norm2_ref, router_ref,
+    output_ref, gin_ref, extra_ref, small_out, zx_out, wo_out,
     held, ext, gext, gw_ref, gout_ref, gtaps_ref, gvec_ref, gnorm_ref, total, parts, extra, zx_ref, wo_ref, small, joint,
     *rest,
 ):
@@ -693,7 +746,7 @@
 
     n1, n2 = 8 if beside else 0, 6
     scratch, main, side = rest[:n1], rest[n1 : n1 + n2], rest[n1 + n2 : n1 + n2 + 4]
-    send, recv, sh_send, sh_recv, send2, recv2, zsend, zrecv, group_send, group_recv, sh_sem, local_sem = rest[n1 + n2 + 4 :]
+    send, recv, send2, recv2, zsend, zrecv, group_send, group_recv, local_sem = rest[n1 + n2 + 4 :]
     pc = Place(S, H)
     X, Y, Z = pc.X, pc.Y, pc.Z
     N, me, R = S * H, pc.slot(), res_ref.shape[0]
@@ -776,34 +829,10 @@
                 before[k].append((acts, 4 * dz + stage))
     final_acts = [(acts, 4 * dz + stage) for dz, stage in ((0, 0), (3, 3), (2, 2), (2, 3), (1, 1), (1, 2), (0, 1), (1, 3), (0, 2), (0, 3))]
     final_acts = [entry for entry in final_acts if all(entry not in before[k] for k in before)]
-    stay = pltpu.make_async_copy(sh_ref.at[me], sh_out.at[me], sh_sem)
-
-    def to_all(function, first, last):
-        def body(m, carry):
-            to = (me + m) % N
-            function(
-                pltpu.make_async_remote_copy(
-                    src_ref=sh_ref.at[to], dst_ref=sh_out.at[me], send_sem=sh_send.at[m], recv_sem=sh_recv.at[m],
-                    device_id=(to // H, to % H), device_id_type=MESH,
-                )
-            )
-            return carry
-
-        lax.fori_loop(first, last, body, 0)
-
     @pl.when(step == 0)
     def _():
         sums.run(0, 1)
-        stay.start()
-        barrier = pltpu.get_barrier_semaphore()
-
-        def hello(m, carry):
-            to = (me + m) % N
-            pl.semaphore_signal(barrier, inc=1, device_id=(to // H, to % H), device_id_type=MESH)
-            return carry
-
-        lax.fori_loop(1, N, hello, 0)
-        pl.semaphore_wait(barrier, N - 1)
+        greet([((seq + m) % S, head) for m in range(1, S)] + [(seq, (head + m) % H) for m in range(1, H)])
         sums.run(1, 2)
 
     for at in range(1, total_steps):
@@ -813,10 +842,6 @@
             def _():
                 for script, stage in before[at]:
                     script.run(stage, stage + 1)
-
-    @pl.when(step == 1)
-    def _():
-        to_all(lambda copy: copy.start(), 1, N)
 
     @pl.when(step == 0)
     def _():
@@ -951,16 +976,14 @@
         for copy in column:
             copy.wait_send()
         keep_joint.wait()
-        to_all(lambda copy: copy.wait(), 1, N)
         for copy in keep_here + group:
             copy.wait()
-        stay.wait()
         mail.finish(scatter_count(S, H) if beside else 0)
         mail2.finish(scatter_count(S, H) - 3 + scatter_count(S, H, (False,)))
 
 
 def mixer_backward(
-    ends, three, one, pre, z, y, states, in_w, taps, rows, cols, out_w, out_part, shared, residual, grad_res, hidden_in, gain,
+    ends, three, one, pre, z, y, states, in_w, taps, rows, cols, out_w, out_part, residual, grad_res, hidden_in, gain,
     norm2, router_part, state, C, S, H,
 ):
     T, depth = three.shape[0], in_w.shape[0]
@@ -991,11 +1014,10 @@
             pl.BlockSpec(memory_space=pltpu.SMEM), block(three.shape[1]), block(one.shape[1], kept), block(conv_width, kept),
             pl.BlockSpec((8, conv_width), halo), block(cp), block(cp),
             pl.BlockSpec((1, state, cp), lambda k: (nb - 1 - k, 0, 0)),
-            VMEM, VMEM, VMEM, VMEM, VMEM, ANY, ANY, VMEM, VMEM, VMEM, VMEM, VMEM, VMEM,
+            VMEM, VMEM, VMEM, VMEM, VMEM, ANY, VMEM, VMEM, VMEM, VMEM, VMEM, VMEM,
         ],
-        out_specs=[ANY, VMEM, VMEM, VMEM, ANY, ANY, ANY],
+        out_specs=[VMEM, VMEM, VMEM, ANY, ANY, ANY],
         out_shape=[
-            jax.ShapeDtypeStruct(shared.shape, shared.dtype),
             jax.ShapeDtypeStruct((R, depth), F32),
             jax.ShapeDtypeStruct((R, depth), F32),
             jax.ShapeDtypeStruct((tall, 2 * state + LANES), F32),
@@ -1023,15 +1045,14 @@
             *sum_scratch(S, H, R, depth),
             *sum_scratch(S, H, tall, 2 * state + LANES, False),
             *sems(scatter_count(S, H)),
-            *sems(N),
             *sems(sent),
             pltpu.SemaphoreType.DMA((4,)), pltpu.SemaphoreType.DMA((3,)),
             pltpu.SemaphoreType.DMA((4, S)), pltpu.SemaphoreType.DMA((4, S)),
-            pltpu.SemaphoreType.DMA, pltpu.SemaphoreType.DMA((3,)),
+            pltpu.SemaphoreType.DMA((3,)),
         ],
         compiler_params=talking(6),
     )(
-        ends, three, one, pre, pre, z, y, states, in_w, taps, rows, cols, out_w, blocks(out_part, S, H), shared, residual,
+        ends, three, one, pre, pre, z, y, states, in_w, taps, rows, cols, out_w, blocks(out_part, S, H), residual,
         grad_res, hidden_in, gain, norm2, router_part,
     )
 
@@ -1065,44 +1086,39 @@
 
 
 def expert_kernel(
-    S, H, F, width, p_ref, in_ref, gain_ref, grad_ref, named_ref, up_ref, down_ref, mine_ref, router_ref, ograd_ref,
-    rows_ref, res_ref, gres_ref, gnorm_ref, grouter_ref, out_ref, gup_out, gdown_ref, gsh_ref,
+    S, H, F, width, total_ref, in_ref, gain_ref, grad_ref, named_ref, up_ref, down_ref, mine_ref, router_ref, ograd_ref,
+    three_ref, res_ref, gres_ref, gnorm_ref, grouter_ref, out_ref, gup_out, gdown_ref, sh_out,
     gup_ref, total, rows, two, grads, names, parts, stage_out, probs, gs_ref, *rest,
 ):
-    buffers, (send1, recv1, send2, recv2, own_sem, load_sem, name_sem, grad_sem, out_sem) = rest[:-9], rest[-9:]
+    buffers, (rows3, pieces, send2, recv2, sh_send, sh_recv, own_sem, own3_sem, sh_sem, name_sem, grad_sem, out_sem) = (
+        rest[:-12], rest[-12:]
+    )
     pc = Place(S, H)
     X, Y, Z = pc.X, pc.Y, pc.Z
     R, D = in_ref.shape
     n = BLOCK
-    mail1, mail2 = Mail(send1, recv1), Mail(send2, recv2)
+    N, me = S * H, pc.slot()
+    mail2 = Mail(send2, recv2)
+    stay = pltpu.make_async_copy(pieces.at[me], sh_out.at[me], sh_sem)
+
+    def to_all(function):
+        def body(m, carry):
+            to = (me + m) % N
+            function(
+                pltpu.make_async_remote_copy(
+                    src_ref=pieces.at[to], dst_ref=sh_out.at[me], send_sem=sh_send.at[m], recv_sem=sh_recv.at[m],
+                    device_id=(to // H, to % H), device_id_type=MESH,
+                )
+            )
+            return carry
+
+        lax.fori_loop(1, N, body, 0)
 
     def cell(dz, yy, xx, rows):
         return parts.at[dz, yy, xx, pc.c, rows]
 
-    sums = Script()
-    first = Sum(
-        pc, mail1, sums, cell, lambda dz: p_ref.at[pc.at(dz=dz)[0], :, :, 1 - pc.c], buffers, R
-    )
-    own = {
-        dz: pltpu.make_async_copy(p_ref.at[pc.at(dz=dz)[0], :, :, pc.c], parts.at[dz, :, :, pc.c], load_sem.at[dz])
-        for dz in ORDER
-    }
-    for copy in own.values():
-        copy.start()
-    sums.stage()
-    for dz in ORDER:
-        first.across(dz)
-    for dz in ORDER:
-        sums.do(own[dz].wait)
-        first.cores(dz)
-    for dz in ORDER:
-        first.firsts(dz)
-        if dz < 3:
-            first.seconds(dz + 1)
-    first.seconds(0)
-    first.last(total)
-
     moves = gather(pc, mail2, rows, two, own_sem, planes=True)
+    onward = gather(pc, mail2, rows3, three_ref, own3_sem)
     acts = Script()
     second = Sum(pc, mail2, acts, cell, lambda dz: parts.at[dz, :, :, 1 - pc.c], buffers, R, direct=True)
     for dz in range(Z):
@@ -1133,23 +1149,28 @@
 
     for copy in loads(0, 0):
         copy.start()
-    gup_ref[...] = jnp.zeros_like(gup_ref)
-    gdown_ref[...] = jnp.zeros_like(gdown_ref)
-    gs_ref[...] = jnp.zeros_like(gs_ref)
-    greet(pc.peers(direct=True))
-    sums.run()
     gain = gain_ref[...]
-    mixed = total[:, :D]
-    square = jnp.sum(total[:, D:], axis=1, keepdims=True)
+    mixed = total_ref[:, :D]
+    square = jnp.sum(total_ref[:, D:], axis=1, keepdims=True)
     inv = lax.rsqrt(square / width + EPS)
     residual = in_ref[...] + inv * mixed
     res_ref[...] = residual
     rows[...] = (residual * inverse_rms(residual) * gain).astype(B16)
-    gres_ref[...] = mixed
     cube = inv * inv * inv / width
-    moves.run(0, 5)
-    for copy in mail1.made:
-        copy.wait_send()
+    barrier = pltpu.get_barrier_semaphore()
+
+    def hello(m, carry):
+        to = (me + m) % N
+        pl.semaphore_signal(barrier, inc=1, device_id=(to // H, to % H), device_id_type=MESH)
+        return carry
+
+    lax.fori_loop(1, N, hello, 0)
+    pl.semaphore_wait(barrier, N - 1)
+    moves.run(0, 1)
+    gup_ref[...] = jnp.zeros_like(gup_ref)
+    gdown_ref[...] = jnp.zeros_like(gdown_ref)
+    gs_ref[...] = jnp.zeros_like(gs_ref)
+    moves.run(1, 5)
     moves.run(12, 13)
 
     count = Y * Z
@@ -1212,10 +1233,14 @@
         script.run(stage, stage + 1)
     for k in range(2):
         gup_out[0, :, k, :] = gup_ref[:, k * F : (k + 1) * F]
+    per, FS = D // N, pieces.shape[2] // 3
+    turned = jnp.concatenate([gs_ref[k * LANES : k * LANES + FS, :] for k in range(3)], axis=0).T
+    for k in range(N):
+        pieces[k, :per, :] = turned[k * per : (k + 1) * per, :].astype(B16)
+        if per < pieces.shape[1]:
+            pieces[k, per:, :] = jnp.zeros((pieces.shape[1] - per, 3 * FS), B16)
     for script, stage in after[1:]:
         script.run(stage, stage + 1)
-    for k in range(3):
-        gsh_ref[k] = gs_ref[k * LANES : k * LANES + gsh_ref.shape[1], :].astype(B16)
     head = lax.axis_index("head")
     p = probs[pl.ds(pl.multiple_of(head * R, R), R), :]
     acts.run(4 * Z)
@@ -1224,31 +1249,36 @@
     gtwo = total[:, :D] + mm(glogits, router_ref[...], NT)
     residual = res_ref[...]
     inv_two = inverse_rms(residual)
-    mixed = gres_ref[...]
     gres = ograd_ref[...] + rms_back(residual, inv_two, gain, gtwo)
     cross = jnp.sum(gres * mixed, axis=1, keepdims=True) * cube
     high, low = hi_lo(cross)
     lane = lax.broadcasted_iota(jnp.int32, (R, LANES), 1)
-    rows_ref[:, :D] = (inv * gres).astype(B16)
-    rows_ref[:, D:] = jnp.where(lane == 0, high.astype(F32), jnp.where(lane == 1, low.astype(F32), 0.0)).astype(B16)
+    rows3[:, :D] = (inv * gres).astype(B16)
+    rows3[:, D:] = jnp.where(lane == 0, high.astype(F32), jnp.where(lane == 1, low.astype(F32), 0.0)).astype(B16)
+    onward.run(0, 1)
+    stay.start()
+    to_all(lambda copy: copy.start())
     gres_ref[...] = gres
     gnorm_ref[...] = jnp.sum(gtwo * residual * inv_two, axis=0, keepdims=True)
     grouter_ref[...] = mm((residual * inv_two * gain).astype(B16), glogits, TN).astype(B16)
     for k in (count - 2, count - 1):
         store(k, k % 2).wait()
-    mail2.finish(gather_count(S, H) + scatter_count(S, H))
-
-
-def experts(part, hidden_in, gain, all_grad, gathered, up_w, down_w, mine, router, out_grad, F, FS, width, S, H):
+    onward.run(1)
+    to_all(lambda copy: copy.wait())
+    stay.wait()
+    mail2.finish(2 * gather_count(S, H) + scatter_count(S, H))
+
+
+def experts(total, hidden_in, gain, all_grad, gathered, up_w, down_w, mine, router, out_grad, F, FS, width, S, H):
     R, D = hidden_in.shape
     X, Y, Z = sizes(S, H)
     T, W = S * H * R, D + LANES
-    tall = -(-FS // 16) * 16
+    tall = -(-(D // (S * H)) // 16) * 16
     assert R * H == BLOCK
     return pl.pallas_call(
         functools.partial(expert_kernel, S, H, F, width),
         out_shape=[
-            jax.ShapeDtypeStruct((R, W), B16),
+            jax.ShapeDtypeStruct((T, W), B16),
             jax.ShapeDtypeStruct((R, D), F32),
             jax.ShapeDtypeStruct((R, D), F32),
             jax.ShapeDtypeStruct((1, D), F32),
@@ -1256,64 +1286,55 @@
             jax.ShapeDtypeStruct((T, D), B16),
             jax.ShapeDtypeStruct((1, D, 2, F), F32),
             jax.ShapeDtypeStruct((F, D), F32),
-            jax.ShapeDtypeStruct((3, tall, D), B16),
+            jax.ShapeDtypeStruct((S * H, tall, 3 * FS), B16),
         ],
-        in_specs=[ANY, VMEM, VMEM, ANY, ANY] + [VMEM] * 5,
-        out_specs=[VMEM] * 5 + [ANY] + [VMEM] * 3,
+        in_specs=[VMEM, VMEM, VMEM, ANY, ANY] + [VMEM] * 5,
+        out_specs=[ANY] + [VMEM] * 4 + [ANY] + [VMEM] * 2 + [ANY],
         scratch_shapes=[
             pltpu.VMEM((D, 2 * F), F32), pltpu.VMEM((R, W), F32), pltpu.VMEM((R, D), B16), pltpu.VMEM((T, D), B16),
             pltpu.VMEM((2, BLOCK, D), B16), pltpu.VMEM((2, BLOCK, LANES), B16),
             pltpu.VMEM((Z, Y, X, 2, R, W), B16), pltpu.VMEM((2, BLOCK, D), B16), pltpu.VMEM((BLOCK, LANES), F32),
             pltpu.VMEM((3 * LANES, D), F32), *sum_scratch(S, H, R, W),
-            *sems(scatter_count(S, H)), *sems(scatter_count(S, H) + gather_count(S, H)),
-            pltpu.SemaphoreType.DMA, pltpu.SemaphoreType.DMA((Z,)), pltpu.SemaphoreType.DMA((2,)),
+            pltpu.VMEM((R, W), B16), pltpu.VMEM((S * H, tall, 3 * FS), B16),
+            *sems(scatter_count(S, H) + 2 * gather_count(S, H)), *sems(S * H),
+            pltpu.SemaphoreType.DMA, pltpu.SemaphoreType.DMA, pltpu.SemaphoreType.DMA, pltpu.SemaphoreType.DMA((2,)),
             pltpu.SemaphoreType.DMA((2,)), pltpu.SemaphoreType.DMA((2,)),
         ],
         compiler_params=talking(2),
-    )(blocks(part, S, H), hidden_in, gain, all_grad, gathered, up_w, down_w, mine, router, out_grad)
-
-
-def third_kernel(S, H, rows_ref, out_ref, send, recv, own_sem):
-    pc = Place(S, H)
-    mail = Mail(send, recv)
-    moves = gather(pc, mail, rows_ref, out_ref, own_sem)
-    greet(pc.peers())
-    moves.run()
-    mail.finish(gather_count(S, H))
-
-
-def third_rows(rows, S, H):
-    R, W = rows.shape
-    return pl.pallas_call(
-        functools.partial(third_kernel, S, H),
-        out_shape=jax.ShapeDtypeStruct((S * H * R, W), B16),
-        in_specs=[VMEM],
-        out_specs=ANY,
-        scratch_shapes=[*sems(gather_count(S, H)), pltpu.SemaphoreType.DMA],
-        compiler_params=talking(3),
-    )(rows)
+    )(total, hidden_in, gain, all_grad, gathered, up_w, down_w, mine, router, out_grad)
 
 
 def finish_kernel(
-    S, H, C, FS, state, zx_ref, wo_ref, sh_ref, small_ref, pick_ref, gain_ref,
+    S, H, C, FS, state, zx_ref, wo_ref, sh_ref, small_ref, pick_ref, kcip_ref, gain_ref, a_in, b_in, c_in, d_in,
     zx_out, dt_out, wo_out, up_out, down_out, norm1_out, norm2_out, taps_out, bc_out, gate_out, heads_out,
+    a_out, b_out, c_out, d_out, a_way, b_way, c_way, d_way, sem,
 ):
+    ways = ((a_in, a_way, a_out), (b_in, b_way, b_out), (c_in, c_way, c_out), (d_in, d_way, d_out))
+    held = [pltpu.make_async_copy(src, way, sem.at[0, k]) for k, (src, way, dst) in enumerate(ways)]
+    gone = [pltpu.make_async_copy(way, dst, sem.at[1, k]) for k, (src, way, dst) in enumerate(ways)]
+    for copy in held:
+        copy.start()
     wide = wo_ref.shape[2]
-    heads = dt_out.shape[1]
+    heads = dt_out.shape[0]
     dt = jnp.zeros(dt_out.shape, F32)
     for t in range(S):
-        turned = zx_ref[t].astype(F32).T
+        piece = zx_ref[t].astype(F32)
+        turned = piece.T
         at = slice(t * C, (t + 1) * C)
         zx_out[:, 0, at] = turned[:wide, :C]
         zx_out[:, 1, at] = turned[wide:, :C]
-        dt = dt + exact(turned[:wide, :], pick_ref[t, : turned.shape[1], :])
-        wo_out[at, :] = wo_ref[t, :C, :].astype(F32)
+        dt = dt + exact(kcip_ref[t, :, : piece.shape[0]], piece[:, :wide])
+        wo_out[:, at] = wo_ref[t].astype(F32).T[:, :C]
     dt_out[...] = dt
-    N, tall, per = sh_ref.shape[0], sh_ref.shape[1] // 3, sh_ref.shape[2]
-    for k in range(2):
-        rows = sh_ref[:, k * tall : (k + 1) * tall, :].astype(F32)[:, :FS, :]
-        up_out[:, k, :] = rows.reshape(N * FS, per).T
-    down_out[...] = sh_ref[:, 2 * tall :, :].astype(F32)[:, :FS, :].reshape(N * FS, per)
+    for come, go in zip(held, gone):
+        come.wait()
+        go.start()
+    for t in range(S * H):
+        piece = sh_ref[t].astype(F32)[: up_out.shape[0]]
+        at = slice(t * FS, (t + 1) * FS)
+        for k in range(2):
+            up_out[:, k, at] = piece[:, k * FS : (k + 1) * FS]
+        down_out[:, at] = piece[:, 2 * FS :]
     lines = gain_ref.shape[1] // LANES
     total = small_ref[0, : 2 * lines + 4 * (2 * state // LANES), :]
     for h in range(1, H):
@@ -1337,21 +1358,25 @@
             by_head = by_head + exact(ours, pick_ref[t])
         for r in range(3):
             heads_out[r : r + 1, h * heads : (h + 1) * heads] = by_head[5 + r : 6 + r, :]
-
-
-def finish(zx, wo, shared, small, pick, gain, C, FS, state, S, H):
-    N, per, wide, heads, D = shared.shape[0], shared.shape[2], wo.shape[2], pick.shape[2], gain.shape[1]
+    for copy in gone:
+        copy.wait()
+
+
+def finish(zx, wo, shared, small, pick, gain, made, C, FS, state, S, H):
+    N, wide, heads, D = S * H, wo.shape[2], pick.shape[2], gain.shape[1]
+    per = D // N
     shapes = (
-        (wide, 2, S * C), (wide, heads), (S * C, wide), (per, 2, N * FS), (N * FS, per), (1, D), (1, D), (4, S * H * C),
+        (wide, 2, S * C), (heads, wide), (wide, S * C), (per, 2, N * FS), (per, N * FS), (1, D), (1, D), (4, S * H * C),
         (4, 2 * state), (1, S * H * C), (3, H * heads),
     )
     return pl.pallas_call(
         functools.partial(finish_kernel, S, H, C, FS, state),
-        out_shape=[jax.ShapeDtypeStruct(shape, F32) for shape in shapes],
-        in_specs=[VMEM] * 6,
-        out_specs=[VMEM] * len(shapes),
+        out_shape=[jax.ShapeDtypeStruct(shape, F32) for shape in shapes + tuple(v.shape for v in made)],
+        in_specs=[VMEM] * 7 + [ANY] * 4,
+        out_specs=[VMEM] * len(shapes) + [ANY] * 4,
+        scratch_shapes=[*(pltpu.VMEM(v.shape, F32) for v in made), pltpu.SemaphoreType.DMA((2, 4))],
         compiler_params=pltpu.CompilerParams(vmem_limit_bytes=56 * 1024 * 1024),
-    )(zx, wo, shared, small, pick, gain)
+    )(zx, wo, shared, small, pick, pick.transpose(0, 2, 1), gain, *made)
 
 
 def local(
@@ -1419,7 +1444,7 @@
     cols = in_free(masks.T)
     ends = jnp.cumsum(seq_lengths)
 
-    pre, z, y, states, part, all_grad = mixer_forward(
+    pre, z, y, states, mixed, all_grad = mixer_forward(
         ends, gathered, in_w, taps, rows, out_w, out_grad.astype(B16), state, C, S, H
     )
 
@@ -1433,33 +1458,31 @@
     )
     down_w = jnp.concatenate([expert_down[0], mine(shared_down, 0, g * FS, FS), jnp.zeros((LANES - FS, D), B16)], axis=0)
     is_mine = (jnp.arange(LANES) == FS + g // 2).astype(F32)[None]
-    rows_three, residual, grad_res, norm2_part, router_part, out_part, grad_up, grad_down, grad_shared = experts(
-        part, hidden_in, gain2, all_grad, gathered, up_w, down_w, is_mine, router_w, out_grad, F, FS, width, S, H
-    )
-    three = third_rows(rows_three, S, H)
-
-    tall_s = grad_shared.shape[1]
-    shared = grad_shared.reshape(3 * tall_s, N, per).transpose(1, 0, 2)
-    sh_in, output, grad_in, extra_sum, small, zx_in, wo_in = mixer_backward(
-        ends, three, gathered, pre, z, y, states, in_w, taps, rows, cols, out_w, out_part, shared, residual,
+    three, residual, grad_res, norm2_part, router_part, out_part, grad_up, grad_down, sh_in = experts(
+        mixed, hidden_in, gain2, all_grad, gathered, up_w, down_w, is_mine, router_w, out_grad, F, FS, width, S, H
+    )
+
+    output, grad_in, extra_sum, small, zx_in, wo_in = mixer_backward(
+        ends, three, gathered, pre, z, y, states, in_w, taps, rows, cols, out_w, out_part, residual,
         grad_res, hidden_in, gain1, norm2_part, router_part, state, C, S, H,
     )
     if H > 4:
         output = output + lax.psum_scatter(out_part, ("seq", "head"), scatter_dimension=0, tiled=True).astype(F32)
     grad_bc, grad_router = extra_sum[:per, : 2 * state], extra_sum[:per, 2 * state :][:, FS : FS + E]
-    pick = jnp.asarray(
-        [[[float(c >= C and firsts[k] + c - C == h) for h in range(heads)] for c in range(LANES)] for k in range(S)], F32
-    ) * (jnp.arange(LANES) < C + 2).astype(F32)[None, :, None]
+    pick = np.array(
+        [[[C <= c < C + 2 and firsts[k] + c - C == h for h in range(heads)] for c in range(LANES)] for k in range(S)], np.float32
+    )
     grad_zx, grad_w_dt, grad_w_out, grad_shared_up, grad_shared_down, *found = finish(
-        zx_in, wo_in, sh_in, small, pick, gain1, C, FS, state, S, H
-    )
-    grad_norm1, grad_norm2, grad_conv_x, grad_conv_bc, grad_gate_gain, by_head = found
+        zx_in, wo_in, sh_in, small, pick, gain1, (grad_up, grad_down[None], output, grad_in), C, FS, state, S, H
+    )
+    grad_norm1, grad_norm2, grad_conv_x, grad_conv_bc, grad_gate_gain, by_head, *made = found
+    grad_up, grad_down, output, grad_in = made
     grad_norm1, grad_norm2, grad_gate_gain = (v.reshape(-1) for v in (grad_norm1, grad_norm2, grad_gate_gain))
     grad_dt_bias, grad_a_log, grad_d_skip = by_head[0], by_head[1], by_head[2]
     return (
-        output, grad_in, grad_norm1, grad_zx, grad_bc, grad_w_dt, grad_conv_x, grad_conv_bc, grad_dt_bias,
-        grad_a_log, grad_d_skip, grad_gate_gain, grad_w_out, grad_norm2, grad_router, grad_up, grad_down[None],
-        grad_shared_up, grad_shared_down,
+        output, grad_in, grad_norm1, grad_zx, grad_bc, grad_w_dt.T, grad_conv_x, grad_conv_bc, grad_dt_bias,
+        grad_a_log, grad_d_skip, grad_gate_gain, grad_w_out.T, grad_norm2, grad_router, grad_up, grad_down,
+        grad_shared_up, grad_shared_down.T,
     )
 
 

time: 440 us -> 415 us (0.943)
  local copies, waits for them, and re-layouts: 39.3 us -> 23.6 us
  Pallas kernels: 386 us -> 378 us
    pallas_call x1 -> x0, Pallas kernels: 44.9 us -> none  [third_rows(): pl.pallas_call(functools.partial(third_kernel, S, H), out_shape=jax.Shape...]
    pallas_call x1, Pallas kernels: 43.5 us -> 73 us  [mixer_forward(): pl.pallas_call(functools.partial(mixer_forward_kernel, S, H, ends.shape[0...]
    unnamed x49 -> x32, local copies, waits for them, and re-layouts: 17.5 us -> 3.83 us
    pallas_call x1, Pallas kernels: 130 us -> 140 us  [experts(): pl.pallas_call(functools.partial(expert_kernel, S, H, F, width), out_shap...]
    pallas_call x1, Pallas kernels: 114 us -> 109 us  [mixer_backward(): pl.pallas_call(functools.partial(mixer_backward_kernel, S, H, beside, end...]
where the time goes in v4:
time: 415 us; the launch traced here: 414 us
  Pallas kernels  378 us (91%)
  local copies, waits for them, and re-layouts  23.6 us (6%)
  other arithmetic  11.4 us (3%)
    pallas_call x1, Pallas kernels, experts(): pl.pallas_call(functools.partial(expert_kernel, S, H, F, width), out_shap...  140 us
    pallas_call x1, Pallas kernels, mixer_backward(): pl.pallas_call(functools.partial(mixer_backward_kernel, S, H, beside, end...  109 us
    pallas_call x1, Pallas kernels, mixer_forward(): pl.pallas_call(functools.partial(mixer_forward_kernel, S, H, ends.shape[0...  73 us
    pallas_call x1, Pallas kernels, first_rows(): pl.pallas_call(functools.partial(first_kernel, S, H), out_shape=jax.Shape...  47.4 us
    pallas_call x1, Pallas kernels, finish(): pl.pallas_call(functools.partial(finish_kernel, S, H, C, FS, state), out_...  8.67 us

profile of v4, /device:TPU:0, one launch (start us, length us, event | category | flops | bytes accessed | tf_op | source)
XLA Modules:
  0.0 414.2 jit_solution(10557481180128092451)
XLA Ops:
  0.7 0.0 copy-start
  0.7 1.0 constant_dynamic-slice_fusion.6
  1.7 0.3 copy.73
  1.9 0.0 copy-start.5
  1.9 4.5 %constant_dynamic-slice_fusion.1 = (bf16[1536,1,96]{2,1,0:T(2,128)(2,1)S(1)}, bf16[1536,1,96]{2,1,0:T(2,128)(2,1)S(1)}) fusion(bf16[1536,2,768]{2,1,0:T(2,128)(2,1)} %param.25, s32[]{:T(128)S(6)} %select_n.41, s32[]{:T(128)S(6)} %add.86), kind=kLoop, calls=%fused_computation.24 | loop fusion | bytes 1179656 | tf_op jit(solution)/shard_map/slice | solution.py:1432
  6.5 0.0 copy-start.10
  6.5 0.0 copy-start.11
  6.5 0.0 copy-start.12
  6.5 0.0 copy-start.8
  6.5 0.1 copy_bitcast_fusion.2
  6.6 0.0 copy-done.5
  6.6 1.5 fusion.7.w_ref
  8.1 0.0 copy-done.10
  8.1 0.0 copy-done.11
  8.1 0.1 exponential_bitcast_fusion
  8.2 0.1 select_maximum_fusion.1
  8.3 0.0 copy-done.12
  8.3 0.2 fusion.10
  8.5 0.8 dynamic_slice.34
  9.3 0.6 pad.50.rows_ref
  9.9 1.0 constant_dynamic-slice_fusion.4
  10.9 0.8 pad.51.out_w_ref
  11.6 0.8 constant_dynamic-slice_fusion.5
  12.4 1.3 select_maximum_fusion.taps_ref
  13.7 0.0 copy-done.8
  13.7 0.6 broadcast_in_dim.21.gain_ref
  14.3 0.7 convert_reduce_fusion
  15.0 0.1 copy.64
  15.1 0.7 pad.44.named_ref
  15.8 47.4 %shard_map.366.in_ref.named_ref.one_ref = bf16[2048,1664]{1,0:T(8,128)(2,1)} custom-call(f32[64,1536]{1,0:T(8,128)} %in_ref.5, f32[1,1536]{1,0:T(1,128)} %broadcast_in_dim.21.gain_ref, bf16[64,128]{1,0:T(8,128)(2,1)} %pad.44.named_ref), custom_call_target="tpu_custom_call" | custom-call | tf_op jit(solution)/shard_map/pallas_call | solution.py:505
  63.2 0.0 copy-done.13
  63.2 0.7 reduce-window.9
  63.9 0.0 copy-done.4
  63.9 0.7 convert_element_type.65.grad_ref
  64.6 73.0 %shard_map.367 = (f32[2048,384]{1,0:T(8,128)}, f32[2048,128]{1,0:T(8,128)}, f32[2048,128]{1,0:T(8,128)}, f32[8,128,128]{2,1,0:T(8,128)}, f32[64,1664]{1,0:T(8,128)}, /*index=5*/bf16[2048,1536]{1,0:T(8,128)(2,1)}) custom-call(s32[4]{0:T(128)} %bitcast.43, bf16[2048,1664]{1,0:T(8,128)(2,1)} %shard_map.366.in_ref.named_ref.one_ref, ...), custom_call_target="tpu_custom_call" | custom-call | tf_op jit(solution)/shard_map/pallas_call | solution.py:706
  137.6 0.5 compare_convert_fusion.mine_ref
  138.1 3.3 constant_dynamic-slice_fusion
  141.4 1.0 copy_bitcast_fusion
  142.4 1.0 copy.68
  143.4 0.0 copy-start.2
  143.5 0.0 copy-start.3
  143.5 0.1 pad_slice_fusion
  143.6 1.8 copy.78
  145.3 0.0 copy-start.6
  145.4 0.0 copy-start.9
  145.4 2.1 fusion.5.up_ref
  147.5 0.0 copy-done
  147.5 0.1 pad.57.clone
  147.6 1.2 maximum_maximum_fusion.down_ref
  148.9 0.9 pad.52.router_ref
  149.8 0.0 copy-done.9
  149.8 0.6 broadcast_in_dim.24.gain_ref
  150.4 139.6 %shard_map.368 = (bf16[2048,1664]{1,0:T(8,128)(2,1)}, f32[64,1536]{1,0:T(8,128)}, f32[64,1536]{1,0:T(8,128)}, f32[1,1536]{1,0:T(1,128)}, bf16[1536,128]{1,0:T(8,...) custom-call(f32[64,1664]{1,0:T(8,128)} %get-tuple-element.55.total_r, ...), custom_call_target="tpu_custom_call" | custom-call | tf_op jit(solution)/shard_map/pallas_call | solution.py:1278
  290.0 0.1 copy.69
  290.1 0.7 pad.54.cols_ref
  290.9 109.3 %shard_map.369 = (f32[64,1536]{1,0:T(8,128)}, f32[64,1536]{1,0:T(8,128)}, f32[48,384]{1,0:T(8,128)}, f32[4,96,128]{2,1,0:T(8,128)}, bf16[8,112,384]{2,1,0:T(8,128)(2,1)}, /*index=5*/bf16[8,96,192]{2,1,0:T(8,128)(2,1)}) custom-call(s32[4]{0:T(128)} %bitcast.44, bf16[2048,1664]{1,0:T(8,128)(2,1)} %get-tuple-element.57.three_ref, ...), custom_call_target="tpu_custom_call" | custom-call | tf_op jit(solution)/shard_map/pallas_call | solution.py:1010
  400.2 0.0 copy-start.1
  400.2 8.7 %shard_map.370 = (f32[192,2,768]{2,1,0:T(2,128)}, f32[12,192]{1,0:T(8,128)}, f32[192,768]{1,0:T(8,128)}, f32[48,2,1024]{2,1,0:T(2,128)}, f32[48,1024]{1,0:T(8,12...) custom-call(bf16[8,112,384]{2,1,0:T(8,128)(2,1)} %get-tuple-element., ...), custom_call_target="tpu_custom_call" | custom-call | tf_op jit(solution)/shard_map/pallas_call | solution.py:1372
  408.9 1.3 reduce
  410.2 1.3 reduce.1
  411.5 1.3 slice_bitcast_fusion
  412.8 0.6 slice.37
  413.4 0.1 slice.41
  413.5 0.7 copy.70
  (14 shorter events, 0.1 us)
Async XLA Ops:
  0.7 146.9 %copy-start = (bf16[1024,1536]{1,0:T(8,128)(2,1)S(1)}, bf16[1024,1536]{1,0:T(8,128)(2,1)}, u32[]{:S(2)}) copy-start(bf16[1024,1536]{1,0:T(8,128)(2,1)} %param.40) | copy-start | bytes 9437188
  1.9 4.7 %copy-start.5 = (bf16[1536,256]{1,0:T(8,128)(2,1)S(1)}, bf16[1536,256]{1,0:T(8,128)(2,1)}, u32[]{:S(2)}) copy-start(bf16[1536,256]{1,0:T(8,128)(2,1)} %param.26) | copy-start | bytes 2359300
  6.5 1.6 copy-start.10
  6.5 1.6 copy-start.11
  6.5 1.8 copy-start.12
  6.5 7.2 %copy-start.8 = (f32[1536]{0:T(1024)S(1)}, f32[1536]{0:T(1024)}, u32[]{:S(2)}) copy-start(f32[1536]{0:T(1024)} %param.24) | copy-start | bytes 18436
  15.8 47.4 %copy-start.13 = (s32[4]{0:T(128)S(1)}, s32[4]{0:T(128)}, u32[]{:S(2)}) copy-start(s32[4]{0:T(128)} %param.42) | copy-start | bytes 52
  15.8 48.1 %copy-start.4 = (f32[64,1536]{1,0:T(8,128)S(1)}, f32[64,1536]{1,0:T(8,128)}, u32[]{:S(2)}) copy-start(f32[64,1536]{1,0:T(8,128)} %ograd_ref.1) | copy-start | bytes 1179652
  143.4 1.9 copy-start.2
  143.5 1.9 copy-start.3
  145.3 2.3 copy-start.6
  145.4 4.4 %copy-start.9 = (f32[1536]{0:T(1024)S(1)}, f32[1536]{0:T(1024)}, u32[]{:S(2)}) copy-start(f32[1536]{0:T(1024)} %param.35) | copy-start | bytes 18436
  400.2 14.0 %copy-start.1 = (bf16[1024,1536]{1,0:T(8,128)(2,1)S(1)}, bf16[1024,1536]{1,0:T(8,128)(2,1)}, u32[]{:S(2)}) copy-start(bf16[1024,1536]{1,0:T(8,128)(2,1)} %param.40) | copy-start | bytes 9437188
  400.2 12.6 %copy-start.7 = (f32[48,384]{1,0:T(8,128)S(1)}, f32[48,384]{1,0:T(8,128)}, u32[]{:S(2)}) copy-start(f32[48,384]{1,0:T(8,128)} %get-tuple-element.79) | copy-start | bytes 221188

commit v5 on v4

--- a/solution.py
+++ b/solution.py
@@ -486,36 +486,124 @@
     return part.reshape(Z, Y, X, 2, part.shape[0] // (S * H), part.shape[1])
 
 
-def first_kernel(S, H, in_ref, gain_ref, named_ref, out_ref, rows, send, recv, own_sem):
+def first_kernel(
+    S, H, C, FS, size, in_ref, gain_ref, routes_ref, conv_ref, conv_bc_ref, gate_ref, zx_ref, bc_ref, dt_ref, up_ref, router_ref,
+    shared_ref, bias_ref, alog_ref, skip_ref,
+    out_ref, rows_ref, taps_ref, cols_ref, in_w_ref, up_w_ref, rows, window, zx_own, up_own, send, recv, own_sem, window_sem,
+):
     pc = Place(S, H)
-    D = in_ref.shape[1]
+    R, D = in_ref.shape
+    base = pl.multiple_of(pc.slot() * FS // LANES * LANES, LANES)
+    fetch = pltpu.make_async_copy(shared_ref.at[:, :, pl.ds(base, LANES)], window, window_sem.at[0])
+    fetch_zx = pltpu.make_async_copy(zx_ref, zx_own, window_sem.at[1])
+    fetch_up = pltpu.make_async_copy(up_ref, up_own, window_sem.at[2])
+    for copy in (fetch_zx, fetch_up, fetch):
+        copy.start()
     values = in_ref[...]
-    rows[:, :D] = (values * inverse_rms(values) * gain_ref[...]).astype(B16)
-    rows[:, D:] = named_ref[...]
+    rows[:, :D] = (values * inverse_rms(values) * gain_ref[...].reshape(1, D)).astype(B16)
+    line = lax.broadcasted_iota(jnp.int32, (LANES, R), 0)
+    named = jnp.zeros((LANES, R), F32)
+    for k in range(routes_ref.shape[0]):
+        named = named + (routes_ref[k : k + 1, :] == line - FS).astype(F32)
+    rows[:, D:] = named.T.astype(B16)
     mail = Mail(send, recv)
     moves = gather(pc, mail, rows, out_ref, own_sem)
     greet(pc.peers())
-    moves.run()
+    moves.run(0, 1)
+
+    heads, inner, width = bias_ref.shape[0], conv_ref.shape[1], rows_ref.shape[1]
+    start = lax.axis_index("seq") * C
+    first = jnp.minimum(start // size, heads - 2)
+    lane = lax.broadcasted_iota(jnp.int32, (1, width), 1)
+    masks = []
+    for j in range(2):
+        low = (first + j) * size - start
+        masks.append(((lane < C) & (lane >= low) & (lane < low + size)).astype(F32))
+    cut = (
+        lax.broadcasted_iota(jnp.int32, (inner, width), 0) == start + lax.broadcasted_iota(jnp.int32, (inner, width), 1)
+    ) & (lax.broadcasted_iota(jnp.int32, (inner, width), 1) < C)
+    ours = exact(jnp.concatenate([conv_ref[...], gate_ref[...].reshape(1, inner), jnp.zeros((3, inner), F32)], axis=0), cut.astype(F32))
+    taps_ref[:, :width] = ours[0:4, :]
+    taps_ref[:, width:] = conv_bc_ref[...]
+
+    def pair(ref):
+        return jnp.where(lane == C, ref[first], ref[first + 1])
+
+    free = (lane == C) | (lane == C + 1)
+    rows_ref[0:1, :] = masks[0]
+    rows_ref[1:2, :] = masks[1]
+    rows_ref[2:3, :] = skip_ref[first] * masks[0] + skip_ref[first + 1] * masks[1]
+    rows_ref[3:4, :] = ours[4:5, :]
+    rows_ref[4:5, :] = jnp.where(free, pair(bias_ref), 0.0)
+    rows_ref[5:6, :] = jnp.where(free, jnp.exp(pair(alog_ref)), 0.0)
+    rows_ref[6:8, :] = jnp.zeros((2, width), F32)
+    channel = lax.broadcasted_iota(jnp.int32, cols_ref.shape, 0)
+    slot = lax.broadcasted_iota(jnp.int32, cols_ref.shape, 1) - C
+    low = (first + slot) * size - start
+    cols_ref[...] = (
+        (slot >= 0) & (slot < 2) & (channel < C) & (channel >= low) & (channel < low + size)
+    ).astype(F32)
+    moves.run(1, 2)
+
+    def take(depth, at):
+        row = lax.broadcasted_iota(jnp.int32, (depth, width), 0)
+        col = lax.broadcasted_iota(jnp.int32, (depth, width), 1)
+        return at(row, col).astype(B16)
+
+    fetch_zx.wait()
+    zx = zx_own[...].reshape(D, 2 * inner)
+    ours = take(inner, lambda row, col: (row == start + col) & (col < C))
+    steps = take(heads, lambda row, col: (row - first == col - C) & (col >= C) & (col < C + 2))
+    in_w_ref[:, :width] = (mm(zx[:, :inner], ours) + mm(dt_ref[...], steps, TN)).astype(B16)
+    in_w_ref[:, width : 2 * width] = mm(zx[:, inner:], ours).astype(B16)
+    in_w_ref[:, 2 * width :] = bc_ref[...]
+    moves.run(2, 3)
+    up = 2 * up_ref.shape[2]
+    fetch_up.wait()
+    up_w_ref[:, :up] = up_own[...].reshape(D, up)
+    fetch.wait()
+    shared = window[...].reshape(D, 2 * LANES)
+    offset = pc.slot() * FS - base
+    units = take(LANES, lambda row, col: (row == offset + col) & (col < FS))
+    names = take(router_ref.shape[0], lambda row, col: col == FS + row)
+    up_w_ref[:, up : up + LANES] = (mm(shared[:, :LANES], units) + mm(router_ref[...], names, TN)).astype(B16)
+    up_w_ref[:, up + LANES :] = mm(shared[:, LANES:], units).astype(B16)
+    moves.run(3)
     mail.finish(gather_count(S, H))
 
 
-def first_rows(hidden_in, gain, named, S, H):
+def first_rows(
+    hidden_in, gain, routes, conv_x, conv_bc, gate, w_zx, w_bc, w_dt, up, router, shared, bias, alog, skip, C, CP, FS, S, H
+):
     R, D = hidden_in.shape
+    assert CP == LANES and LANES % FS == 0
     W = D + LANES
+    scalars = pl.BlockSpec(memory_space=pltpu.SMEM)
     return pl.pallas_call(
-        functools.partial(first_kernel, S, H),
-        out_shape=jax.ShapeDtypeStruct((S * H * R, W), B16),
-        in_specs=[VMEM] * 3,
-        out_specs=ANY,
-        scratch_shapes=[pltpu.VMEM((R, W), B16), *sems(gather_count(S, H)), pltpu.SemaphoreType.DMA],
+        functools.partial(first_kernel, S, H, C, FS, conv_x.shape[1] // bias.shape[0]),
+        out_shape=[
+            jax.ShapeDtypeStruct((S * H * R, W), B16),
+            jax.ShapeDtypeStruct((8, CP), F32),
+            jax.ShapeDtypeStruct((4, CP + conv_bc.shape[1]), F32),
+            jax.ShapeDtypeStruct((CP, LANES), F32),
+            jax.ShapeDtypeStruct((D, 2 * CP + w_bc.shape[1]), B16),
+            jax.ShapeDtypeStruct((D, 2 * up.shape[2] + 2 * LANES), B16),
+        ],
+        in_specs=[VMEM] * 6 + [ANY, VMEM, VMEM, ANY, VMEM, ANY] + [scalars] * 3,
+        out_specs=[ANY] + [VMEM] * 5,
+        scratch_shapes=[
+            pltpu.VMEM((R, W), B16), pltpu.VMEM((D, 2, LANES), B16), pltpu.VMEM(w_zx.shape, B16), pltpu.VMEM(up.shape, B16),
+            *sems(gather_count(S, H)), pltpu.SemaphoreType.DMA, pltpu.SemaphoreType.DMA((3,)),
+        ],
         compiler_params=talking(1),
-    )(hidden_in, gain, named)
-
-
-def seg_of(pos, ends_ref, count):
-    found = jnp.zeros(pos.shape, jnp.int32)
+    )(hidden_in, gain, routes, conv_x, conv_bc, gate, w_zx, w_bc, w_dt, up, router, shared, bias, alog, skip)
+
+
+def seg_of(pos, lengths_ref, count):
+    found, end = jnp.zeros(pos.shape, jnp.int32), 0
     for k in range(count):
-        found = found + (pos >= ends_ref[k]).astype(jnp.int32)
+        end = end + lengths_ref[k]
+        found = found + (pos >= end).astype(jnp.int32)
     return jnp.where(pos < 0, -1, found)
 
 
@@ -532,13 +620,13 @@
 
 
 class Block:
-    def __init__(self, i, pre, ext, z, taps_ref, rows_ref, ends_ref, count, state, C):
+    def __init__(self, i, pre, ext, z, taps_ref, rows_ref, lengths_ref, count, state, C):
         n = BLOCK
-        pos = i * n + lax.broadcasted_iota(jnp.int32, (n, 1), 0)
         pos_row = i * n + lax.broadcasted_iota(jnp.int32, (1, n), 1)
-        seg, seg_row = seg_of(pos, ends_ref, count), seg_of(pos_row, ends_ref, count)
-        self.joined = {k: ((pos >= k) & (seg_of(pos - k, ends_ref, count) == seg)).astype(F32) for k in (1, 2, 3)}
-        self.later = {k: (seg_of(pos + k, ends_ref, count) == seg).astype(F32) for k in (1, 2, 3)}
+        around = seg_of(i * n - 8 + lax.broadcasted_iota(jnp.int32, (n + 16, 1), 0), lengths_ref, count)
+        seg, seg_row = around[8 : 8 + n], seg_of(pos_row, lengths_ref, count)
+        self.joined = {k: (around[8 - k : 8 - k + n] == seg).astype(F32) for k in (1, 2, 3)}
+        self.later = {k: (around[8 + k : 8 + k + n] == seg).astype(F32) for k in (1, 2, 3)}
         conv = taps_ref[3:4, :] * pre
         for k in (1, 2, 3):
             conv = conv + taps_ref[3 - k : 4 - k, :] * ext[8 - k : 8 - k + n, :] * self.joined[k]
@@ -564,8 +652,8 @@
         ]
         scores = mm(self.c, self.b, NT)
         self.mats = [(scores * d).astype(B16) for d in self.decays]
-        before = jnp.where(i == 0, -1, seg_of(jnp.full((1, 1), i * n - 1, jnp.int32), ends_ref, count))
-        final = seg_of(jnp.full((1, 1), i * n + n - 1, jnp.int32), ends_ref, count)
+        before = jnp.where(i == 0, -1, seg_of(jnp.full((1, 1), i * n - 1, jnp.int32), lengths_ref, count))
+        final = seg_of(jnp.full((1, 1), i * n + n - 1, jnp.int32), lengths_ref, count)
         last = logdec[n - 1 : n, :]
         self.carry = self.spread(jnp.where(seg == before, jnp.exp(logdec), 0.0))
         self.tail = self.spread(jnp.where(seg == final, jnp.exp(last - logdec), 0.0))
@@ -584,8 +672,8 @@
 
 
 def mixer_forward_kernel(
-    S, H, count, state, C, ends_ref, in_ref, w_ref, taps_ref, rows_ref, out_w_ref, grad_ref,
-    pre_ref, z_ref, y_ref, st_ref, total_ref, all_ref, held, ext, parts, *rest,
+    S, H, count, state, C, lengths_ref, in_ref, w_ref, taps_ref, rows_ref, out_w_ref, grad_ref,
+    pre_ref, z_ref, y_ref, st_ref, total_ref, all_ref, held, ext, parts, grad_low, *rest,
 ):
     i = pl.program_id(0)
     pc = Place(S, H)
@@ -593,7 +681,7 @@
     X, Y, Z = pc.X, pc.Y, pc.Z
     R = grad_ref.shape[0]
     mail = Mail(send, recv)
-    moves = gather(pc, mail, grad_ref, all_ref, own_sem)
+    moves = gather(pc, mail, grad_low, all_ref, own_sem)
     acts = Script()
     sums = Sum(
         pc, mail, acts, lambda dz, yy, xx, rows: parts.at[dz, yy, xx, pc.c, rows], lambda dz: parts.at[dz, :, :, 1 - pc.c],
@@ -625,6 +713,7 @@
 
     @pl.when(i == 0)
     def _():
+        grad_low[...] = grad_ref[...].astype(B16)
         greet(pc.peers(direct=True))
         moves.run(0, 1)
 
@@ -655,7 +744,7 @@
     pre = made[:, cp:]
     z_ref[...], pre_ref[...] = z, pre
     ext[8 : 8 + n, :] = pre
-    blk = Block(i, pre, ext, z, taps_ref, rows_ref, ends_ref, count, state, C)
+    blk = Block(i, pre, ext, z, taps_ref, rows_ref, lengths_ref, count, state, C)
     ext[0:8, :] = pre[n - 8 :, :]
     st = held[...]
     st_ref[0] = st
@@ -693,7 +782,7 @@
     return pltpu.CompilerParams(dimension_semantics=("arbitrary",), vmem_limit_bytes=60 * 1024 * 1024)
 
 
-def mixer_forward(ends, gathered, in_w, taps, rows, out_w, grad, state, C, S, H):
+def mixer_forward(lengths, gathered, in_w, taps, rows, out_w, grad, state, C, S, H):
     T, depth = gathered.shape[0], in_w.shape[0]
     X, Y, Z = sizes(S, H)
     R = grad.shape[0]
@@ -704,7 +793,7 @@
         return pl.BlockSpec((BLOCK, width), lambda i: (i, 0))
 
     return pl.pallas_call(
-        functools.partial(mixer_forward_kernel, S, H, ends.shape[0], state, C),
+        functools.partial(mixer_forward_kernel, S, H, lengths.shape[0], state, C),
         grid=(nb,),
         in_specs=[
             pl.BlockSpec(memory_space=pltpu.SMEM), block(gathered.shape[1]), whole(in_w.shape), whole(taps.shape),
@@ -724,16 +813,16 @@
         ],
         scratch_shapes=[
             pltpu.VMEM((state, cp), F32), pltpu.VMEM((BLOCK + 8, conv_width), F32),
-            pltpu.VMEM((Z, Y, X, 2, R, depth + LANES), B16), *sum_scratch(S, H, R, depth + LANES),
+            pltpu.VMEM((Z, Y, X, 2, R, depth + LANES), B16), pltpu.VMEM((R, depth), B16), *sum_scratch(S, H, R, depth + LANES),
             *sems(gather_count(S, H) + scatter_count(S, H) - 3),
             pltpu.SemaphoreType.DMA((4,)), pltpu.SemaphoreType.DMA((3,)), pltpu.SemaphoreType.DMA,
         ],
         compiler_params=talking(5),
-    )(ends, gathered, in_w, taps, rows, out_w, grad)
+    )(lengths, gathered, in_w, taps, rows, out_w, grad)
 
 
 def mixer_backward_kernel(
-    S, H, beside, count, state, C, ends_ref, three_ref, one_ref, pre_ref, halo_ref, z_ref, y_ref, st_ref,
+    S, H, beside, count, state, C, lengths_ref, three_ref, one_ref, pre_ref, halo_ref, z_ref, y_ref, st_ref,
     w_ref, taps_ref, rows_ref, cols_ref, out_w_ref, p_ref, res_ref, gres_ref, in_ref, gain_ref, norm2_ref, router_ref,
     output_ref, gin_ref, extra_ref, small_out, zx_out, wo_out,
     held, ext, gext, gw_ref, gout_ref, gtaps_ref, gvec_ref, gnorm_ref, total, parts, extra, zx_ref, wo_ref, small, joint,
@@ -859,7 +948,7 @@
     pre, z, y = pre_ref[...], z_ref[...], y_ref[...]
     ext[0:8, :] = jnp.where(i == 0, 0.0, halo_ref[...])
     ext[8 : 8 + n, :] = pre
-    blk = Block(i, pre, ext, z, taps_ref, rows_ref, ends_ref, count, state, C)
+    blk = Block(i, pre, ext, z, taps_ref, rows_ref, lengths_ref, count, state, C)
     three = three_ref[:, :depth]
     pg = mm(three, out_w_ref[...], NT)
     cross = jnp.sum(three_ref[:, depth:].astype(F32), axis=1, keepdims=True)
@@ -970,7 +1059,7 @@
         sides.run(3)
         acts.run(4 * Z)
         values, gone = in_ref[...], total[...]
-        gin_ref[...] = gres_ref[...] + rms_back(values, inverse_rms(values), gain_ref[...], gone)
+        gin_ref[...] = gres_ref[...] + rms_back(values, inverse_rms(values), gain_ref[...].reshape(1, depth), gone)
         for copy in row:
             copy.wait()
         for copy in column:
@@ -983,7 +1072,7 @@
 
 
 def mixer_backward(
-    ends, three, one, pre, z, y, states, in_w, taps, rows, cols, out_w, out_part, residual, grad_res, hidden_in, gain,
+    lengths, three, one, pre, z, y, states, in_w, taps, rows, cols, out_w, out_part, residual, grad_res, hidden_in, gain,
     norm2, router_part, state, C, S, H,
 ):
     T, depth = three.shape[0], in_w.shape[0]
@@ -1008,7 +1097,7 @@
         return (jnp.maximum((nb - 1 - k) * (BLOCK // 8) - 1, 0), 0)
 
     return pl.pallas_call(
-        functools.partial(mixer_backward_kernel, S, H, beside, ends.shape[0], state, C),
+        functools.partial(mixer_backward_kernel, S, H, beside, lengths.shape[0], state, C),
         grid=(nb,),
         in_specs=[
             pl.BlockSpec(memory_space=pltpu.SMEM), block(three.shape[1]), block(one.shape[1], kept), block(conv_width, kept),
@@ -1052,7 +1141,7 @@
         ],
         compiler_params=talking(6),
     )(
-        ends, three, one, pre, pre, z, y, states, in_w, taps, rows, cols, out_w, blocks(out_part, S, H), residual,
+        lengths, three, one, pre, pre, z, y, states, in_w, taps, rows, cols, out_w, blocks(out_part, S, H), residual,
         grad_res, hidden_in, gain, norm2, router_part,
     )
 
@@ -1086,7 +1175,7 @@
 
 
 def expert_kernel(
-    S, H, F, width, total_ref, in_ref, gain_ref, grad_ref, named_ref, up_ref, down_ref, mine_ref, router_ref, ograd_ref,
+    S, H, F, width, total_ref, in_ref, gain_ref, grad_ref, named_ref, up_ref, down_ref, mine_ref, ograd_ref,
     three_ref, res_ref, gres_ref, gnorm_ref, grouter_ref, out_ref, gup_out, gdown_ref, sh_out,
     gup_ref, total, rows, two, grads, names, parts, stage_out, probs, gs_ref, *rest,
 ):
@@ -1149,7 +1238,7 @@
 
     for copy in loads(0, 0):
         copy.start()
-    gain = gain_ref[...]
+    gain = gain_ref[...].reshape(1, D)
     mixed = total_ref[:, :D]
     square = jnp.sum(total_ref[:, D:], axis=1, keepdims=True)
     inv = lax.rsqrt(square / width + EPS)
@@ -1246,7 +1335,7 @@
     acts.run(4 * Z)
     gp = total[:, D:]
     glogits = (p * (gp - jnp.sum(p * gp, axis=1, keepdims=True))).astype(B16)
-    gtwo = total[:, :D] + mm(glogits, router_ref[...], NT)
+    gtwo = total[:, :D] + mm(glogits, up_ref[:, 2 * F : 2 * F + LANES], NT)
     residual = res_ref[...]
     inv_two = inverse_rms(residual)
     gres = ograd_ref[...] + rms_back(residual, inv_two, gain, gtwo)
@@ -1269,7 +1358,7 @@
     mail2.finish(2 * gather_count(S, H) + scatter_count(S, H))
 
 
-def experts(total, hidden_in, gain, all_grad, gathered, up_w, down_w, mine, router, out_grad, F, FS, width, S, H):
+def experts(total, hidden_in, gain, all_grad, gathered, up_w, down_w, mine, out_grad, F, FS, width, S, H):
     R, D = hidden_in.shape
     X, Y, Z = sizes(S, H)
     T, W = S * H * R, D + LANES
@@ -1288,7 +1377,7 @@
             jax.ShapeDtypeStruct((F, D), F32),
             jax.ShapeDtypeStruct((S * H, tall, 3 * FS), B16),
         ],
-        in_specs=[VMEM, VMEM, VMEM, ANY, ANY] + [VMEM] * 5,
+        in_specs=[VMEM, VMEM, VMEM, ANY, ANY] + [VMEM] * 4,
         out_specs=[ANY] + [VMEM] * 4 + [ANY] + [VMEM] * 2 + [ANY],
         scratch_shapes=[
             pltpu.VMEM((D, 2 * F), F32), pltpu.VMEM((R, W), F32), pltpu.VMEM((R, D), B16), pltpu.VMEM((T, D), B16),
@@ -1301,7 +1390,7 @@
             pltpu.SemaphoreType.DMA((2,)), pltpu.SemaphoreType.DMA((2,)),
         ],
         compiler_params=talking(2),
-    )(total, hidden_in, gain, all_grad, gathered, up_w, down_w, mine, router, out_grad)
+    )(total, hidden_in, gain, all_grad, gathered, up_w, down_w, mine, out_grad)
 
 
 def finish_kernel(
@@ -1335,13 +1424,14 @@
         for k in range(2):
             up_out[:, k, at] = piece[:, k * FS : (k + 1) * FS]
         down_out[:, at] = piece[:, 2 * FS :]
-    lines = gain_ref.shape[1] // LANES
+    gain = gain_ref[...].reshape(1, gain_ref.shape[0])
+    lines = gain.shape[1] // LANES
     total = small_ref[0, : 2 * lines + 4 * (2 * state // LANES), :]
     for h in range(1, H):
         total = total + small_ref[h, : total.shape[0], :]
     for j in range(lines):
         at = slice(j * LANES, (j + 1) * LANES)
-        norm1_out[:, at] = total[j : j + 1, :] / gain_ref[:, at]
+        norm1_out[:, at] = total[j : j + 1, :] / gain[:, at]
         norm2_out[:, at] = total[lines + j : lines + j + 1, :]
     line = 2 * lines
     for r in range(4):
@@ -1363,7 +1453,7 @@
 
 
 def finish(zx, wo, shared, small, pick, gain, made, C, FS, state, S, H):
-    N, wide, heads, D = S * H, wo.shape[2], pick.shape[2], gain.shape[1]
+    N, wide, heads, D = S * H, wo.shape[2], pick.shape[2], gain.shape[0]
     per = D // N
     shapes = (
         (wide, 2, S * C), (heads, wide), (wide, S * C), (per, 2, N * FS), (per, N * FS), (1, D), (1, D), (4, S * H * C),
@@ -1400,19 +1490,13 @@
     FS = shared_down.shape[0] // N
     per = D // N
 
-    named = jnp.sum(
-        (routes[:, :, None] == jnp.arange(E, dtype=jnp.int32)[None, None, :]).astype(F32), axis=1
+    gain1, gain2 = norm1_gain, norm2_gain
+    gathered, rows, taps, cols, in_w, up_w = first_rows(
+        hidden_in, gain1, routes.T, conv_x, conv_bc, gate_gain, w_zx, w_bc, w_dt.T, expert_up[0], router.T, shared_up,
+        dt_bias, a_log, d_skip, C, CP, FS, S, H
     )
-    named = jnp.pad(named.astype(B16), ((0, 0), (FS, LANES - FS - E)))
-    gain1, gain2 = norm1_gain[None], norm2_gain[None]
-    gathered = first_rows(hidden_in, gain1, named, S, H)
 
     firsts = [min(k * C // size, heads - 2) for k in range(S)]
-    first = jnp.minimum(s * C // size, heads - 2)
-    channel = jnp.arange(CP)
-    masks = jnp.stack(
-        [((channel < C) & ((s * C + channel) // size - first == j)).astype(F32) for j in range(2)]
-    )
 
     def mine(values, axis, offset, length):
         return lax.dynamic_slice_in_dim(values, offset, length, axis)
@@ -1423,47 +1507,20 @@
         pads[axis] = (0, CP - C)
         return jnp.pad(cut, pads)
 
-    def in_free(values):
-        return jnp.pad(values, [(0, 0)] * (values.ndim - 1) + [(C, CP - C - 2)])
-
-    zx_w = mine(w_zx, 2, s * C, C)
-    in_w = jnp.concatenate(
-        [
-            zx_w[:, 0], pad_lanes(mine(w_dt, 1, first, 2), CP - C), pad_lanes(zx_w[:, 1], CP), w_bc,
-        ],
-        axis=1,
+    out_w = channels(w_out, 0)
+
+    pre, z, y, states, mixed, all_grad = mixer_forward(
+        seq_lengths, gathered, in_w, taps, rows, out_w, out_grad, state, C, S, H
     )
-    taps = jnp.concatenate([channels(conv_x, 1), conv_bc], axis=1)
-    bias, alog, skip = (mine(v, 0, first, 2) for v in (dt_bias, a_log, d_skip))
-    gain = channels(gate_gain, 0)
-    out_w = channels(w_out, 0)
-    rows = jnp.concatenate(
-        [masks, (skip @ masks)[None], gain[None], in_free(jnp.stack([bias, jnp.exp(alog)]))], axis=0
-    )
-    rows = jnp.pad(rows, ((0, 2), (0, 0)))
-    cols = in_free(masks.T)
-    ends = jnp.cumsum(seq_lengths)
-
-    pre, z, y, states, mixed, all_grad = mixer_forward(
-        ends, gathered, in_w, taps, rows, out_w, out_grad.astype(B16), state, C, S, H
-    )
-
-    sup = mine(shared_up, 2, g * FS, FS)
-    router_w = jnp.pad(router, ((0, 0), (FS, LANES - FS - E)))
-    up_w = jnp.concatenate(
-        [
-            expert_up[0].reshape(D, 2 * F), sup[:, 0], router_w[:, FS:], pad_lanes(sup[:, 1], LANES),
-        ],
-        axis=1,
-    )
+
     down_w = jnp.concatenate([expert_down[0], mine(shared_down, 0, g * FS, FS), jnp.zeros((LANES - FS, D), B16)], axis=0)
     is_mine = (jnp.arange(LANES) == FS + g // 2).astype(F32)[None]
     three, residual, grad_res, norm2_part, router_part, out_part, grad_up, grad_down, sh_in = experts(
-        mixed, hidden_in, gain2, all_grad, gathered, up_w, down_w, is_mine, router_w, out_grad, F, FS, width, S, H
+        mixed, hidden_in, gain2, all_grad, gathered, up_w, down_w, is_mine, out_grad, F, FS, width, S, H
     )
 
     output, grad_in, extra_sum, small, zx_in, wo_in = mixer_backward(
-        ends, three, gathered, pre, z, y, states, in_w, taps, rows, cols, out_w, out_part, residual,
+        seq_lengths, three, gathered, pre, z, y, states, in_w, taps, rows, cols, out_w, out_part, residual,
         grad_res, hidden_in, gain1, norm2_part, router_part, state, C, S, H,
     )
     if H > 4:

time: 415 us -> 395 us (0.952)
  local copies, waits for them, and re-layouts: 23.6 us -> 7.34 us
  other arithmetic: 11.4 us -> 5.51 us
    slice x3 -> x0, local copies, waits for them, and re-layouts: 7.91 us -> none  [the longest x1 4.51 us: local(): zx_w[:, 0]]
    concatenate x3 -> x0, other arithmetic: 4.87 us -> none  [the longest x1 2.12 us: local(): jnp.concatenate([expert_up[0].reshape(D, 2 * F), sup[:, 0], router_w[:, F...]
where the time goes in v5:
time: 395 us; the launch traced here: 394 us
  Pallas kernels  381 us (96%)
  local copies, waits for them, and re-layouts  7.34 us (2%)
  other arithmetic  5.51 us (1%)
    pallas_call x1, Pallas kernels, experts(): pl.pallas_call(functools.partial(expert_kernel, S, H, F, width), out_shap...  139 us
    pallas_call x1, Pallas kernels, mixer_backward(): pl.pallas_call(functools.partial(mixer_backward_kernel, S, H, beside, len...  109 us
    pallas_call x1, Pallas kernels, mixer_forward(): pl.pallas_call(functools.partial(mixer_forward_kernel, S, H, lengths.shap...  73.8 us
    pallas_call x1, Pallas kernels, first_rows(): pl.pallas_call(functools.partial(first_kernel, S, H, C, FS, conv_x.shape[...  49.8 us
    pallas_call x1, Pallas kernels, finish(): pl.pallas_call(functools.partial(finish_kernel, S, H, C, FS, state), out_...  8.77 us

profile of v5, /device:TPU:0, one launch (start us, length us, event | category | flops | bytes accessed | tf_op | source)
XLA Modules:
  0.0 394.5 jit_solution(18370266129417050934)
XLA Ops:
  0.7 0.0 copy-start
  0.7 0.5 compare_convert_fusion.mine_ref
  1.2 0.1 pad.7.clone
  1.3 1.3 copy-done
  2.6 1.0 constant_dynamic-slice_fusion.1
  3.5 0.8 pad.4.out_w_ref
  4.3 2.4 maximum_maximum_fusion.down_ref
  6.7 49.8 %shard_map.366 = (bf16[2048,1664]{1,0:T(8,128)(2,1)}, f32[8,128]{1,0:T(8,128)}, f32[4,384]{1,0:T(4,128)}, f32[128,128]{1,0:T(8,128)}, bf16[1536,512]{1,0:T(8,128)(2,1)}, /*index=5*/bf16[1536,768]{1,0:T(8,128)(2,1)}) custom-call(f32[64,1536]{1,0:T(8,128)} %in_ref.5, f32[1536]{0:T(1024)} %gain_ref.7, s32[6,64]{1,0:T(8,128)} %bitcast.23, f32[4,768]{1,0:T(4,128)} %conv_ref.1, ...), custom_call_target="tpu_custom_call" | custom-call | tf_op jit(solution)/shard_map/pallas_call | solution.py:582
  56.5 73.8 %shard_map.367 = (f32[2048,384]{1,0:T(8,128)}, f32[2048,128]{1,0:T(8,128)}, f32[2048,128]{1,0:T(8,128)}, f32[8,128,128]{2,1,0:T(8,128)}, f32[64,1664]{1,0:T(8,128)}, /*index=5*/bf16[2048,1536]{1,0:T(8,128)(2,1)}) custom-call(s32[4]{0:T(128)} %lengths_ref.3, bf16[2048,1664]{1,0:T(8,128)(2,1)} %get-tuple-element.61.in_ref.named_ref.one_ref, ...), custom_call_target="tpu_custom_call" | custom-call | tf_op jit(solution)/shard_map/pallas_call | solution.py:795
  130.3 139.4 %shard_map.368 = (bf16[2048,1664]{1,0:T(8,128)(2,1)}, f32[64,1536]{1,0:T(8,128)}, f32[64,1536]{1,0:T(8,128)}, f32[1,1536]{1,0:T(1,128)}, bf16[1536,128]{1,0:T(8,...) custom-call(f32[64,1664]{1,0:T(8,128)} %get-tuple-element.65.total_r, ...), custom_call_target="tpu_custom_call" | custom-call | tf_op jit(solution)/shard_map/pallas_call | solution.py:1367
  269.7 109.1 %shard_map.369 = (f32[64,1536]{1,0:T(8,128)}, f32[64,1536]{1,0:T(8,128)}, f32[48,384]{1,0:T(8,128)}, f32[4,96,128]{2,1,0:T(8,128)}, bf16[8,112,384]{2,1,0:T(8,128)(2,1)}, /*index=5*/bf16[8,96,192]{2,1,0:T(8,128)(2,1)}) custom-call(s32[4]{0:T(128)} %lengths_ref.3, bf16[2048,1664]{1,0:T(8,128)(2,1)} %get-tuple-element.68.three_ref, ...), custom_call_target="tpu_custom_call" | custom-call | tf_op jit(solution)/shard_map/pallas_call | solution.py:1099
  378.9 0.8 slice.21
  379.7 1.4 slice.17
  381.1 0.0 copy-start.1
  381.1 0.7 copy.42
  381.8 8.8 %shard_map.370 = (f32[192,2,768]{2,1,0:T(2,128)}, f32[12,192]{1,0:T(8,128)}, f32[192,768]{1,0:T(8,128)}, f32[48,2,1024]{2,1,0:T(2,128)}, f32[48,1024]{1,0:T(8,12...) custom-call(bf16[8,112,384]{2,1,0:T(8,128)(2,1)} %get-tuple-element., ...), custom_call_target="tpu_custom_call" | custom-call | tf_op jit(solution)/shard_map/pallas_call | solution.py:1462
  390.6 1.3 slice_bitcast_fusion
  391.9 1.3 reduce
  393.2 1.3 reduce.1
  394.5 0.0 copy-done.1
  (2 shorter events, 0.0 us)
Async XLA Ops:
  0.7 1.9 copy-start
  381.1 13.4 %copy-start.1 = (bf16[1024,1536]{1,0:T(8,128)(2,1)S(1)}, bf16[1024,1536]{1,0:T(8,128)(2,1)}, u32[]{:S(2)}) copy-start(bf16[1024,1536]{1,0:T(8,128)(2,1)} %param.40) | copy-start | bytes 9437188

commit v6 on v5

--- a/solution.py
+++ b/solution.py
@@ -88,11 +88,13 @@
         return out + [self.dev(dc=1)]
 
 
-def greet(peers):
-    barrier = pltpu.get_barrier_semaphore()
+def hail(peers):
     for peer in peers:
-        pl.semaphore_signal(barrier, inc=1, device_id=peer, device_id_type=MESH)
-    pl.semaphore_wait(barrier, len(peers))
+        pl.semaphore_signal(pltpu.get_barrier_semaphore(), inc=1, device_id=peer, device_id_type=MESH)
+
+
+def settle(count):
+    pl.semaphore_wait(pltpu.get_barrier_semaphore(), count)
 
 
 class Mail:
@@ -493,6 +495,8 @@
 ):
     pc = Place(S, H)
     R, D = in_ref.shape
+    peers = pc.peers()
+    hail(peers)
     base = pl.multiple_of(pc.slot() * FS // LANES * LANES, LANES)
     fetch = pltpu.make_async_copy(shared_ref.at[:, :, pl.ds(base, LANES)], window, window_sem.at[0])
     fetch_zx = pltpu.make_async_copy(zx_ref, zx_own, window_sem.at[1])
@@ -508,7 +512,7 @@
     rows[:, D:] = named.T.astype(B16)
     mail = Mail(send, recv)
     moves = gather(pc, mail, rows, out_ref, own_sem)
-    greet(pc.peers())
+    settle(len(peers))
     moves.run(0, 1)
 
     heads, inner, width = bias_ref.shape[0], conv_ref.shape[1], rows_ref.shape[1]
@@ -713,8 +717,10 @@
 
     @pl.when(i == 0)
     def _():
+        peers = pc.peers(direct=True)
+        hail(peers)
         grad_low[...] = grad_ref[...].astype(B16)
-        greet(pc.peers(direct=True))
+        settle(len(peers))
         moves.run(0, 1)
 
     for step, stage, until in ((1, 1, 2), (2, 2, 3), (3, 3, 5), (4, 5, 7), (5, 7, 9), (6, 9, 11)):
@@ -920,17 +926,8 @@
     final_acts = [entry for entry in final_acts if all(entry not in before[k] for k in before)]
     @pl.when(step == 0)
     def _():
+        hail([((seq + m) % S, head) for m in range(1, S)] + [(seq, (head + m) % H) for m in range(1, H)])
         sums.run(0, 1)
-        greet([((seq + m) % S, head) for m in range(1, S)] + [(seq, (head + m) % H) for m in range(1, H)])
-        sums.run(1, 2)
-
-    for at in range(1, total_steps):
-        if before[at]:
-
-            @pl.when(step == at)
-            def _():
-                for script, stage in before[at]:
-                    script.run(stage, stage + 1)
 
     @pl.when(step == 0)
     def _():
@@ -941,9 +938,19 @@
         extra[...] = jnp.zeros_like(extra)
         zx_ref[...] = jnp.zeros_like(zx_ref)
         wo_ref[...] = jnp.zeros_like(wo_ref)
+        settle(S + H - 2)
+        sums.run(1, 2)
         gout_ref[...] = jnp.zeros_like(gout_ref)
         gtaps_ref[...] = jnp.zeros_like(gtaps_ref)
         gvec_ref[...] = jnp.zeros_like(gvec_ref)
+
+    for at in range(1, total_steps):
+        if before[at]:
+
+            @pl.when(step == at)
+            def _():
+                for script, stage in before[at]:
+                    script.run(stage, stage + 1)
 
     pre, z, y = pre_ref[...], z_ref[...], y_ref[...]
     ext[0:8, :] = jnp.where(i == 0, 0.0, halo_ref[...])
@@ -1188,6 +1195,13 @@
     n = BLOCK
     N, me = S * H, pc.slot()
     mail2 = Mail(send2, recv2)
+
+    def hello(m, carry):
+        to = (me + m) % N
+        hail([(to // H, to % H)])
+        return carry
+
+    lax.fori_loop(1, N, hello, 0)
     stay = pltpu.make_async_copy(pieces.at[me], sh_out.at[me], sh_sem)
 
     def to_all(function):
@@ -1246,15 +1260,7 @@
     res_ref[...] = residual
     rows[...] = (residual * inverse_rms(residual) * gain).astype(B16)
     cube = inv * inv * inv / width
-    barrier = pltpu.get_barrier_semaphore()
-
-    def hello(m, carry):
-        to = (me + m) % N
-        pl.semaphore_signal(barrier, inc=1, device_id=(to // H, to % H), device_id_type=MESH)
-        return carry
-
-    lax.fori_loop(1, N, hello, 0)
-    pl.semaphore_wait(barrier, N - 1)
+    settle(N - 1)
     moves.run(0, 1)
     gup_ref[...] = jnp.zeros_like(gup_ref)
     gdown_ref[...] = jnp.zeros_like(gdown_ref)

time: 395 us -> 394 us (level)
  no operation moved by 1% of the time
where the time goes in v6:
time: 394 us
  Pallas kernels  380 us (96%)
  local copies, waits for them, and re-layouts  7.34 us (2%)
  other arithmetic  5.51 us (1%)
    pallas_call x1, Pallas kernels, experts(): pl.pallas_call(functools.partial(expert_kernel, S, H, F, width), out_shap...  138 us
    pallas_call x1, Pallas kernels, mixer_backward(): pl.pallas_call(functools.partial(mixer_backward_kernel, S, H, beside, len...  110 us
    pallas_call x1, Pallas kernels, mixer_forward(): pl.pallas_call(functools.partial(mixer_forward_kernel, S, H, lengths.shap...  73.8 us
    pallas_call x1, Pallas kernels, first_rows(): pl.pallas_call(functools.partial(first_kernel, S, H, C, FS, conv_x.shape[...  49.7 us
    pallas_call x1, Pallas kernels, finish(): pl.pallas_call(functools.partial(finish_kernel, S, H, C, FS, state), out_...  8.77 us

profile of v6, /device:TPU:0, one launch (start us, length us, event | category | flops | bytes accessed | tf_op | source)
XLA Modules:
  0.0 393.9 jit_solution(6033134382574050634)
XLA Ops:
  0.7 0.0 copy-start
  0.7 0.5 compare_convert_fusion.mine_ref
  1.2 0.1 pad.7.clone
  1.3 1.3 copy-done
  2.6 1.0 constant_dynamic-slice_fusion.1
  3.5 0.8 pad.4.out_w_ref
  4.3 2.4 maximum_maximum_fusion.down_ref
  6.7 49.7 %shard_map.366 = (bf16[2048,1664]{1,0:T(8,128)(2,1)}, f32[8,128]{1,0:T(8,128)}, f32[4,384]{1,0:T(4,128)}, f32[128,128]{1,0:T(8,128)}, bf16[1536,512]{1,0:T(8,128)(2,1)}, /*index=5*/bf16[1536,768]{1,0:T(8,128)(2,1)}) custom-call(f32[64,1536]{1,0:T(8,128)} %in_ref.5, f32[1536]{0:T(1024)} %gain_ref.7, s32[6,64]{1,0:T(8,128)} %bitcast.23, f32[4,768]{1,0:T(4,128)} %conv_ref.1, ...), custom_call_target="tpu_custom_call" | custom-call | tf_op jit(solution)/shard_map/pallas_call | solution.py:586
  56.4 73.8 %shard_map.367 = (f32[2048,384]{1,0:T(8,128)}, f32[2048,128]{1,0:T(8,128)}, f32[2048,128]{1,0:T(8,128)}, f32[8,128,128]{2,1,0:T(8,128)}, f32[64,1664]{1,0:T(8,128)}, /*index=5*/bf16[2048,1536]{1,0:T(8,128)(2,1)}) custom-call(s32[4]{0:T(128)} %lengths_ref.3, bf16[2048,1664]{1,0:T(8,128)(2,1)} %get-tuple-element.61.in_ref.named_ref.one_ref, ...), custom_call_target="tpu_custom_call" | custom-call | tf_op jit(solution)/shard_map/pallas_call | solution.py:801
  130.2 138.2 %shard_map.368 = (bf16[2048,1664]{1,0:T(8,128)(2,1)}, f32[64,1536]{1,0:T(8,128)}, f32[64,1536]{1,0:T(8,128)}, f32[1,1536]{1,0:T(1,128)}, bf16[1536,128]{1,0:T(8,...) custom-call(f32[64,1664]{1,0:T(8,128)} %get-tuple-element.65.total_r, ...), custom_call_target="tpu_custom_call" | custom-call | tf_op jit(solution)/shard_map/pallas_call | solution.py:1373
  268.5 109.8 %shard_map.369 = (f32[64,1536]{1,0:T(8,128)}, f32[64,1536]{1,0:T(8,128)}, f32[48,384]{1,0:T(8,128)}, f32[4,96,128]{2,1,0:T(8,128)}, bf16[8,112,384]{2,1,0:T(8,128)(2,1)}, /*index=5*/bf16[8,96,192]{2,1,0:T(8,128)(2,1)}) custom-call(s32[4]{0:T(128)} %lengths_ref.3, bf16[2048,1664]{1,0:T(8,128)(2,1)} %get-tuple-element.68.three_ref, ...), custom_call_target="tpu_custom_call" | custom-call | tf_op jit(solution)/shard_map/pallas_call | solution.py:1106
  378.2 0.8 slice.21
  379.1 1.4 slice.17
  380.5 0.0 copy-start.1
  380.5 0.7 copy.42
  381.2 8.8 %shard_map.370 = (f32[192,2,768]{2,1,0:T(2,128)}, f32[12,192]{1,0:T(8,128)}, f32[192,768]{1,0:T(8,128)}, f32[48,2,1024]{2,1,0:T(2,128)}, f32[48,1024]{1,0:T(8,12...) custom-call(bf16[8,112,384]{2,1,0:T(8,128)(2,1)} %get-tuple-element., ...), custom_call_target="tpu_custom_call" | custom-call | tf_op jit(solution)/shard_map/pallas_call | solution.py:1468
  389.9 1.3 slice_bitcast_fusion
  391.3 1.3 reduce
  392.6 1.3 reduce.1
  393.9 0.0 copy-done.1
  (2 shorter events, 0.0 us)
Async XLA Ops:
  0.7 1.9 copy-start
  380.5 13.4 %copy-start.1 = (bf16[1024,1536]{1,0:T(8,128)(2,1)S(1)}, bf16[1024,1536]{1,0:T(8,128)(2,1)}, u32[]{:S(2)}) copy-start(bf16[1024,1536]{1,0:T(8,128)(2,1)} %param.40) | copy-start | bytes 9437188
